TPU v7x, 32 devices: a whole 2x2x4 slice. The times are simulated.
32 devices in a mesh: rep: 8 (over y, x, core), shard: 4 (over z).
Axes of the slice: x: 2, y: 2, z: 4, core: 2. Of those that a mesh axis runs over, the one named last changes fastest.
Arguments:
- hidden_in: bfloat16 [8, 1104, 1024], P('rep', 'shard'), may hold values from -6 to 6
- skip_path: bfloat16 [8, 1104, 1024], P('rep', 'shard'), may hold values from -6 to 6
- cotangent: bfloat16 [8, 1104, 1024], P('rep', 'shard'), may hold values from -6 to 6
- skip_weight: float32 [2048, 1024], P('shard')
- heads_in: float32 [1024, 3072], P('shard')
- heads_out: float32 [1024, 1024], P('shard')
- expand_weight: float32 [1024, 4096], P('shard')
- reduce_weight: float32 [4096, 1024], P('shard')
- vectors: float32 [11, 1024], P(None, 'shard'), as said below
- moments_skip: float32 [2, 2048, 1024], P(None, 'shard'), as said below
- moments_in: float32 [2, 1024, 3072], P(None, 'shard'), as said below
- moments_out: float32 [2, 1024, 1024], P(None, 'shard'), as said below
- moments_expand: float32 [2, 1024, 4096], P(None, 'shard'), as said below
- moments_reduce: float32 [2, 4096, 1024], P(None, 'shard'), as said below
- moments_vectors: float32 [2, 11, 1024], P(None, None, 'shard'), as said below
Outputs:
- block_out: bfloat16 [8, 1104, 1024], P('rep', 'shard')
- input_gradient: bfloat16 [8, 1104, 1024], P('rep', 'shard')
- skip_gradient: bfloat16 [8, 1104, 1024], P('rep', 'shard')
- gradient_skip: float32 [2048, 1024], P('shard')
- gradient_in: float32 [1024, 3072], P('shard')
- gradient_out: float32 [1024, 1024], P('shard')
- gradient_expand: float32 [1024, 4096], P('shard')
- gradient_reduce: float32 [4096, 1024], P('shard')
- gradient_vectors: float32 [11, 1024], P(None, 'shard')
- new_moments_skip: float32 [2, 2048, 1024], P(None, 'shard')
- new_moments_in: float32 [2, 1024, 3072], P(None, 'shard')
- new_moments_out: float32 [2, 1024, 1024], P(None, 'shard')
- new_moments_expand: float32 [2, 1024, 4096], P(None, 'shard')
- new_moments_reduce: float32 [2, 4096, 1024], P(None, 'shard')
- new_moments_vectors: float32 [2, 11, 1024], P(None, None, 'shard')
- new_skip_weight: float32 [2048, 1024], P('shard')
- new_heads_in: float32 [1024, 3072], P('shard')
- new_heads_out: float32 [1024, 1024], P('shard')
- new_expand_weight: float32 [1024, 4096], P('shard')
- new_reduce_weight: float32 [4096, 1024], P('shard')
- new_vectors: float32 [11, 1024], P(None, 'shard')
- norms: float32 [2, 6], replicated
Inputs may be any that keep to these rules, and one draw needn't show every extreme that they name: `vectors`: gains in rows 1 and 4 are positive. `moments_skip`: root mean squares positive. `moments_in`: root mean squares positive. `moments_out`: root mean squares positive. `moments_expand`: root mean squares positive. `moments_reduce`: root mean squares positive. `moments_vectors`: root mean squares positive.
All inputs are finite; a program needn't handle non-finite values.
Results may differ from a plain program's by a relative error of at most 0.015.
The roundings to bfloat16 on the way count: a program that leaves them out, or rounds other values in their place, can miss the bound.
Values may be sent and summed in bfloat16 or wider, within the bound.
A program may use at most 320 MiB of HBM per device.

v0:
```python
import math

import jax
import jax.numpy as jnp
from jax import lax
from jax.sharding import PartitionSpec as P

HEADS = 16
HEAD_DIM = 64


step_rate = 0.3


def normalize(stream, gain_row, bias_row):
    center = stream - jnp.mean(stream, -1, keepdims=True)
    spread = jnp.mean(center * center, -1, keepdims=True)
    return center * lax.rsqrt(spread + 1e-05) * gain_row + bias_row


def exact_gelu(inputs):
    return jax.nn.gelu(inputs, approximate=False)


def matmul(left, right):
    return jnp.dot(left, right, preferred_element_type=jnp.float32)


def row_sums(matrix):
    return jnp.sum(matrix, 0, dtype=jnp.float32)


def moment_step(gradient, moments):
    first_moment = 0.5 * moments[0] + 0.5 * gradient
    root_square = jnp.sqrt(0.5 * moments[1] * moments[1] + 0.5 * gradient * gradient)
    direction = first_moment / (root_square + 1e-06)
    return (jnp.stack([first_moment, root_square]), direction)


def on_device(
    hidden_in,
    skip_path,
    cotangent,
    skip_weight,
    heads_in,
    heads_out,
    expand_weight,
    reduce_weight,
    vectors,
    moments_skip,
    moments_in,
    moments_out,
    moments_expand,
    moments_reduce,
    moments_vectors,
):
    sequences, portion, model_width = hidden_in.shape
    row_count = sequences * portion
    factor = 1.0 / math.sqrt(HEAD_DIM)
    masters = (skip_weight, heads_in, heads_out, expand_weight, reduce_weight, vectors)
    lowered = tuple((matrix.astype(jnp.bfloat16) for matrix in masters))
    gathered = (
        lax.all_gather(lowered[0], "shard", axis=0, tiled=True),
        lax.all_gather(lowered[1], "shard", axis=0, tiled=True),
        lax.all_gather(lowered[2], "shard", axis=0, tiled=True),
        lax.all_gather(lowered[3], "shard", axis=0, tiled=True),
        lax.all_gather(lowered[4], "shard", axis=0, tiled=True),
        lax.all_gather(lowered[5], "shard", axis=1, tiled=True),
    )
    skip_matrix, in_matrix, out_matrix, expand_matrix, reduce_matrix, table_low = gathered
    table_rows = table_low.astype(jnp.float32)
    source = hidden_in.reshape(row_count, model_width)
    skip_rows = skip_path.reshape(row_count, model_width)
    joined = jnp.concatenate([source, skip_rows], 1)
    entering = matmul(joined, skip_matrix) + table_rows[0]
    normed_one, norm_back_one = jax.vjp(normalize, entering, table_rows[1], table_rows[2])
    first_in = normed_one.astype(jnp.bfloat16)
    triple = matmul(first_in, in_matrix).astype(jnp.bfloat16)
    queries = triple[:, :model_width].reshape(sequences, portion, HEADS, HEAD_DIM)
    key_value = triple[:, model_width:].reshape(sequences, portion, 2 * model_width)
    all_keys = lax.all_gather(key_value, "shard", axis=1, tiled=True)
    full_length = all_keys.shape[1]
    keys_full = all_keys[..., :model_width].reshape(sequences, full_length, HEADS, HEAD_DIM)
    values_full = all_keys[..., model_width:].reshape(sequences, full_length, HEADS, HEAD_DIM)
    scores = (
        jnp.einsum("sqhd,skhd->shqk", queries, keys_full, preferred_element_type=jnp.float32)
        * factor
    )
    row_max = jnp.max(scores, -1)
    row_total = jnp.sum(jnp.exp(scores - row_max[..., None]), -1)
    log_total = row_max + jnp.log(row_total)
    probability = jnp.exp(scores - log_total[..., None])
    mixed = jnp.einsum(
        "shqk,skhd->sqhd",
        probability.astype(jnp.bfloat16),
        values_full,
        preferred_element_type=jnp.float32,
    )
    mixed_low = mixed.reshape(row_count, model_width).astype(jnp.bfloat16)
    middle = entering + matmul(mixed_low, out_matrix) + table_rows[3]
    normed_two, norm_back_two = jax.vjp(normalize, middle, table_rows[4], table_rows[5])
    second_in = normed_two.astype(jnp.bfloat16)
    expanded = matmul(second_in, expand_matrix) + table_rows[7:].reshape(-1)
    activated, gelu_back = jax.vjp(exact_gelu, expanded)
    activated_low = activated.astype(jnp.bfloat16)
    block_result = middle + matmul(activated_low, reduce_matrix) + table_rows[6]
    block_out = block_result.astype(jnp.bfloat16).reshape(sequences, portion, model_width)
    refreshed = (
        lax.all_gather(lowered[0], "shard", axis=0, tiled=True),
        lax.all_gather(lowered[1], "shard", axis=0, tiled=True),
        lax.all_gather(lowered[2], "shard", axis=0, tiled=True),
        lax.all_gather(lowered[3], "shard", axis=0, tiled=True),
        lax.all_gather(lowered[4], "shard", axis=0, tiled=True),
        lax.all_gather(lowered[5], "shard", axis=1, tiled=True),
    )
    skip_matrix = refreshed[0]
    in_matrix = refreshed[1]
    out_matrix = refreshed[2]
    expand_matrix = refreshed[3]
    reduce_matrix = refreshed[4]
    grad_out = cotangent.reshape(row_count, model_width)
    grad_reduce = matmul(activated_low.T, grad_out)
    grad_act = matmul(grad_out, reduce_matrix.T)
    grad_inner = gelu_back(grad_act)[0].astype(jnp.bfloat16)
    grad_expand = matmul(second_in.T, grad_inner)
    grad_second = matmul(grad_inner, expand_matrix.T)
    grad_mid_norm, grad_gain_two, grad_bias_two = norm_back_two(grad_second)
    grad_middle = grad_out.astype(jnp.float32) + grad_mid_norm
    grad_middle_low = grad_middle.astype(jnp.bfloat16)
    grad_outw = matmul(mixed_low.T, grad_middle_low)
    grad_mixed = (
        matmul(grad_middle_low, out_matrix.T)
        .astype(jnp.bfloat16)
        .reshape(sequences, portion, HEADS, HEAD_DIM)
    )
    scores = (
        jnp.einsum("sqhd,skhd->shqk", queries, keys_full, preferred_element_type=jnp.float32)
        * factor
    )
    probability = jnp.exp(scores - log_total[..., None])
    grad_prob = jnp.einsum(
        "sqhd,skhd->shqk", grad_mixed, values_full, preferred_element_type=jnp.float32
    )
    delta = jnp.sum(probability * grad_prob, -1)
    grad_scores = (probability * (grad_prob - delta[..., None])).astype(jnp.bfloat16)
    grad_query = (
        jnp.einsum("shqk,skhd->sqhd", grad_scores, keys_full, preferred_element_type=jnp.float32)
        * factor
    )
    grad_keys = (
        jnp.einsum("shqk,sqhd->skhd", grad_scores, queries, preferred_element_type=jnp.float32)
        * factor
    )
    grad_values = jnp.einsum(
        "shqk,sqhd->skhd",
        probability.astype(jnp.bfloat16),
        grad_mixed,
        preferred_element_type=jnp.float32,
    )
    both_grads = jnp.concatenate(
        [
            grad_keys.reshape(sequences, full_length, model_width),
            grad_values.reshape(sequences, full_length, model_width),
        ],
        -1,
    )
    local_grads = lax.psum_scatter(both_grads, "shard", scatter_dimension=1, tiled=True)
    grad_triple = jnp.concatenate(
        [
            grad_query.reshape(row_count, model_width),
            local_grads.reshape(row_count, 2 * model_width),
        ],
        1,
    ).astype(jnp.bfloat16)
    grad_inw = matmul(first_in.T, grad_triple)
    grad_first = matmul(grad_triple, in_matrix.T)
    grad_pre_norm, grad_gain_one, grad_bias_one = norm_back_one(grad_first)
    grad_entering = (grad_middle + grad_pre_norm).astype(jnp.bfloat16)
    grad_skipw = matmul(joined.T, grad_entering)
    grad_joined = matmul(grad_entering, skip_matrix.T)
    input_gradient = (
        grad_joined[:, :model_width].astype(jnp.bfloat16).reshape(sequences, portion, model_width)
    )
    skip_gradient = (
        grad_joined[:, model_width:].astype(jnp.bfloat16).reshape(sequences, portion, model_width)
    )
    grad_table = jnp.concatenate(
        [
            jnp.stack(
                [
                    row_sums(grad_entering),
                    grad_gain_one,
                    grad_bias_one,
                    row_sums(grad_middle_low),
                    grad_gain_two,
                    grad_bias_two,
                    row_sums(grad_out),
                ]
            ),
            row_sums(grad_inner).reshape(-1, model_width),
        ],
        0,
    )
    partials = (grad_skipw, grad_inw, grad_outw, grad_expand, grad_reduce, grad_table)
    shares = (
        lax.psum_scatter(partials[0], "shard", scatter_dimension=0, tiled=True),
        lax.psum_scatter(partials[1], "shard", scatter_dimension=0, tiled=True),
        lax.psum_scatter(partials[2], "shard", scatter_dimension=0, tiled=True),
        lax.psum_scatter(partials[3], "shard", scatter_dimension=0, tiled=True),
        lax.psum_scatter(partials[4], "shard", scatter_dimension=0, tiled=True),
        lax.psum_scatter(partials[5], "shard", scatter_dimension=1, tiled=True),
    )
    pieces = (
        lax.psum_scatter(shares[0], "rep", scatter_dimension=1, tiled=True),
        lax.psum_scatter(shares[1], "rep", scatter_dimension=1, tiled=True),
        lax.psum_scatter(shares[2], "rep", scatter_dimension=1, tiled=True),
        lax.psum_scatter(shares[3], "rep", scatter_dimension=1, tiled=True),
        lax.psum_scatter(shares[4], "rep", scatter_dimension=1, tiled=True),
    )
    vector_total = lax.psum(shares[5], "rep")
    replicas = lax.axis_size("rep")
    rep_index = lax.axis_index("rep")
    states = (moments_skip, moments_in, moments_out, moments_expand, moments_reduce)
    piece_states = []
    piece_updates = []
    weight_squares = []
    direction_squares = []
    piece_weights = []
    piece_directions = []
    for position in range(5):
        width = masters[position].shape[1] // replicas
        weight_piece = lax.dynamic_slice_in_dim(masters[position], rep_index * width, width, 1)
        moment_piece = lax.dynamic_slice_in_dim(states[position], rep_index * width, width, 2)
        new_state, direction = moment_step(pieces[position], moment_piece)
        piece_states.append(new_state)
        piece_weights.append(weight_piece)
        piece_directions.append(direction)
        weight_squares.append(jnp.sum(weight_piece * weight_piece))
        direction_squares.append(jnp.sum(direction * direction))
    vector_state, vector_direction = moment_step(vector_total, moments_vectors)
    weight_squares.append(jnp.sum(vectors * vectors) / replicas)
    direction_squares.append(jnp.sum(vector_direction * vector_direction) / replicas)
    weight_total, direction_total = lax.psum(
        (jnp.stack(weight_squares), jnp.stack(direction_squares)), ("rep", "shard")
    )
    weight_norm = jnp.sqrt(weight_total)
    direction_norm = jnp.sqrt(direction_total)
    ratio = weight_norm / (direction_norm + 1e-06)
    for position in range(5):
        piece_updates.append(
            piece_weights[position] - step_rate * ratio[position] * piece_directions[position]
        )
    new_vectors = vectors - step_rate * ratio[5] * vector_direction
    whole = (
        lax.all_gather(pieces[0], "rep", axis=1, tiled=True),
        lax.all_gather(pieces[1], "rep", axis=1, tiled=True),
        lax.all_gather(pieces[2], "rep", axis=1, tiled=True),
        lax.all_gather(pieces[3], "rep", axis=1, tiled=True),
        lax.all_gather(pieces[4], "rep", axis=1, tiled=True),
        lax.all_gather(piece_states[0], "rep", axis=2, tiled=True),
        lax.all_gather(piece_states[1], "rep", axis=2, tiled=True),
        lax.all_gather(piece_states[2], "rep", axis=2, tiled=True),
        lax.all_gather(piece_states[3], "rep", axis=2, tiled=True),
        lax.all_gather(piece_states[4], "rep", axis=2, tiled=True),
        lax.all_gather(piece_updates[0], "rep", axis=1, tiled=True),
        lax.all_gather(piece_updates[1], "rep", axis=1, tiled=True),
        lax.all_gather(piece_updates[2], "rep", axis=1, tiled=True),
        lax.all_gather(piece_updates[3], "rep", axis=1, tiled=True),
        lax.all_gather(piece_updates[4], "rep", axis=1, tiled=True),
    )
    norms = jnp.stack([weight_norm, direction_norm])
    return (
        block_out,
        input_gradient,
        skip_gradient,
        whole[0],
        whole[1],
        whole[2],
        whole[3],
        whole[4],
        vector_total,
        whole[5],
        whole[6],
        whole[7],
        whole[8],
        whole[9],
        vector_state,
        whole[10],
        whole[11],
        whole[12],
        whole[13],
        whole[14],
        new_vectors,
        norms,
    )


def solution(mesh):
    placed = (
        P("rep", "shard", None),
        P("rep", "shard", None),
        P("rep", "shard", None),
        P("shard", None),
        P("shard", None),
        P("shard", None),
        P("shard", None),
        P("shard", None),
        P(None, "shard"),
        P(None, "shard", None),
        P(None, "shard", None),
        P(None, "shard", None),
        P(None, "shard", None),
        P(None, "shard", None),
        P(None, None, "shard"),
    )
    return jax.shard_map(
        on_device,
        mesh=mesh,
        in_specs=placed,
        out_specs=(
            P("rep", "shard", None),
            P("rep", "shard", None),
            P("rep", "shard", None),
            P("shard", None),
            P("shard", None),
            P("shard", None),
            P("shard", None),
            P("shard", None),
            P(None, "shard"),
            P(None, "shard", None),
            P(None, "shard", None),
            P(None, "shard", None),
            P(None, "shard", None),
            P(None, "shard", None),
            P(None, None, "shard"),
            P("shard", None),
            P("shard", None),
            P("shard", None),
            P("shard", None),
            P("shard", None),
            P(None, "shard"),
            P(),
        ),
        check_vma=False,
    )
```

profile of v0, /device:TPU:0, one launch (start us, length us, event | category | flops | bytes accessed | tf_op | source)
XLA Modules:
  0.0 5051.6 jit_solution(17971204375813850605)
XLA Ops:
  12.3 14.8 all_gather.72
  27.7 66.1 %all-gather.24.cloned.1.call-done = bf16[2048,1024]{1,0:T(8,128)(2,1)} async-done(((bf16[512,1024]{1,0:T(8,128)(2,1)}), bf16[2048,1024]{1,0:T(8,128)(2,1)}) %all-gather.24.cloned.1.call-update) | async-done | bytes 4194320 | tf_op jit(solution)/shard_map/all_gather | solution.py:63
  98.2 111.7 %all-gather.26.cloned.1.call-done = bf16[1024,3072]{1,0:T(8,128)(2,1)} async-done(((bf16[256,3072]{1,0:T(8,128)(2,1)}), bf16[1024,3072]{1,0:T(8,128)(2,1)}) %all-gather.26.cloned.1.call-update) | async-done | bytes 6291472 | tf_op jit(solution)/shard_map/all_gather | solution.py:64
  228.5 74.4 %all-gather.64.cloned.1.call-done = bf16[4,276,2048]{2,1,0:T(8,128)(2,1)} async-done(((bf16[1,276,2048]{2,1,0:T(8,128)(2,1)}), bf16[4,276,2048]{2,1,0:T(8,128)(2,1)}) %all-gather.64.cloned.1.call-update) | async-done | bytes 4522000 | tf_op jit(solution)/shard_map/all_gather | solution.py:81
  352.1 147.6 %all-gather.30.cloned.1.call-done = bf16[1024,4096]{1,0:T(8,128)(2,1)} async-done(((bf16[256,4096]{1,0:T(8,128)(2,1)}), bf16[1024,4096]{1,0:T(8,128)(2,1)}) %all-gather.30.cloned.1.call-update) | async-done | bytes 8388624 | tf_op jit(solution)/shard_map/all_gather | solution.py:66
  499.7 17.1 multiply_convert_fusion.1
  516.8 132.8 %all-gather.32.cloned.1.call-done = bf16[4096,1024]{1,0:T(8,128)(2,1)} async-done(((bf16[1024,1024]{1,0:T(8,128)(2,1)}), bf16[4096,1024]{1,0:T(8,128)(2,1)}) %all-gather.32.cloned.1.call-update) | async-done | bytes 8388624 | tf_op jit(solution)/shard_map/all_gather | solution.py:67
  714.9 14.0 multiply_convert_fusion
  756.0 2455.6 %all-reduce.3 = bf16[1,1104,2048]{2,0,1:T(2,128)(2,1)} all-reduce(f32[1,1104,2048]{2,0,1:T(1,128)} %pad_maximum_fusion), channel_id=3, replica_groups=mesh['rep'=8,'shard'=4] {'shard'}, use_global_device_ids=true, to_apply=%region_9.0.clone | all-reduce | flops 2260992 | bytes 13565952
  3269.9 111.6 %reduce-scatter.12.cloned.1.call-done = f32[512,1024]{1,0:T(8,128)} async-done(((f32[2048,1024]{1,0:T(8,128)}), f32[512,1024]{1,0:T(8,128)}) %reduce-scatter.12.cloned.1.call-update) | async-done | bytes 2097168 | tf_op jit(solution)/shard_map/reduce_scatter | solution.py:206
  3381.6 215.0 %reduce-scatter.16.cloned.1.call-done = f32[256,3072]{1,0:T(8,128)} async-done(((f32[1024,3072]{1,0:T(8,128)}), f32[256,3072]{1,0:T(8,128)}) %reduce-scatter.16.cloned.1.call-update) | async-done | bytes 3145744 | tf_op jit(solution)/shard_map/reduce_scatter | solution.py:207
  3598.9 281.4 %reduce-scatter.24.cloned.1.call-done = f32[256,4096]{1,0:T(8,128)} async-done(((f32[1024,4096]{1,0:T(8,128)}), f32[256,4096]{1,0:T(8,128)}) %reduce-scatter.24.cloned.1.call-update) | async-done | bytes 4194320 | tf_op jit(solution)/shard_map/reduce_scatter | solution.py:209
  3880.4 283.4 %reduce-scatter.28.cloned.1.call-done = f32[1024,1024]{1,0:T(8,128)} async-done(((f32[4096,1024]{1,0:T(8,128)}), f32[1024,1024]{1,0:T(8,128)}) %reduce-scatter.28.cloned.1.call-update) | async-done | bytes 4194320 | tf_op jit(solution)/shard_map/reduce_scatter | solution.py:210
  4163.8 40.1 reduce-scatter.22.cloned.1.call-done
  4207.2 41.6 reduce-scatter.14.cloned.1.call-done
  4251.7 46.6 reduce-scatter.18.cloned.1.call-done
  4320.1 22.9 psum.21
  4344.9 28.0 reduce-scatter.26.cloned.1.call-done
  4376.0 51.9 %reduce-scatter.30.cloned.1.call-done = f32[1024,128]{1,0:T(8,128)} async-done(((f32[1024,1024]{1,0:T(8,128)}), f32[1024,128]{1,0:T(8,128)}) %reduce-scatter.30.cloned.1.call-update) | async-done | bytes 524304 | tf_op jit(solution)/shard_map/reduce_scatter | solution.py:218
  4434.3 39.5 all-reduce.1
  4514.1 39.9 all-gather.44.cloned.1.call-done
  4554.1 34.2 all-gather.36.cloned.1.call-done
  4590.3 45.9 all-gather.46.cloned.1.call-done
  4636.2 25.9 all-gather.58.cloned.1.call-done
  4662.1 30.7 all-gather.54.cloned.1.call-done
  4692.8 34.6 all-gather.56.cloned.1.call-done
  4727.4 38.5 all-gather.40.cloned.1.call-done
  4765.9 39.3 all-gather.42.cloned.1.call-done
  4805.2 39.2 all-gather.60.cloned.1.call-done
  4844.5 39.8 all-gather.62.cloned.1.call-done
  4884.2 56.9 %all-gather.50.cloned.1.call-done = f32[2,256,4096]{2,1,0:T(8,128)} async-done(((f32[2,256,512]{2,1,0:T(8,128)}), f32[2,256,4096]{2,1,0:T(8,128)}) %all-gather.50.cloned.1.call-update) | async-done | bytes 8388624 | tf_op jit(solution)/shard_map/all_gather | solution.py:263
  4941.1 58.4 %all-gather.52.cloned.1.call-done = f32[2,1024,1024]{2,1,0:T(8,128)} async-done(((f32[2,1024,128]{2,1,0:T(8,128)}), f32[2,1024,1024]{2,1,0:T(8,128)}) %all-gather.52.cloned.1.call-update) | async-done | bytes 8388624 | tf_op jit(solution)/shard_map/all_gather | solution.py:264
  (307 shorter events, 350.6 us)
Async XLA Ops:
  7.2 86.7 %all-gather.24.cloned.1.call-start = ((), (), s32[]{:S(2)}) async-start(), calls=%async_computation.11 | async-start | bytes 5242880 | tf_op jit(solution)/shard_map/all_gather | solution.py:63
  10.2 199.8 %all-gather.26.cloned.1.call-start = ((), (), s32[]{:S(2)}) async-start(), calls=%async_computation.12 | async-start | bytes 7864320 | tf_op jit(solution)/shard_map/all_gather | solution.py:64
  11.6 291.3 %all-gather.64.cloned.1.call-start = ((), (), s32[]{:S(2)}) async-start(), calls=%async_computation.42 | async-start | bytes 5734400 | tf_op jit(solution)/shard_map/all_gather | solution.py:81
  217.2 132.1 %all-gather.28.cloned.1.call-start = ((), (), s32[]{:S(2)}) async-start(), calls=%async_computation.13 | async-start | bytes 2621440 | tf_op jit(solution)/shard_map/all_gather | solution.py:65
  218.2 281.5 %all-gather.30.cloned.1.call-start = ((), (), s32[]{:S(2)}) async-start(), calls=%async_computation.14 | async-start | bytes 10485760 | tf_op jit(solution)/shard_map/all_gather | solution.py:66
  222.1 427.5 %all-gather.32.cloned.1.call-start = ((), (), s32[]{:S(2)}) async-start(), calls=%async_computation.15 | async-start | bytes 10485760 | tf_op jit(solution)/shard_map/all_gather | solution.py:67
  226.5 3042.8 %reduce-scatter.20.cloned.1.call-start = ((), (), s32[]{:S(2)}) async-start(), calls=%async_computation.22 | async-start | bytes 5242880 | tf_op jit(solution)/shard_map/reduce_scatter | solution.py:208
  756.0 2625.6 %reduce-scatter.12.cloned.1.call-start = ((), (), s32[]{:S(2)}) async-start(), calls=%async_computation.16 | async-start | bytes 10485760 | tf_op jit(solution)/shard_map/reduce_scatter | solution.py:206
  3239.9 356.8 %reduce-scatter.16.cloned.1.call-start = ((), (), s32[]{:S(2)}) async-start(), calls=%async_computation.19 | async-start | bytes 15728640 | tf_op jit(solution)/shard_map/reduce_scatter | solution.py:207
  3249.1 631.2 %reduce-scatter.24.cloned.1.call-start = ((), (), s32[]{:S(2)}) async-start(), calls=%async_computation.25 | async-start | bytes 20971520 | tf_op jit(solution)/shard_map/reduce_scatter | solution.py:209
  3259.4 904.4 %reduce-scatter.28.cloned.1.call-start = ((), (), s32[]{:S(2)}) async-start(), calls=%async_computation.28 | async-start | bytes 20971520 | tf_op jit(solution)/shard_map/reduce_scatter | solution.py:210
  3269.3 934.6 %reduce-scatter.22.cloned.1.call-start = ((), (), s32[]{:S(2)}) async-start(), calls=%async_computation.23 | async-start | bytes 1179648 | tf_op jit(solution)/shard_map/reduce_scatter | solution.py:216
  3269.9 978.9 %reduce-scatter.14.cloned.1.call-start = ((), (), s32[]{:S(2)}) async-start(), calls=%async_computation.17 | async-start | bytes 2359296 | tf_op jit(solution)/shard_map/reduce_scatter | solution.py:214
  3381.6 916.7 %reduce-scatter.18.cloned.1.call-start = ((), (), s32[]{:S(2)}) async-start(), calls=%async_computation.20 | async-start | bytes 3538944 | tf_op jit(solution)/shard_map/reduce_scatter | solution.py:215
  3596.7 723.4 %reduce-scatter.32.cloned.1.call-start = ((), (), s32[]{:S(2)}) async-start(), calls=%async_computation.31 | async-start | bytes 81920 | tf_op jit(solution)/shard_map/reduce_scatter | solution.py:211
  3598.9 774.0 %reduce-scatter.26.cloned.1.call-start = ((), (), s32[]{:S(2)}) async-start(), calls=%async_computation.26 | async-start | bytes 4718592 | tf_op jit(solution)/shard_map/reduce_scatter | solution.py:217
  3880.4 547.5 %reduce-scatter.30.cloned.1.call-start = ((), (), s32[]{:S(2)}) async-start(), calls=%async_computation.29 | async-start | bytes 4718592 | tf_op jit(solution)/shard_map/reduce_scatter | solution.py:218
  4163.8 341.2 %all-gather.38.cloned.1.call-start = ((), (), s32[]{:S(2)}) async-start(), calls=%async_computation.24 | async-start | bytes 1179648 | tf_op jit(solution)/shard_map/all_gather | solution.py:257
  4203.9 301.1 %all-gather.48.cloned.1.call-start = ((), (), s32[]{:S(2)}) async-start(), calls=%async_computation.34 | async-start | bytes 2359296 | tf_op jit(solution)/shard_map/all_gather | solution.py:262
  4207.1 307.0 %all-gather.34.cloned.1.call-start = ((), (), s32[]{:S(2)}) async-start(), calls=%async_computation.18 | async-start | bytes 2359296 | tf_op jit(solution)/shard_map/all_gather | solution.py:255
  4248.8 305.2 %all-gather.44.cloned.1.call-start = ((), (), s32[]{:S(2)}) async-start(), calls=%async_computation.32 | async-start | bytes 4718592 | tf_op jit(solution)/shard_map/all_gather | solution.py:260
  4251.6 336.6 %all-gather.36.cloned.1.call-start = ((), (), s32[]{:S(2)}) async-start(), calls=%async_computation.21 | async-start | bytes 3538944 | tf_op jit(solution)/shard_map/all_gather | solution.py:256
  4298.3 337.8 %all-gather.46.cloned.1.call-start = ((), (), s32[]{:S(2)}) async-start(), calls=%async_computation.33 | async-start | bytes 7077888 | tf_op jit(solution)/shard_map/all_gather | solution.py:261
  4302.2 359.9 %all-gather.58.cloned.1.call-start = ((), (), s32[]{:S(2)}) async-start(), calls=%async_computation.39 | async-start | bytes 1179648 | tf_op jit(solution)/shard_map/all_gather | solution.py:267
  4477.2 215.6 %all-gather.54.cloned.1.call-start = ((), (), s32[]{:S(2)}) async-start(), calls=%async_computation.37 | async-start | bytes 2359296 | tf_op jit(solution)/shard_map/all_gather | solution.py:265
  4479.6 247.8 %all-gather.56.cloned.1.call-start = ((), (), s32[]{:S(2)}) async-start(), calls=%async_computation.38 | async-start | bytes 3538944 | tf_op jit(solution)/shard_map/all_gather | solution.py:266
  4482.2 283.7 %all-gather.40.cloned.1.call-start = ((), (), s32[]{:S(2)}) async-start(), calls=%async_computation.27 | async-start | bytes 4718592 | tf_op jit(solution)/shard_map/all_gather | solution.py:258
  4482.8 322.4 %all-gather.42.cloned.1.call-start = ((), (), s32[]{:S(2)}) async-start(), calls=%async_computation.30 | async-start | bytes 4718592 | tf_op jit(solution)/shard_map/all_gather | solution.py:259
  4483.5 360.9 %all-gather.60.cloned.1.call-start = ((), (), s32[]{:S(2)}) async-start(), calls=%async_computation.40 | async-start | bytes 4718592 | tf_op jit(solution)/shard_map/all_gather | solution.py:268
  4486.2 398.0 %all-gather.62.cloned.1.call-start = ((), (), s32[]{:S(2)}) async-start(), calls=%async_computation.41 | async-start | bytes 4718592 | tf_op jit(solution)/shard_map/all_gather | solution.py:269
  4489.0 452.1 %all-gather.50.cloned.1.call-start = ((), (), s32[]{:S(2)}) async-start(), calls=%async_computation.35 | async-start | bytes 9437184 | tf_op jit(solution)/shard_map/all_gather | solution.py:263
  4491.2 508.4 %all-gather.52.cloned.1.call-start = ((), (), s32[]{:S(2)}) async-start(), calls=%async_computation.36 | async-start | bytes 9437184 | tf_op jit(solution)/shard_map/all_gather | solution.py:264
  (63 other events, 1950.2 us)
Sparse Core Ops, SparseCore 0:
  10.3 83.5 all-gather.23
  96.0 113.8 all-gather.25
  217.4 85.4 all-gather.63
  304.9 44.4 all-gather.27
  351.3 148.3 all-gather.29
  501.7 147.8 all-gather.31
  756.1 138.9 reduce-scatter.19
  3240.0 141.4 reduce-scatter.11
  3384.0 212.5 reduce-scatter.15
  3599.0 281.3 reduce-scatter.23
  3882.7 281.0 reduce-scatter.27
  4167.1 36.7 reduce-scatter.21
  4207.6 41.2 reduce-scatter.13
  4252.0 46.2 reduce-scatter.17
  4301.1 19.0 reduce-scatter.31
  4323.3 49.5 reduce-scatter.25
  4376.5 51.3 reduce-scatter.29
  4429.6 23.8 all-gather.37
  4455.9 28.1 all-gather.47
  4485.9 28.1 all-gather.33
  4516.6 37.4 all-gather.43
  4556.0 32.2 all-gather.35
  4590.7 45.3 all-gather.45
  4638.5 23.5 all-gather.57
  4664.5 28.1 all-gather.53
  4695.1 32.2 all-gather.55
  4729.1 36.7 all-gather.39
  4767.8 37.4 all-gather.41
  4807.7 36.7 all-gather.59
  4846.8 37.4 all-gather.61
  4886.7 54.3 all-gather.49
  4943.6 55.9 all-gather.51
where the time goes:
time: 5060 us; the launch traced here: 5050 us
  blocking collectives  2530 us (50%)
  waiting for transfers between devices  2140 us (42%)
  matrix products  156 us (3%)
  local copies, waits for them, and re-layouts  118 us (2%)
  other arithmetic  83.6 us (2%)
    unnamed x1, blocking collectives  2460 us
    reduce_scatter x1, waiting for transfers between devices, on_device(): lax.psum_scatter(partials[4], 'shard', scatter_dimension=0, tiled=True)  283 us
    reduce_scatter x1, waiting for transfers between devices, on_device(): lax.psum_scatter(partials[3], 'shard', scatter_dimension=0, tiled=True)  281 us
    reduce_scatter x1, waiting for transfers between devices, on_device(): lax.psum_scatter(partials[1], 'shard', scatter_dimension=0, tiled=True)  215 us
    all_gather x1, waiting for transfers between devices, on_device(): lax.all_gather(lowered[3], 'shard', axis=0, tiled=True)  148 us
    all_gather x1, waiting for transfers between devices, on_device(): lax.all_gather(lowered[4], 'shard', axis=0, tiled=True)  133 us
    all_gather x1, waiting for transfers between devices, on_device(): lax.all_gather(lowered[1], 'shard', axis=0, tiled=True)  112 us
    reduce_scatter x1, waiting for transfers between devices, on_device(): lax.psum_scatter(partials[0], 'shard', scatter_dimension=0, tiled=True)  112 us
  transfers between devices with their start and end apart: 32, of which 29 were waited for; matrix products, arithmetic and copies ran while one was open for 4% of the time, Pallas kernels for 0%

commit v1 on v0

v1 whole, which is shorter than its diff:
```python
import math

import jax
import jax.numpy as jnp
from jax import lax
from jax.sharding import PartitionSpec as P

HEADS = 16
HEAD_DIM = 64


step_rate = 0.3


def normalize(stream, gain_row, bias_row):
    center = stream - jnp.mean(stream, -1, keepdims=True)
    spread = jnp.mean(center * center, -1, keepdims=True)
    return center * lax.rsqrt(spread + 1e-05) * gain_row + bias_row


def exact_gelu(inputs):
    return jax.nn.gelu(inputs, approximate=False)


def matmul(left, right):
    return jnp.dot(left, right, preferred_element_type=jnp.float32)


def row_sums(matrix):
    return jnp.sum(matrix, 0, dtype=jnp.float32)


def moment_step(gradient, moments):
    first_moment = 0.5 * moments[0] + 0.5 * gradient
    root_square = jnp.sqrt(0.5 * moments[1] * moments[1] + 0.5 * gradient * gradient)
    direction = first_moment / (root_square + 1e-06)
    return (jnp.stack([first_moment, root_square]), direction)


def to_heads(rows, sequences, portion, shards):
    parts = rows.shape[1] // (HEADS * HEAD_DIM)
    width = HEADS * HEAD_DIM // shards
    blocks = rows.reshape(sequences, portion, parts, shards, width).transpose(3, 0, 1, 2, 4)
    blocks = blocks.reshape(shards, sequences * portion, parts * width)
    blocks = lax.all_to_all(blocks, "shard", 0, 0, tiled=True)
    blocks = blocks.reshape(shards, sequences, portion, parts, width).transpose(1, 0, 2, 3, 4)
    return blocks.reshape(sequences, shards * portion, parts, width // HEAD_DIM, HEAD_DIM)


def to_tokens(blocks, sequences, portion, shards):
    parts = blocks.shape[2]
    width = HEADS * HEAD_DIM // shards
    rows = blocks.reshape(sequences, shards, portion, parts, width).transpose(1, 0, 2, 3, 4)
    rows = rows.reshape(shards, sequences * portion, parts * width)
    rows = lax.all_to_all(rows, "shard", 0, 0, tiled=True)
    rows = rows.reshape(shards, sequences * portion, parts, width).transpose(1, 2, 0, 3)
    return rows.reshape(sequences * portion, parts * shards * width)


def on_device(
    hidden_in,
    skip_path,
    cotangent,
    skip_weight,
    heads_in,
    heads_out,
    expand_weight,
    reduce_weight,
    vectors,
    moments_skip,
    moments_in,
    moments_out,
    moments_expand,
    moments_reduce,
    moments_vectors,
):
    sequences, portion, model_width = hidden_in.shape
    shards = lax.axis_size("shard")
    replicas = lax.axis_size("rep")
    rep_index = lax.axis_index("rep")
    row_count = sequences * portion
    factor = 1.0 / math.sqrt(HEAD_DIM)
    masters = (skip_weight, heads_in, heads_out, expand_weight, reduce_weight, vectors)
    gathered = []
    for matrix in masters[:5]:
        height = matrix.shape[0] // replicas
        piece = lax.dynamic_slice_in_dim(matrix, rep_index * height, height, 0)
        piece = piece.astype(jnp.bfloat16)
        gathered.append(lax.all_gather(piece, ("shard", "rep"), axis=0, tiled=True))
    skip_matrix, in_matrix, out_matrix, expand_matrix, reduce_matrix = gathered
    table_low = lax.all_gather(vectors.astype(jnp.bfloat16), "shard", axis=1, tiled=True)
    table_rows = table_low.astype(jnp.float32)
    source = hidden_in.reshape(row_count, model_width)
    skip_rows = skip_path.reshape(row_count, model_width)
    joined = jnp.concatenate([source, skip_rows], 1)
    entering = matmul(joined, skip_matrix) + table_rows[0]
    normed_one, norm_back_one = jax.vjp(normalize, entering, table_rows[1], table_rows[2])
    first_in = normed_one.astype(jnp.bfloat16)
    triple = matmul(first_in, in_matrix).astype(jnp.bfloat16)
    heads = to_heads(triple, sequences, portion, shards)
    queries, keys_full, values_full = heads[:, :, 0], heads[:, :, 1], heads[:, :, 2]
    scores = (
        jnp.einsum("sqhd,skhd->shqk", queries, keys_full, preferred_element_type=jnp.float32)
        * factor
    )
    row_max = jnp.max(scores, -1)
    row_total = jnp.sum(jnp.exp(scores - row_max[..., None]), -1)
    log_total = row_max + jnp.log(row_total)
    probability = jnp.exp(scores - log_total[..., None])
    mixed = jnp.einsum(
        "shqk,skhd->sqhd",
        probability.astype(jnp.bfloat16),
        values_full,
        preferred_element_type=jnp.float32,
    )
    mixed_low = to_tokens(mixed.astype(jnp.bfloat16)[:, :, None], sequences, portion, shards)
    middle = entering + matmul(mixed_low, out_matrix) + table_rows[3]
    normed_two, norm_back_two = jax.vjp(normalize, middle, table_rows[4], table_rows[5])
    second_in = normed_two.astype(jnp.bfloat16)
    expanded = matmul(second_in, expand_matrix) + table_rows[7:].reshape(-1)
    activated, gelu_back = jax.vjp(exact_gelu, expanded)
    activated_low = activated.astype(jnp.bfloat16)
    block_result = middle + matmul(activated_low, reduce_matrix) + table_rows[6]
    block_out = block_result.astype(jnp.bfloat16).reshape(sequences, portion, model_width)
    grad_out = cotangent.reshape(row_count, model_width)
    grad_reduce = matmul(activated_low.T, grad_out)
    grad_act = matmul(grad_out, reduce_matrix.T)
    grad_inner = gelu_back(grad_act)[0].astype(jnp.bfloat16)
    grad_expand = matmul(second_in.T, grad_inner)
    grad_second = matmul(grad_inner, expand_matrix.T)
    grad_mid_norm, grad_gain_two, grad_bias_two = norm_back_two(grad_second)
    grad_middle = grad_out.astype(jnp.float32) + grad_mid_norm
    grad_middle_low = grad_middle.astype(jnp.bfloat16)
    grad_outw = matmul(mixed_low.T, grad_middle_low)
    grad_mixed = matmul(grad_middle_low, out_matrix.T).astype(jnp.bfloat16)
    grad_mixed = to_heads(grad_mixed, sequences, portion, shards)[:, :, 0]
    grad_prob = jnp.einsum(
        "sqhd,skhd->shqk", grad_mixed, values_full, preferred_element_type=jnp.float32
    )
    delta = jnp.sum(probability * grad_prob, -1)
    grad_scores = (probability * (grad_prob - delta[..., None])).astype(jnp.bfloat16)
    grad_query = (
        jnp.einsum("shqk,skhd->sqhd", grad_scores, keys_full, preferred_element_type=jnp.float32)
        * factor
    )
    grad_keys = (
        jnp.einsum("shqk,sqhd->skhd", grad_scores, queries, preferred_element_type=jnp.float32)
        * factor
    )
    grad_values = jnp.einsum(
        "shqk,sqhd->skhd",
        probability.astype(jnp.bfloat16),
        grad_mixed,
        preferred_element_type=jnp.float32,
    )
    grad_heads = jnp.stack([grad_query, grad_keys, grad_values], 2).astype(jnp.bfloat16)
    grad_triple = to_tokens(grad_heads, sequences, portion, shards)
    grad_inw = matmul(first_in.T, grad_triple)
    grad_first = matmul(grad_triple, in_matrix.T)
    grad_pre_norm, grad_gain_one, grad_bias_one = norm_back_one(grad_first)
    grad_entering = (grad_middle + grad_pre_norm).astype(jnp.bfloat16)
    grad_skipw = matmul(joined.T, grad_entering)
    grad_joined = matmul(grad_entering, skip_matrix.T)
    input_gradient = (
        grad_joined[:, :model_width].astype(jnp.bfloat16).reshape(sequences, portion, model_width)
    )
    skip_gradient = (
        grad_joined[:, model_width:].astype(jnp.bfloat16).reshape(sequences, portion, model_width)
    )
    grad_table = jnp.concatenate(
        [
            jnp.stack(
                [
                    row_sums(grad_entering),
                    grad_gain_one,
                    grad_bias_one,
                    row_sums(grad_middle_low),
                    grad_gain_two,
                    grad_bias_two,
                    row_sums(grad_out),
                ]
            ),
            row_sums(grad_inner).reshape(-1, model_width),
        ],
        0,
    )
    width = vectors.shape[1]
    grad_table = lax.psum(grad_table, ("rep", "shard"))
    vector_total = lax.dynamic_slice_in_dim(grad_table, lax.axis_index("shard") * width, width, 1)
    totals = []
    for partial in (grad_skipw, grad_inw, grad_outw, grad_expand, grad_reduce):
        piece = lax.psum_scatter(
            partial.astype(jnp.bfloat16), ("shard", "rep"), scatter_dimension=0, tiled=True
        )
        whole = lax.all_gather(piece, "rep", axis=0, tiled=True)
        totals.append(whole.astype(jnp.float32))
    totals.append(vector_total)
    states = (
        moments_skip,
        moments_in,
        moments_out,
        moments_expand,
        moments_reduce,
        moments_vectors,
    )
    steps = [moment_step(total, state) for total, state in zip(totals, states)]
    squares = jnp.stack(
        [
            jnp.stack([jnp.sum(matrix * matrix) for matrix in masters]),
            jnp.stack([jnp.sum(direction * direction) for _, direction in steps]),
        ]
    )
    norms = jnp.sqrt(lax.psum(squares, "shard"))
    ratio = norms[0] / (norms[1] + 1e-06)
    updated = [
        masters[position] - step_rate * ratio[position] * steps[position][1]
        for position in range(6)
    ]
    return (
        block_out,
        input_gradient,
        skip_gradient,
        *totals,
        *(state for state, _ in steps),
        *updated,
        norms,
    )


def solution(mesh):
    placed = (
        P("rep", "shard", None),
        P("rep", "shard", None),
        P("rep", "shard", None),
        P("shard", None),
        P("shard", None),
        P("shard", None),
        P("shard", None),
        P("shard", None),
        P(None, "shard"),
        P(None, "shard", None),
        P(None, "shard", None),
        P(None, "shard", None),
        P(None, "shard", None),
        P(None, "shard", None),
        P(None, None, "shard"),
    )
    return jax.shard_map(
        on_device,
        mesh=mesh,
        in_specs=placed,
        out_specs=(
            P("rep", "shard", None),
            P("rep", "shard", None),
            P("rep", "shard", None),
            P("shard", None),
            P("shard", None),
            P("shard", None),
            P("shard", None),
            P("shard", None),
            P(None, "shard"),
            P(None, "shard", None),
            P(None, "shard", None),
            P(None, "shard", None),
            P(None, "shard", None),
            P(None, "shard", None),
            P(None, None, "shard"),
            P("shard", None),
            P("shard", None),
            P("shard", None),
            P("shard", None),
            P("shard", None),
            P(None, "shard"),
            P(),
        ),
        check_vma=False,
    )
```

time: 5060 us -> 1410 us (0.28)
  blocking collectives: 2530 us -> 195 us
  waiting for transfers between devices: 2140 us -> 844 us
    unnamed x1 -> x0, blocking collectives: 2460 us -> none
    all_gather x21 -> x9, waiting for transfers between devices: 1030 us -> 232 us  [the longest x5 182 us: on_device(): gathered.append(lax.all_gather(piece, ('shard', 'rep'), axis=0, tiled=True))]
    reduce_scatter x11 -> x5, waiting for transfers between devices: 1110 us -> 585 us  [on_device(): lax.psum_scatter(partial.astype(jnp.bfloat16), ('shard', 'rep'), scatter_...]
    all_to_all x0 -> x3, blocking collectives: none -> 116 us  [the longest x2 72.9 us: to_heads(): blocks = lax.all_to_all(blocks, 'shard', 0, 0, tiled=True)]
  transfers between devices with their start and end apart: 32 -> 15, of which waited for: 29 -> 14; matrix products, arithmetic and copies ran while one was open for 4% -> 13% of each run, Pallas kernels for 0% -> 0%
where the time goes in v1:
time: 1410 us; the launch traced here: 1400 us
  waiting for transfers between devices  844 us (60%)
  blocking collectives  195 us (14%)
  matrix products  140 us (10%)
  other arithmetic  130 us (9%)
  local copies, waits for them, and re-layouts  72.8 us (5%)
  between operations  18.8 us (1%)
    reduce_scatter x5, waiting for transfers between devices, on_device(): lax.psum_scatter(partial.astype(jnp.bfloat16), ('shard', 'rep'), scatter_...  585 us
    all_gather x5, waiting for transfers between devices, on_device(): gathered.append(lax.all_gather(piece, ('shard', 'rep'), axis=0, tiled=True))  182 us
    dot_general x15, matrix products, matmul(): return jnp.dot(left, right, preferred_element_type=jnp.float32)  94 us
    all_to_all x2, blocking collectives, to_heads(): blocks = lax.all_to_all(blocks, 'shard', 0, 0, tiled=True)  72.9 us
    all_gather x4, waiting for transfers between devices, on_device(): whole = lax.all_gather(piece, 'rep', axis=0, tiled=True)  50.1 us
    another operation x12, other arithmetic, moment_step(): return (jnp.stack([first_moment, root_square]), direction)  45.8 us
    all_to_all x1, blocking collectives, to_tokens(): rows = lax.all_to_all(rows, 'shard', 0, 0, tiled=True)  43.3 us
    psum x1, blocking collectives, on_device(): grad_table = lax.psum(grad_table, ('rep', 'shard'))  42 us
  transfers between devices with their start and end apart: 15, of which 14 were waited for; matrix products, arithmetic and copies ran while one was open for 13% of the time, Pallas kernels for 0%

profile of v1, /device:TPU:0, one launch (start us, length us, event | category | flops | bytes accessed | tf_op | source)
XLA Modules:
  0.0 1404.6 jit_solution(5232595855646200945)
XLA Ops:
  17.4 14.8 %all_gather.34 = bf16[11,1024]{1,0:T(8,128)(2,1)S(1)} all-gather(bf16[11,256]{1,0:T(8,128)(2,1)S(1)} %get-tuple-element.167), channel_id=1, replica_groups=mesh['rep'=8,'shard'=4] {'shard'}, dimensions={1}, use_global_device_ids=true | all-gather | bytes 28160 | tf_op jit(solution)/shard_map/all_gather | solution.py:91
  32.8 43.4 %all-gather.10.cloned.1.call-done = bf16[2048,1024]{1,0:T(8,128)(2,1)} async-done(((bf16[64,1024]{1,0:T(8,128)(2,1)}), bf16[2048,1024]{1,0:T(8,128)(2,1)}) %all-gather.10.cloned.1.call-update) | async-done | bytes 4194320 | tf_op jit(solution)/shard_map/all_gather | solution.py:89
  80.6 67.2 %all-gather.12.cloned.1.call-done = bf16[1024,3072]{1,0:T(8,128)(2,1)} async-done(((bf16[32,3072]{1,0:T(8,128)(2,1)}), bf16[1024,3072]{1,0:T(8,128)(2,1)}) %all-gather.12.cloned.1.call-update) | async-done | bytes 6291472 | tf_op jit(solution)/shard_map/all_gather | solution.py:89
  160.1 53.7 %all_to_all.20 = bf16[4,276,768]{2,1,0:T(8,128)(2,1)S(1)} all-to-all(bf16[4,276,768]{2,1,0:T(8,128)(2,1)} %reshape.311), channel_id=1, replica_groups=mesh['rep'=8,'shard'=4] {'shard'}, dimensions={0} | all-to-all | bytes 3391488 | tf_op jit(solution)/shard_map/all_to_all | solution.py:45
  229.2 9.5 exponential_reduce_fusion
  238.8 10.0 fusion.30
  255.0 25.9 %all-to-all-done.1 = bf16[4,276,256]{2,1,0:T(8,128)(2,1)S(1)} async-done(((bf16[4,276,256]{2,1,0:T(8,128)(2,1)}), bf16[4,276,256]{2,1,0:T(8,128)(2,1)S(1)}, u32[]{:S(2)}, u32[]{:S(2)}) %all-to-all-start.1) | async-done | bytes 565280 | tf_op jit(solution)/shard_map/all_to_all | solution.py:55
  284.8 9.6 all-gather.16.cloned.1.call-done
  294.4 16.9 %multiply_convert_fusion.1 = (bf16[276,4096]{1,0:T(8,128)(2,1)}, f32[276,4096]{1,0:T(8,128)}, f32[276,4096]{1,0:T(8,128)}) fusion(f32[4096]{0:T(1024)} %bitcast.293, bf16[1024,4096]{1,0:T(8,128)(2,1)} %all-gather.16.cloned.1.call-done, f32[276,1024]{1,0:T(8,128)S(1)} %get-tuple-element.181, f32[1024]{0:T(1024)S(1)} %bitcast.299, f32[1024]{0:T(1024)S(1)} %bitcast.285, ...), kind=kOutput, calls=%fused_computation.25 | convolution fusion | flops 2391281664 | bytes 20850848 | tf_op jit(solution)/shard_map/dot_general | solution.py:26
  311.3 62.1 %all-gather.18.cloned.1.call-done = bf16[4096,1024]{1,0:T(8,128)(2,1)} async-done(((bf16[128,1024]{1,0:T(8,128)(2,1)}), bf16[4096,1024]{1,0:T(8,128)(2,1)}) %all-gather.18.cloned.1.call-update) | async-done | bytes 8388624 | tf_op jit(solution)/shard_map/all_gather | solution.py:89
  373.4 12.5 convert_reduce_fusion
  395.7 19.2 %all_to_all.21 = bf16[4,276,256]{2,1,0:T(8,128)(2,1)S(1)} all-to-all(bf16[4,276,256]{2,1,0:T(8,128)(2,1)S(1)} %bitcast.278), channel_id=1, replica_groups=mesh['rep'=8,'shard'=4] {'shard'}, dimensions={0} | all-to-all | bytes 1130496 | tf_op jit(solution)/shard_map/all_to_all | solution.py:45
  418.0 10.0 fusion.27
  428.0 12.6 multiply_reduce_fusion
  440.5 13.7 multiply_convert_fusion
  466.7 43.3 %all_to_all.22 = bf16[4,276,768]{2,1,0:T(8,128)(2,1)} all-to-all(bf16[4,276,768]{2,1,0:T(8,128)(2,1)S(1)} %copy.82), channel_id=1, replica_groups=mesh['rep'=8,'shard'=4] {'shard'}, dimensions={0} | all-to-all | bytes 3391488 | tf_op jit(solution)/shard_map/all_to_all | solution.py:55
  540.3 8.9 convolution_convert_fusion.1
  553.2 118.1 %reduce-scatter.6.cloned.1.call-done = bf16[64,1024]{1,0:T(8,128)(2,1)} async-done(((bf16[2048,1024]{1,0:T(8,128)(2,1)}), bf16[64,1024]{1,0:T(8,128)(2,1)}) %reduce-scatter.6.cloned.1.call-update) | async-done | bytes 131088 | tf_op jit(solution)/shard_map/reduce_scatter | solution.py:192
  671.3 116.4 %reduce-scatter.8.cloned.1.call-done = bf16[32,3072]{1,0:T(8,128)(2,1)} async-done(((bf16[1024,3072]{1,0:T(8,128)(2,1)}), bf16[32,3072]{1,0:T(8,128)(2,1)}) %reduce-scatter.8.cloned.1.call-update) | async-done | bytes 196624 | tf_op jit(solution)/shard_map/reduce_scatter | solution.py:192
  787.8 8.5 convolution_convert_fusion
  818.3 42.0 %psum.14 = f32[11,1024]{1,0:T(8,128)S(1)} all-reduce(f32[11,1024]{1,0:T(8,128)S(1)} %concatenate.10), channel_id=1, replica_groups=mesh['rep'=8,'shard'=4] {'rep','shard'}, use_global_device_ids=true, to_apply=%region_24.0 | all-reduce | flops 11264 | bytes 90112 | tf_op jit(solution)/shard_map/psum | solution.py:188
  861.0 77.8 %reduce-scatter.12.cloned.1.call-done = bf16[32,4096]{1,0:T(8,128)(2,1)} async-done(((bf16[1024,4096]{1,0:T(8,128)(2,1)}), bf16[32,4096]{1,0:T(8,128)(2,1)}) %reduce-scatter.12.cloned.1.call-update) | async-done | bytes 262160 | tf_op jit(solution)/shard_map/reduce_scatter | solution.py:192
  944.6 129.8 %reduce-scatter.10.cloned.1.call-done = bf16[32,1024]{1,0:T(8,128)(2,1)} async-done(((bf16[1024,1024]{1,0:T(8,128)(2,1)}), bf16[32,1024]{1,0:T(8,128)(2,1)}) %reduce-scatter.10.cloned.1.call-update) | async-done | bytes 65552 | tf_op jit(solution)/shard_map/reduce_scatter | solution.py:192
  1074.4 10.7 all_gather.41
  1106.0 17.2 %all-gather.22.cloned.1.call-done = bf16[256,3072]{1,0:T(8,128)(2,1)} async-done(((bf16[32,3072]{1,0:T(8,128)(2,1)}), bf16[256,3072]{1,0:T(8,128)(2,1)}) %all-gather.22.cloned.1.call-update) | async-done | bytes 1572880 | tf_op jit(solution)/shard_map/all_gather | solution.py:195
  1123.2 8.6 multiply_reduce_fusion.5
  1131.7 142.9 %reduce-scatter.14.cloned.1.call-done = bf16[128,1024]{1,0:T(8,128)(2,1)} async-done(((bf16[4096,1024]{1,0:T(8,128)(2,1)}), bf16[128,1024]{1,0:T(8,128)(2,1)}) %reduce-scatter.14.cloned.1.call-update) | async-done | bytes 262160 | tf_op jit(solution)/shard_map/reduce_scatter | solution.py:192
  1282.9 17.5 %all-gather.24.cloned.1.call-done = bf16[256,4096]{1,0:T(8,128)(2,1)} async-done(((bf16[32,4096]{1,0:T(8,128)(2,1)}), bf16[256,4096]{1,0:T(8,128)(2,1)}) %all-gather.24.cloned.1.call-update) | async-done | bytes 2097168 | tf_op jit(solution)/shard_map/all_gather | solution.py:195
  1309.9 8.9 fusion.39
  1318.8 11.3 all-gather.26.cloned.1.call-done
  1342.0 10.5 fusion.40
  1352.6 11.7 psum.15
  (231 shorter events, 220.7 us)
Async XLA Ops:
  7.2 69.1 %all-gather.10.cloned.1.call-start = ((), (), s32[]{:S(2)}) async-start(), calls=%async_computation.9 | async-start | bytes 4325376 | tf_op jit(solution)/shard_map/all_gather | solution.py:89
  8.9 138.9 %all-gather.12.cloned.1.call-start = ((), (), s32[]{:S(2)}) async-start(), calls=%async_computation.10 | async-start | bytes 6488064 | tf_op jit(solution)/shard_map/all_gather | solution.py:89
  10.7 270.8 %all-gather.14.cloned.1.call-start = ((), (), s32[]{:S(2)}) async-start(), calls=%async_computation.11 | async-start | bytes 2162688 | tf_op jit(solution)/shard_map/all_gather | solution.py:89
  12.3 282.1 %all-gather.16.cloned.1.call-start = ((), (), s32[]{:S(2)}) async-start(), calls=%async_computation.12 | async-start | bytes 8650752 | tf_op jit(solution)/shard_map/all_gather | solution.py:89
  14.1 359.3 %all-gather.18.cloned.1.call-start = ((), (), s32[]{:S(2)}) async-start(), calls=%async_computation.13 | async-start | bytes 8650752 | tf_op jit(solution)/shard_map/all_gather | solution.py:89
  32.8 115.0 %copy-start.44 = (f32[1,1024]{1,0:T(1,128)}, f32[1,1024]{1,0:T(1,128)S(1)}, u32[]{:S(2)}) copy-start(f32[1,1024]{1,0:T(1,128)S(1)} %get-tuple-element.162) | copy-start | bytes 12292
  32.8 261.6 %copy-start.42 = (f32[1,1024]{1,0:T(1,128)}, f32[1,1024]{1,0:T(1,128)S(1)}, u32[]{:S(2)}) copy-start(f32[1,1024]{1,0:T(1,128)S(1)} %get-tuple-element.159) | copy-start | bytes 12292
  80.3 72.4 %copy-start.18 = (f32[276,1024]{1,0:T(8,128)}, f32[276,1024]{1,0:T(8,128)S(1)}, u32[]{:S(2)}) copy-start(f32[276,1024]{1,0:T(8,128)S(1)} %get-tuple-element.177) | copy-start | bytes 3391492
  80.6 72.1 %copy-start.35 = (f32[276]{0:T(512)}, f32[276]{0:T(512)S(1)}, u32[]{:S(2)}) copy-start(f32[276]{0:T(512)S(1)} %fusion.60) | copy-start | bytes 3316
  250.8 30.1 %all-to-all-start.1 = ((bf16[4,276,256]{2,1,0:T(8,128)(2,1)}), bf16[4,276,256]{2,1,0:T(8,128)(2,1)S(1)}, u32[]{:S(2)}, u32[]{:S(2)}) async-start(bf16[4,276,256]{2,1,0:T(8,128)(2,1)} %copy.75), calls=%async_computation.1 | async-start | bytes 1146880 | tf_op jit(solution)/shard_map/all_to_all | solution.py:55
  254.3 417.0 %reduce-scatter.6.cloned.1.call-start = ((), (), s32[]{:S(2)}) async-start(), calls=%async_computation.14 | async-start | bytes 4325376 | tf_op jit(solution)/shard_map/reduce_scatter | solution.py:192
  284.5 101.4 %copy-start.16 = (f32[276,1024]{1,0:T(8,128)}, f32[276,1024]{1,0:T(8,128)S(1)}, u32[]{:S(2)}) copy-start(f32[276,1024]{1,0:T(8,128)S(1)} %get-tuple-element.181) | copy-start | bytes 3391492
  284.8 104.5 %copy-start.37 = (f32[276]{0:T(512)}, f32[276]{0:T(512)S(1)}, u32[]{:S(2)}) copy-start(f32[276]{0:T(512)S(1)} %fusion.61) | copy-start | bytes 3316
  294.4 79.0 %copy-start.23 = (bf16[1,276,1024]{2,1,0:T(8,128)(2,1)S(1)}, bf16[1,276,1024]{2,1,0:T(8,128)(2,1)}, u32[]{:S(2)}) copy-start(bf16[1,276,1024]{2,1,0:T(8,128)(2,1)} %param.17) | copy-start | bytes 1695748
  373.4 12.5 copy-start.47
  519.3 6.0 copy-start.19
  531.9 255.8 %reduce-scatter.8.cloned.1.call-start = ((), (), s32[]{:S(2)}) async-start(), calls=%async_computation.16 | async-start | bytes 6488064 | tf_op jit(solution)/shard_map/reduce_scatter | solution.py:192
  539.1 399.7 %reduce-scatter.12.cloned.1.call-start = ((), (), s32[]{:S(2)}) async-start(), calls=%async_computation.19 | async-start | bytes 8650752 | tf_op jit(solution)/shard_map/reduce_scatter | solution.py:192
  549.3 525.1 %reduce-scatter.10.cloned.1.call-start = ((), (), s32[]{:S(2)}) async-start(), calls=%async_computation.18 | async-start | bytes 2162688 | tf_op jit(solution)/shard_map/reduce_scatter | solution.py:192
  553.1 542.4 %all-gather.20.cloned.1.call-start = ((), (), s32[]{:S(2)}) async-start(), calls=%async_computation.15 | async-start | bytes 1179648 | tf_op jit(solution)/shard_map/all_gather | solution.py:195
  671.3 451.9 %all-gather.22.cloned.1.call-start = ((), (), s32[]{:S(2)}) async-start(), calls=%async_computation.17 | async-start | bytes 1769472 | tf_op jit(solution)/shard_map/all_gather | solution.py:195
  787.7 486.9 %reduce-scatter.14.cloned.1.call-start = ((), (), s32[]{:S(2)}) async-start(), calls=%async_computation.21 | async-start | bytes 8650752 | tf_op jit(solution)/shard_map/reduce_scatter | solution.py:192
  796.3 504.1 %all-gather.24.cloned.1.call-start = ((), (), s32[]{:S(2)}) async-start(), calls=%async_computation.20 | async-start | bytes 2359296 | tf_op jit(solution)/shard_map/all_gather | solution.py:195
  796.4 6.5 copy-start
  810.3 7.8 copy-start.39
  810.3 7.8 copy-start.40
  861.0 82.6 %copy-start.32 = (f32[11,256]{1,0:T(8,128)}, f32[11,256]{1,0:T(8,128)S(1)}, u32[]{:S(2)}) copy-start(f32[11,256]{1,0:T(8,128)S(1)} %get-tuple-element.118) | copy-start | bytes 33796
  938.8 391.2 %all-gather.26.cloned.1.call-start = ((), (), s32[]{:S(2)}) async-start(), calls=%async_computation.22 | async-start | bytes 2359296 | tf_op jit(solution)/shard_map/all_gather | solution.py:195
  1074.4 14.5 %copy-start.15 = (f32[2,256,1024]{2,1,0:T(8,128)S(1)}, f32[2,256,1024]{2,1,0:T(8,128)}, u32[]{:S(2)}) copy-start(f32[2,256,1024]{2,1,0:T(8,128)} %param.26) | copy-start | bytes 6291460
  1364.2 12.6 copy-start.46
  1368.8 8.0 copy-start.6
  1368.8 8.0 copy-start.7
  (35 other events, 106.1 us)
Sparse Core Ops, SparseCore 0:
  11.5 64.7 all-gather.9
  79.7 68.0 all-gather.11
  151.2 58.5 all-gather.13
  213.1 81.2 all-gather.15
  297.7 75.7 all-gather.17
  532.1 139.1 reduce-scatter.5
  677.5 110.1 reduce-scatter.7
  790.7 148.0 reduce-scatter.11
  941.8 132.5 reduce-scatter.9
  1076.1 19.3 all-gather.19
  1097.4 25.6 all-gather.21
  1125.9 148.6 reduce-scatter.13
  1276.5 23.8 all-gather.23
  1302.1 27.8 all-gather.25

commit v2 on v1

--- a/solution.py
+++ b/solution.py
@@ -1,9 +1,569 @@
+import functools
 import math
 
 import jax
 import jax.numpy as jnp
 from jax import lax
+from jax.experimental import pallas as pl
+from jax.experimental.pallas import tpu as pltpu
 from jax.sharding import PartitionSpec as P
+
+MESH = pl.DeviceIdType.MESH
+LOW = jnp.bfloat16
+ANY = pl.BlockSpec(memory_space=pl.ANY)
+SHARDS, REPLICAS = 4, 8
+UNIT = 16
+BLOCK = 1024
+
+
+class Place:
+    def __init__(self):
+        self.rep = lax.axis_index("rep")
+        self.shard = lax.axis_index("shard")
+        self.core = lax.rem(self.rep, 2)
+        self.x = lax.rem(self.rep // 2, 2)
+        self.y = self.rep // 4
+
+    def across(self, axis):
+        own, step = {"core": (self.core, 1), "x": (self.x, 2), "y": (self.y, 4)}[axis]
+        return (self.rep + step - 2 * step * own, self.shard)
+
+    def along(self, offset):
+        return (self.rep, lax.rem(self.shard + offset, SHARDS))
+
+    def source(self, offset):
+        return lax.rem(self.shard + SHARDS - offset, SHARDS)
+
+    def partners(self):
+        return [self.across("core"), self.across("x"), self.across("y")] + [
+            self.along(offset) for offset in range(1, SHARDS)
+        ]
+
+
+def greet(place):
+    barrier = pltpu.get_barrier_semaphore()
+    partners = place.partners()
+    for partner in partners:
+        pl.semaphore_signal(barrier, inc=1, device_id=partner, device_id_type=MESH)
+    pl.semaphore_wait(barrier, len(partners))
+
+
+def chunk_list(shapes):
+    chunks = []
+    for index, (rows, columns) in enumerate(shapes):
+        for group in range(rows // SHARDS // 256):
+            for part in range(columns // BLOCK):
+                chunks.append((index, group, part))
+    return chunks
+
+
+def folded(matrix):
+    rows, columns = matrix.shape
+    groups = rows // (SHARDS * 256)
+    return matrix.reshape(SHARDS, groups, 2, 2, 2, 2, UNIT, columns)
+
+
+class Ring:
+    def __init__(self, send_sems, recv_sems):
+        self.send_sems, self.recv_sems = send_sems, recv_sems
+        self.open = []
+
+    def send(self, source, target, device, slot):
+        copy = pltpu.make_async_remote_copy(
+            src_ref=source,
+            dst_ref=target,
+            send_sem=self.send_sems.at[slot],
+            recv_sem=self.recv_sems.at[slot],
+            device_id=device,
+            device_id_type=MESH,
+        )
+        copy.start()
+        return copy
+
+
+def gather_kernel(chunks, *refs):
+    count = 5
+    masters = refs[:count]
+    wholes = refs[count : 2 * count]
+    wide, own, load_sems, keep_sems, send_sems, recv_sems = refs[2 * count :]
+    place = Place()
+    s, k, x, y = place.shard, place.core, place.x, place.y
+    total = len(chunks)
+    ring = Ring(send_sems, recv_sems)
+
+    def load(at):
+        index, group, part = chunks[at]
+        return pltpu.make_async_copy(
+            masters[index].at[group, :, :, :, :, :, pl.ds(part * BLOCK, BLOCK)],
+            wide.at[at % 2],
+            load_sems.at[at % 2],
+        )
+
+    def whole(at, *where):
+        index, group, part = chunks[at]
+        shard, rest = where[0], where[1:]
+        rest = rest + (slice(None),) * (5 - len(rest))
+        return wholes[index].at[(shard, group) + rest + (pl.ds(part * BLOCK, BLOCK),)]
+
+    sent = []
+    arrivals = {}
+
+    def go(at, name, position, source, target, device):
+        slot = at * 18 + position
+        copy = ring.send(source, target, device, slot)
+        sent.append(copy)
+        arrivals.setdefault((at, name), []).append(copy)
+
+    def arrived(at, name):
+        for copy in arrivals[(at, name)]:
+            copy.wait_recv()
+
+    load(0).start()
+    load(1).start()
+    greet(place)
+    kept = []
+
+    def stage_cast(at):
+        load(at).wait()
+
+        @pl.loop(0, 16)
+        def _(row):
+            a, b = row // 8, lax.rem(row // 4, 2)
+            c, d = lax.rem(row // 2, 2), lax.rem(row, 2)
+            own[at, a, b, c, d] = wide[at % 2, a, b, c, d].astype(LOW)
+
+        if at + 2 < total:
+            load(at + 2).start()
+        copy = pltpu.make_async_copy(own.at[at], whole(at, s), keep_sems.at[at])
+        copy.start()
+        kept.append(copy)
+
+    def stage_z(at):
+        for offset in range(1, SHARDS):
+            go(
+                at,
+                "z",
+                offset - 1,
+                own.at[at, k, :, y, x],
+                whole(at, s, k, slice(None), y, x),
+                place.along(offset),
+            )
+
+    def stage_first(at):
+        arrived(at, "z")
+        for offset in range(1, SHARDS):
+            e = place.source(offset)
+            ref = whole(at, e, k, 0, y, x)
+            go(at, "first", 3 + 2 * (offset - 1), ref, ref, place.across("x"))
+            ref = whole(at, e, k, 1, y, x)
+            go(at, "first", 4 + 2 * (offset - 1), ref, ref, place.across("y"))
+
+    def stage_second(at):
+        arrived(at, "first")
+        for offset in range(1, SHARDS):
+            e = place.source(offset)
+            ref = whole(at, e, k, 0, y)
+            go(at, "second", 9 + 2 * (offset - 1), ref, ref, place.across("y"))
+            ref = whole(at, e, k, 1, slice(None), x)
+            go(at, "second", 10 + 2 * (offset - 1), ref, ref, place.across("x"))
+
+    def stage_core(at):
+        arrived(at, "second")
+        for offset in range(1, SHARDS):
+            e = place.source(offset)
+            ref = whole(at, e, k)
+            go(at, "core", 15 + offset - 1, ref, ref, place.across("core"))
+
+    def stage_end(at):
+        arrived(at, "core")
+
+    stages = (stage_z, stage_first, stage_second, stage_core, stage_end)
+    lead = 4
+    for at in range(min(lead, total)):
+        stage_cast(at)
+        stage_z(at)
+    for step in range(total + 4):
+        for position in range(1, 5):
+            at = step - (position - 1)
+            if 0 <= at < total:
+                stages[position](at)
+        if step + lead < total:
+            stage_cast(step + lead)
+            stage_z(step + lead)
+    for copy in sent:
+        copy.wait_send()
+    for copy in kept:
+        copy.wait()
+
+
+def gather_weights(masters):
+    shapes = [(matrix.shape[0] * SHARDS, matrix.shape[1]) for matrix in masters]
+    chunks = chunk_list(shapes)
+    total = len(chunks)
+    own = [
+        matrix.reshape(matrix.shape[0] // 256, 2, 2, 2, 2, UNIT, matrix.shape[1])
+        for matrix in masters
+    ]
+    outs = pl.pallas_call(
+        functools.partial(gather_kernel, chunks),
+        out_shape=[
+            jax.ShapeDtypeStruct((SHARDS, r // SHARDS // 256, 2, 2, 2, 2, UNIT, c), LOW)
+            for r, c in shapes
+        ],
+        in_specs=[ANY] * 5,
+        out_specs=[ANY] * 5,
+        scratch_shapes=[
+            pltpu.VMEM((2, 2, 2, 2, 2, UNIT, BLOCK), jnp.float32),
+            pltpu.VMEM((total, 2, 2, 2, 2, UNIT, BLOCK), LOW),
+            pltpu.SemaphoreType.DMA((2,)),
+            pltpu.SemaphoreType.DMA((total,)),
+            pltpu.SemaphoreType.DMA((total * 18,)),
+            pltpu.SemaphoreType.DMA((total * 18,)),
+        ],
+        compiler_params=pltpu.CompilerParams(
+            collective_id=1, has_side_effects=True, vmem_limit_bytes=40 * 2**20
+        ),
+        name="gather_weights",
+    )(*own)
+    return [out.reshape(shape) for out, shape in zip(outs, shapes)]
+
+
+def add_into(target, source, height):
+    @pl.loop(0, height)
+    def _(row):
+        target[row] = (target[row].astype(jnp.float32) + source[row].astype(jnp.float32)).astype(
+            LOW
+        )
+
+
+def reduce_kernel(chunks, *refs):
+    count = 5
+    partials = refs[:count]
+    table = refs[count]
+    sums = refs[count + 1 : 2 * count + 1]
+    table_sum = refs[2 * count + 1]
+    (
+        mine,
+        from_core,
+        from_first,
+        from_second,
+        final,
+        from_z,
+        done,
+        table_own,
+        table_in,
+        table_z,
+        load_sems,
+        keep_sems,
+        send_sems,
+        recv_sems,
+        table_send,
+        table_recv,
+    ) = refs[2 * count + 2 :]
+    place = Place()
+    s, k, x, y = place.shard, place.core, place.x, place.y
+    total = len(chunks)
+    ring = Ring(send_sems, recv_sems)
+    depth = 2
+
+    def part_of(at, shard_slice, core):
+        index, group, part = chunks[at]
+        return partials[index].at[shard_slice, group, core, :, :, :, :, pl.ds(part * BLOCK, BLOCK)]
+
+    def load(at):
+        return pltpu.make_async_copy(
+            part_of(at, slice(None), k), mine.at[at % 3], load_sems.at[at % 3]
+        )
+
+    copies = {}
+
+    def go(at, name, position, source, target, device):
+        slot = at * 14 + position
+        copies.setdefault((at, name), []).append(ring.send(source, target, device, slot))
+
+    def arrived(at, name):
+        for copy in copies[(at, name)]:
+            copy.wait_recv()
+
+    def left(at, name):
+        for copy in copies.pop((at, name), []):
+            copy.wait_send()
+
+    def stage_core(at):
+        go(
+            at,
+            "core",
+            0,
+            part_of(at, slice(None), 1 - k),
+            from_core.at[at % depth],
+            place.across("core"),
+        )
+
+    def stage_first(at):
+        slot = at % 3
+        load(at).wait()
+        arrived(at, "core")
+        left(at, "core")
+
+        @pl.loop(0, SHARDS)
+        def _(shard):
+            for h in range(2):
+                for i in range(2):
+                    for j in range(2):
+                        mine[slot, shard, h, i, j] = (
+                            mine[slot, shard, h, i, j].astype(jnp.float32)
+                            + from_core[at % depth, shard, h, i, j].astype(jnp.float32)
+                        ).astype(LOW)
+
+        go(
+            at,
+            "first",
+            1,
+            mine.at[slot, :, 0, :, 1 - x],
+            from_first.at[at % depth, 0],
+            place.across("x"),
+        )
+        go(
+            at,
+            "first",
+            2,
+            mine.at[slot, :, 1, 1 - y],
+            from_first.at[at % depth, 1],
+            place.across("y"),
+        )
+
+    def stage_second(at):
+        slot = at % 3
+        arrived(at, "first")
+        left(at, "first")
+
+        @pl.loop(0, SHARDS)
+        def _(shard):
+            for i in range(2):
+                mine[slot, shard, 0, i, x] = (
+                    mine[slot, shard, 0, i, x].astype(jnp.float32)
+                    + from_first[at % depth, 0, shard, i].astype(jnp.float32)
+                ).astype(LOW)
+                mine[slot, shard, 1, y, i] = (
+                    mine[slot, shard, 1, y, i].astype(jnp.float32)
+                    + from_first[at % depth, 1, shard, i].astype(jnp.float32)
+                ).astype(LOW)
+
+        go(
+            at,
+            "second",
+            3,
+            mine.at[slot, :, 0, 1 - y, x],
+            from_second.at[at % depth, 0],
+            place.across("y"),
+        )
+        go(
+            at,
+            "second",
+            4,
+            mine.at[slot, :, 1, y, 1 - x],
+            from_second.at[at % depth, 1],
+            place.across("x"),
+        )
+
+    def stage_z(at):
+        slot = at % 3
+        arrived(at, "second")
+        left(at, "second")
+
+        @pl.loop(0, SHARDS)
+        def _(shard):
+            for h in range(2):
+                final[at % depth, shard, h] = (
+                    mine[slot, shard, h, y, x].astype(jnp.float32)
+                    + from_second[at % depth, h, shard].astype(jnp.float32)
+                ).astype(LOW)
+
+        if at + 3 < total:
+            load(at + 3).start()
+        for offset in range(1, SHARDS):
+            target = lax.rem(s + offset, SHARDS)
+            go(
+                at,
+                "z",
+                5 + offset - 1,
+                final.at[at % depth, target],
+                from_z.at[at % depth, offset - 1],
+                place.along(offset),
+            )
+
+    def done_at(at, *where):
+        index, group, part = chunks[at]
+        rest = where + (slice(None),) * (5 - len(where))
+        return done.at[(at,) + rest]
+
+    def stage_back(at):
+        arrived(at, "z")
+        left(at, "z")
+        for h in range(2):
+            value = final[at % depth, s, h].astype(jnp.float32)
+            for offset in range(1, SHARDS):
+                value = value + from_z[at % depth, offset - 1, h].astype(jnp.float32)
+            done[at, k, h, y, x] = value.astype(LOW)
+        ref = done_at(at, k, 0, y, x)
+        go(at, "back", 8, ref, ref, place.across("y"))
+        ref = done_at(at, k, 1, y, x)
+        go(at, "back", 9, ref, ref, place.across("x"))
+
+    def stage_wide(at):
+        arrived(at, "back")
+        ref = done_at(at, k, 0, slice(None), x)
+        go(at, "wide", 10, ref, ref, place.across("x"))
+        ref = done_at(at, k, 1, y)
+        go(at, "wide", 11, ref, ref, place.across("y"))
+
+    def stage_twin(at):
+        arrived(at, "wide")
+        ref = done_at(at, k)
+        go(at, "twin", 12, ref, ref, place.across("core"))
+
+    kept = []
+
+    def stage_keep(at):
+        arrived(at, "twin")
+        index, group, part = chunks[at]
+        copy = pltpu.make_async_copy(
+            done.at[at],
+            sums[index].at[group, :, :, :, :, :, pl.ds(part * BLOCK, BLOCK)],
+            keep_sems.at[at],
+        )
+        copy.start()
+        kept.append(copy)
+
+    for at in range(min(3, total)):
+        load(at).start()
+    table_copy = pltpu.make_async_copy(table, table_own.at[0], table_send.at[0])
+    table_copy.start()
+    greet(place)
+    table_copy.wait()
+
+    def table_step(position, axis):
+        copy = pltpu.make_async_remote_copy(
+            src_ref=table_own.at[position],
+            dst_ref=table_in.at[position],
+            send_sem=table_send.at[1 + position],
+            recv_sem=table_recv.at[position],
+            device_id=place.across(axis),
+            device_id_type=MESH,
+        )
+        copy.start()
+        return copy
+
+    table_copies = []
+
+    def table_sum_step(position, axis):
+        if position:
+            table_copies[-1].wait_recv()
+            table_own[position] = table_own[position - 1] + table_in[position - 1]
+        if axis:
+            table_copies.append(table_step(position, axis))
+
+    def table_along():
+        for offset in range(1, SHARDS):
+            target = lax.rem(s + offset, SHARDS)
+            copy = pltpu.make_async_remote_copy(
+                src_ref=table_own.at[3, target],
+                dst_ref=table_z.at[offset - 1],
+                send_sem=table_send.at[3 + offset],
+                recv_sem=table_recv.at[2 + offset],
+                device_id=place.along(offset),
+                device_id_type=MESH,
+            )
+            copy.start()
+            table_copies.append(copy)
+
+    def table_end():
+        for copy in table_copies[3:]:
+            copy.wait_recv()
+        value = table_own[3, s]
+        for offset in range(1, SHARDS):
+            value = value + table_z[offset - 1]
+        table_sum[...] = value
+
+    stages = (
+        stage_core,
+        stage_first,
+        stage_second,
+        stage_z,
+        stage_back,
+        stage_wide,
+        stage_twin,
+        stage_keep,
+    )
+    for step in range(total + len(stages) - 1):
+        for position in reversed(range(len(stages))):
+            at = step - position
+            if 0 <= at < total:
+                stages[position](at)
+        if step == 1:
+            table_sum_step(0, "core")
+        if step == 2:
+            table_sum_step(1, "x")
+        if step == 3:
+            table_sum_step(2, "y")
+        if step == 4:
+            table_sum_step(3, None)
+            table_along()
+        if step == 5:
+            table_end()
+    for key in sorted(copies):
+        for copy in copies[key]:
+            copy.wait_send()
+    for copy in table_copies:
+        copy.wait_send()
+    for copy in kept:
+        copy.wait()
+
+
+def reduce_gradients(partials, table):
+    shapes = [matrix.shape for matrix in partials]
+    chunks = chunk_list(shapes)
+    total = len(chunks)
+    width = table.shape[1] // SHARDS
+    split = jnp.pad(table, ((0, 16 - table.shape[0]), (0, 0)))
+    split = split.reshape(16, SHARDS, width).transpose(1, 0, 2)
+    piece = (UNIT, BLOCK)
+    outs = pl.pallas_call(
+        functools.partial(reduce_kernel, chunks),
+        out_shape=[
+            jax.ShapeDtypeStruct((r // SHARDS // 256, 2, 2, 2, 2, UNIT, c), LOW) for r, c in shapes
+        ]
+        + [jax.ShapeDtypeStruct((16, width), jnp.float32)],
+        in_specs=[ANY] * 6,
+        out_specs=[ANY] * 5 + [pl.BlockSpec(memory_space=pltpu.VMEM)],
+        scratch_shapes=[
+            pltpu.VMEM((3, SHARDS, 2, 2, 2) + piece, LOW),
+            pltpu.VMEM((2, SHARDS, 2, 2, 2) + piece, LOW),
+            pltpu.VMEM((2, 2, SHARDS, 2) + piece, LOW),
+            pltpu.VMEM((2, 2, SHARDS) + piece, LOW),
+            pltpu.VMEM((2, SHARDS, 2) + piece, LOW),
+            pltpu.VMEM((2, SHARDS - 1, 2) + piece, LOW),
+            pltpu.VMEM((total, 2, 2, 2, 2) + piece, LOW),
+            pltpu.VMEM((4, SHARDS, 16, width), jnp.float32),
+            pltpu.VMEM((3, SHARDS, 16, width), jnp.float32),
+            pltpu.VMEM((SHARDS - 1, 16, width), jnp.float32),
+            pltpu.SemaphoreType.DMA((3,)),
+            pltpu.SemaphoreType.DMA((total,)),
+            pltpu.SemaphoreType.DMA((total * 14,)),
+            pltpu.SemaphoreType.DMA((total * 14,)),
+            pltpu.SemaphoreType.DMA((7,)),
+            pltpu.SemaphoreType.DMA((6,)),
+        ],
+        compiler_params=pltpu.CompilerParams(
+            collective_id=2, has_side_effects=True, vmem_limit_bytes=40 * 2**20
+        ),
+        name="reduce_gradients",
+    )(*[folded(matrix) for matrix in partials], split)
+    sums = [
+        out.reshape(shape[0] // SHARDS, shape[1]) for out, shape in zip(outs[:5], shapes)
+    ]
+    return sums, outs[5][: table.shape[0]]
+
 
 HEADS = 16
 HEAD_DIM = 64
@@ -55,6 +615,35 @@
     rows = lax.all_to_all(rows, "shard", 0, 0, tiled=True)
     rows = rows.reshape(shards, sequences * portion, parts, width).transpose(1, 2, 0, 3)
     return rows.reshape(sequences * portion, parts * shards * width)
+
+
+def fits(shards, replicas, masters):
+    return (
+        shards == SHARDS
+        and replicas == REPLICAS
+        and all(m.shape[0] % 256 == 0 and m.shape[1] % BLOCK == 0 for m in masters)
+    )
+
+
+def gather_plain(masters):
+    replicas, rep_index = lax.axis_size("rep"), lax.axis_index("rep")
+    gathered = []
+    for matrix in masters:
+        height = matrix.shape[0] // replicas
+        piece = lax.dynamic_slice_in_dim(matrix, rep_index * height, height, 0)
+        gathered.append(lax.all_gather(piece.astype(LOW), ("shard", "rep"), axis=0, tiled=True))
+    return gathered
+
+
+def reduce_plain(partials, table):
+    width = table.shape[1] // lax.axis_size("shard")
+    table = lax.psum(table, ("rep", "shard"))
+    table = lax.dynamic_slice_in_dim(table, lax.axis_index("shard") * width, width, 1)
+    sums = []
+    for partial in partials:
+        piece = lax.psum_scatter(partial, ("shard", "rep"), scatter_dimension=0, tiled=True)
+        sums.append(lax.all_gather(piece, "rep", axis=0, tiled=True))
+    return sums, table
 
 
 def on_device(
@@ -77,16 +666,11 @@
     sequences, portion, model_width = hidden_in.shape
     shards = lax.axis_size("shard")
     replicas = lax.axis_size("rep")
-    rep_index = lax.axis_index("rep")
     row_count = sequences * portion
     factor = 1.0 / math.sqrt(HEAD_DIM)
     masters = (skip_weight, heads_in, heads_out, expand_weight, reduce_weight, vectors)
-    gathered = []
-    for matrix in masters[:5]:
-        height = matrix.shape[0] // replicas
-        piece = lax.dynamic_slice_in_dim(matrix, rep_index * height, height, 0)
-        piece = piece.astype(jnp.bfloat16)
-        gathered.append(lax.all_gather(piece, ("shard", "rep"), axis=0, tiled=True))
+    fast = fits(shards, replicas, masters[:5])
+    gathered = gather_weights(masters[:5]) if fast else gather_plain(masters[:5])
     skip_matrix, in_matrix, out_matrix, expand_matrix, reduce_matrix = gathered
     table_low = lax.all_gather(vectors.astype(jnp.bfloat16), "shard", axis=1, tiled=True)
     table_rows = table_low.astype(jnp.float32)
@@ -184,16 +768,13 @@
         ],
         0,
     )
-    width = vectors.shape[1]
-    grad_table = lax.psum(grad_table, ("rep", "shard"))
-    vector_total = lax.dynamic_slice_in_dim(grad_table, lax.axis_index("shard") * width, width, 1)
-    totals = []
-    for partial in (grad_skipw, grad_inw, grad_outw, grad_expand, grad_reduce):
-        piece = lax.psum_scatter(
-            partial.astype(jnp.bfloat16), ("shard", "rep"), scatter_dimension=0, tiled=True
-        )
-        whole = lax.all_gather(piece, "rep", axis=0, tiled=True)
-        totals.append(whole.astype(jnp.float32))
+    partials = [
+        partial.astype(LOW)
+        for partial in (grad_skipw, grad_inw, grad_outw, grad_expand, grad_reduce)
+    ]
+    reduce = reduce_gradients if fast else reduce_plain
+    lows, vector_total = reduce(partials, grad_table)
+    totals = [low.astype(jnp.float32) for low in lows]
     totals.append(vector_total)
     states = (
         moments_skip,

time: 1410 us -> 747 us (0.53)
  waiting for transfers between devices: 844 us -> 35 us
  Pallas kernels: 0 us -> 284 us
  blocking collectives: 195 us -> 76.1 us
  matrix products: 140 us -> 121 us
    reduce_scatter x5 -> x0, waiting for transfers between devices: 585 us -> none  [on_device(): lax.psum_scatter(partial.astype(jnp.bfloat16), ('shard', 'rep'), scatter_...]
    pallas_call x0 -> x2, Pallas kernels: none -> 284 us  [the longest x1 170 us: reduce_gradients(): pl.pallas_call(functools.partial(reduce_kernel, chunks), out_shape=[jax.S...]
    all_gather x9 -> x0, waiting for transfers between devices: 232 us -> none  [the longest x5 182 us: on_device(): gathered.append(lax.all_gather(piece, ('shard', 'rep'), axis=0, tiled=True))]
    all_to_all x1 -> x0, blocking collectives: 43.3 us -> none  [to_tokens(): rows = lax.all_to_all(rows, 'shard', 0, 0, tiled=True)]
    psum x1 -> x0, blocking collectives: 42 us -> none  [on_device(): grad_table = lax.psum(grad_table, ('rep', 'shard'))]
    another operation x12 -> x7, other arithmetic: 45.8 us -> 19.2 us  [moment_step(): return (jnp.stack([first_moment, root_square]), direction)]
    add x0 -> x5, other arithmetic: none -> 23.4 us  [moment_step(): first_moment = 0.5 * moments[0] + 0.5 * gradient]
    all_to_all x2 -> x1, blocking collectives: 72.9 us -> 50.1 us  [to_heads(): blocks = lax.all_to_all(blocks, 'shard', 0, 0, tiled=True)]
  transfers between devices with their start and end apart: 15 -> 3, of which waited for: 14 -> 3; matrix products, arithmetic and copies ran while one was open for 13% -> 5% of each run, Pallas kernels for 0% -> 0%
where the time goes in v2:
time: 747 us; the launch traced here: 738 us
  Pallas kernels  284 us (38%)
  matrix products  121 us (16%)
  other arithmetic  116 us (16%)
  local copies, waits for them, and re-layouts  86.5 us (12%)
  blocking collectives  76.1 us (10%)
  waiting for transfers between devices  35 us (5%)
  starting transfers between devices  13.4 us (2%)
    pallas_call x1, Pallas kernels, reduce_gradients(): pl.pallas_call(functools.partial(reduce_kernel, chunks), out_shape=[jax.S...  170 us
    pallas_call x1, Pallas kernels, gather_weights(): pl.pallas_call(functools.partial(gather_kernel, chunks), out_shape=[jax.S...  114 us
    dot_general x15, matrix products, matmul(): return jnp.dot(left, right, preferred_element_type=jnp.float32)  74.7 us
    all_to_all x1, blocking collectives, to_heads(): blocks = lax.all_to_all(blocks, 'shard', 0, 0, tiled=True)  50.1 us
    all_to_all x2, waiting for transfers between devices, to_tokens(): rows = lax.all_to_all(rows, 'shard', 0, 0, tiled=True)  30.9 us
    unnamed x165, local copies, waits for them, and re-layouts  28.3 us
    reduce_sum x6, other arithmetic, on_device(): jnp.sum(direction * direction)  24.8 us
    add x5, other arithmetic, moment_step(): first_moment = 0.5 * moments[0] + 0.5 * gradient  23.4 us
  transfers between devices with their start and end apart: 3, of which 3 were waited for; matrix products, arithmetic and copies ran while one was open for 5% of the time, Pallas kernels for 0%

profile of v2, /device:TPU:0, one launch (start us, length us, event | category | flops | bytes accessed | tf_op | source)
XLA Modules:
  0.0 738.0 jit_solution(16967579194293701511)
XLA Ops:
  2.1 14.8 %all_gather.3 = bf16[11,1024]{1,0:T(8,128)(2,1)S(1)} all-gather(bf16[11,256]{1,0:T(8,128)(2,1)S(1)} %get-tuple-element.187), channel_id=1, replica_groups=mesh['rep'=8,'shard'=4] {'shard'}, dimensions={1}, use_global_device_ids=true | all-gather | bytes 28160 | tf_op jit(solution)/shard_map/all_gather | solution.py:675
  22.2 114.1 %gather_weights.1 = (bf16[4,2,2,2,2,2,16,1024]{7,6,5,4,3,2,1,0:T(8,128)(2,1)S(1)}, bf16[4,1,2,2,2,2,16,3072]{7,6,5,4,3,2,1,0:T(8,128)(2,1)}, bf16[4,1,2,2,2,2,16...) custom-call(f32[2,2,2,2,2,16,1024]{6,5,4,3,2,1,0:T(8,128)S(1)} %bitc, ...), custom_call_target="tpu_custom_call" | custom-call | tf_op jit(solution)/shard_map/gather_weights/pallas_call | solution.py:207
  151.2 50.1 %all_to_all.20 = bf16[4,276,768]{2,1,0:T(8,128)(2,1)S(1)} all-to-all(bf16[4,276,768]{2,1,0:T(8,128)(2,1)} %reshape.491), channel_id=1, replica_groups=mesh['rep'=8,'shard'=4] {'shard'}, dimensions={0} | all-to-all | bytes 3391488 | tf_op jit(solution)/shard_map/all_to_all | solution.py:605
  208.3 8.4 %fusion.87 = (f32[4,1104]{1,0:T(4,128)S(1)}, f32[4,1104,1104]{1,2,0:T(8,128)}) fusion(bf16[1,1104,3,4,64]{1,4,3,2,0:T(8,128)(2,1)S(1)} %reshape_transpose_reshape.4), kind=kOutput, calls=%fused_computation.206 | convolution fusion | flops 633779904 | bytes 20698368 | tf_op jit(solution)/shard_map/sqhd,skhd->shqk/dot_general | solution.py:687
  216.7 9.5 %exponential_reduce_fusion = f32[4,1104]{1,0:T(4,128)S(1)} fusion(f32[4,1104,1104]{1,2,0:T(8,128)} %get-tuple-element.199, f32[4,1104]{1,0:T(4,128)S(1)} %get-tuple-element.198), kind=kLoop, calls=%fused_computation.4 | loop fusion | flops 9746112 | bytes 19536384 | tf_op jit(solution)/shard_map/reduce_sum | solution.py:691
  226.2 10.8 %fusion.42 = bf16[1,1104,4,64]{1,3,2,0:T(8,128)(2,1)} fusion(f32[4,1104,1104]{1,2,0:T(8,128)} %get-tuple-element.199, f32[4,1104]{1,0:T(4,128)S(1)} %log_add_fusion, bf16[1,1104,3,4,64]{1,4,3,2,0:T(8,128)(2,1)S(1)} %reshape_transpose_reshape.4), kind=kOutput, calls=%fused_computation.101 | convolution fusion | flops 634066944 | bytes 20674560 | tf_op jit(solution)/shard_map/shqk,skhd->sqhd/dot_general | solution.py:694
  247.8 14.6 %all-to-all-done.1 = bf16[4,276,256]{2,1,0:T(8,128)(2,1)} async-done(((bf16[4,276,256]{2,1,0:T(8,128)(2,1)}), bf16[4,276,256]{2,1,0:T(8,128)(2,1)}, u32[]{:S(2)}, u32[]{:S(2)}) %all-to-all-start.1) | async-done | bytes 565280 | tf_op jit(solution)/shard_map/all_to_all | solution.py:615
  265.2 17.6 %multiply_convert_fusion.1 = (bf16[276,4096]{1,0:T(8,128)(2,1)}, f32[276,4096]{1,0:T(8,128)}, f32[276,4096]{1,0:T(8,128)}) fusion(f32[4096]{0:T(1024)S(1)} %bitcast.302, bf16[1024,4096]{1,0:T(8,128)(2,1)} %bitcast.320, f32[276,1024]{1,0:T(8,128)S(1)} %get-tuple-element.201, f32[1024]{0:T(1024)S(1)} %bitcast.310, f32[1024]{0:T(1024)S(1)} %bitcast.298, ...), kind=kOutput, calls=%fused_computation.32 | convolution fusion | flops 2391281664 | bytes 20850848 | tf_op jit(solution)/shard_map/dot_general | solution.py:586
  282.9 6.7 convert_reduce_fusion
  301.2 4.6 all-to-all-start.2
  322.9 10.1 %fusion.39 = bf16[1,1104,1,4,64]{1,4,3,2,0:T(8,128)(2,1)S(1)} fusion(bf16[1104,4,64]{0,2,1:T(8,128)(2,1)S(1)} %reshape.504, f32[4,1104,1104]{1,2,0:T(8,128)} %get-tuple-element.199, f32[4,1104]{1,0:T(4,128)S(1)} %log_add_fusion), kind=kOutput, calls=%fused_computation.100 | convolution fusion | flops 634066944 | bytes 20649216 | tf_op jit(solution)/shard_map/shqk,sqhd->skhd/dot_general | solution.py:734
  333.0 12.6 %multiply_reduce_fusion = (f32[4,1104]{1,0:T(4,128)S(1)}, f32[4,1104,1104]{1,2,0:T(8,128)}) fusion(f32[4,1104,1104]{1,2,0:T(8,128)} %get-tuple-element.199, f32[4,1104]{1,0:T(4,128)S(1)} %log_add_fusion, bf16[1104,4,64]{0,2,1:T(8,128)(2,1)S(1)} %reshape.504, bf16[1,1104,3,4,64]{1,4,3,2,0:T(8,128)(2,1)S(1)} %copy-done.26), kind=kOutput, calls=%fused_computation.2 | convolution fusion | flops 638655168 | bytes 40217856 | tf_op jit(solution)/shard_map/sqhd,skhd->shqk/dot_general | solution.py:721
  345.6 13.7 %multiply_convert_fusion = bf16[4,1104,1104]{1,2,0:T(8,128)(2,1)S(1)} fusion(f32[4,1104,1104]{1,2,0:T(8,128)} %get-tuple-element.205, f32[4,1104,1104]{1,2,0:T(8,128)} %get-tuple-element.199, f32[4,1104]{1,0:T(4,128)S(1)} %get-tuple-element.204, f32[4,1104]{1,0:T(4,128)S(1)} %log_add_fusion), kind=kLoop, calls=%fused_computation.1 | loop fusion | flops 19501056 | bytes 48787968 | tf_op jit(solution)/shard_map/convert_element_type | solution.py:725
  365.6 4.7 convert_element_type.216
  373.6 4.5 all-to-all-start.3
  380.8 6.8 convolution_convert_fusion
  387.6 7.1 convolution_convert_fusion.1
  394.8 6.7 fusion.54
  401.5 16.3 %all-to-all-done.3 = bf16[4,276,768]{2,1,0:T(8,128)(2,1)} async-done(((bf16[4,276,768]{2,1,0:T(8,128)(2,1)}), bf16[4,276,768]{2,1,0:T(8,128)(2,1)}, u32[]{:S(2)}, u32[]{:S(2)}) %all-to-all-start.3) | async-done | bytes 1695776 | tf_op jit(solution)/shard_map/all_to_all | solution.py:615
  430.6 5.6 multiply_reduce_fusion.10
  441.3 4.4 convolution_convert_fusion.4
  445.7 5.7 convolution_convert_fusion.2
  453.9 170.1 %reduce_gradients.1 = (bf16[2,2,2,2,2,16,1024]{6,5,4,3,2,1,0:T(8,128)(2,1)S(1)}, bf16[1,2,2,2,2,16,3072]{6,5,4,3,2,1,0:T(8,128)(2,1)S(1)}, bf16[1,2,2,2,2,16,102...) custom-call(bf16[4,2,2,2,2,2,16,1024]{7,6,5,4,3,2,1,0:T(8,128)(2,1)S, ...), custom_call_target="tpu_custom_call" | custom-call | tf_op jit(solution)/shard_map/reduce_gradients/pallas_call | solution.py:531
  624.0 8.3 %multiply_reduce_fusion.5 = (f32[]{:T(128)}, f32[256,3072]{1,0:T(8,128)}, f32[256,3072]{1,0:T(8,128)}) fusion(f32[2,256,3072]{2,1,0:T(8,128)} %param.25, bf16[1,2,2,2,2,16,3072]{6,5,4,3,2,1,0:T(8,128)(2,1)S(1)} %get-tuple-element.39), kind=kLoop, calls=%fused_computation.80 | loop fusion | flops 9437183 | bytes 14155780 | tf_op jit(solution)/shard_map/reduce_sum | solution.py:791
  632.3 7.2 multiply_add_fusion.5
  643.7 5.6 multiply_reduce_fusion.2
  649.3 5.5 multiply_add_fusion.3
  665.9 4.7 multiply_reduce_fusion.1
  670.6 5.9 multiply_add_fusion.2
  681.7 11.3 %psum.7 = f32[2,6]{1,0:T(2,128)S(1)} all-reduce(f32[2,6]{1,0:T(2,128)S(1)} %pad_maximum_fusion.10), channel_id=1, replica_groups=mesh['rep'=8,'shard'=4] {'shard'}, use_global_device_ids=true, to_apply=%region_31.32 | all-reduce | flops 12 | bytes 96 | tf_op jit(solution)/shard_map/psum | solution.py:794
  697.3 5.0 pad_maximum_fusion.3
  709.6 4.8 pad_maximum_fusion
  (250 shorter events, 154.6 us)
Async XLA Ops:
  17.5 122.3 %copy-start.56 = (f32[1,1024]{1,0:T(1,128)}, f32[1,1024]{1,0:T(1,128)S(1)}, u32[]{:S(2)}) copy-start(f32[1,1024]{1,0:T(1,128)S(1)} %get-tuple-element.181) | copy-start | bytes 12292
  17.5 122.3 %copy-start.60 = (f32[1,1024]{1,0:T(1,128)}, f32[1,1024]{1,0:T(1,128)S(1)}, u32[]{:S(2)}) copy-start(f32[1,1024]{1,0:T(1,128)S(1)} %get-tuple-element.182) | copy-start | bytes 12292
  22.2 114.2 %copy-start.65 = (bf16[1,276,1024]{2,1,0:T(8,128)(2,1)S(1)}, bf16[1,276,1024]{2,1,0:T(8,128)(2,1)}, u32[]{:S(2)}) copy-start(bf16[1,276,1024]{2,1,0:T(8,128)(2,1)} %param.16) | copy-start | bytes 1695748
  22.2 114.2 %copy-start.67 = (bf16[1,276,1024]{2,1,0:T(8,128)(2,1)S(1)}, bf16[1,276,1024]{2,1,0:T(8,128)(2,1)}, u32[]{:S(2)}) copy-start(bf16[1,276,1024]{2,1,0:T(8,128)(2,1)} %param.15) | copy-start | bytes 1695748
  139.5 124.5 %copy-start.35 = (f32[276,1024]{1,0:T(8,128)}, f32[276,1024]{1,0:T(8,128)S(1)}, u32[]{:S(2)}) copy-start(f32[276,1024]{1,0:T(8,128)S(1)} %get-tuple-element.197) | copy-start | bytes 3391492
  208.3 17.9 %copy-start.25 = (bf16[1,1104,3,4,64]{1,4,3,2,0:T(8,128)(2,1)}, bf16[1,1104,3,4,64]{1,4,3,2,0:T(8,128)(2,1)S(1)}, u32[]{:S(2)}) copy-start(bf16[1,1104,3,4,64]{1,4,3,2,0:T(8,128)(2,1)S(1)} %reshape_transpose_reshape.4) | copy-start | bytes 5087236
  237.0 9.6 %copy-start.4 = (f32[512,1024]{1,0:T(8,128)S(1)}, f32[512,1024]{1,0:T(8,128)}, u32[]{:S(2)}) copy-start(f32[512,1024]{1,0:T(8,128)} %param.18) | copy-start | bytes 6291460
  242.2 20.1 %all-to-all-start.1 = ((bf16[4,276,256]{2,1,0:T(8,128)(2,1)}), bf16[4,276,256]{2,1,0:T(8,128)(2,1)}, u32[]{:S(2)}, u32[]{:S(2)}) async-start(bf16[4,276,256]{2,1,0:T(8,128)(2,1)} %copy.77), calls=%async_computation.1 | async-start | bytes 1146880 | tf_op jit(solution)/shard_map/all_to_all | solution.py:615
  247.8 16.2 %copy-start.12 = (bf16[4,1,2,2,2,2,16,1024]{7,6,5,4,3,2,1,0:T(8,128)(2,1)S(1)}, bf16[4,1,2,2,2,2,16,1024]{7,6,5,4,3,2,1,0:T(8,128)(2,1)}, u32[]{:S(2)}) copy-start(bf16[4,1,2,2,2,2,16,1024]{7,6,5,4,3,2,1,0:T(8,128)(2,1)} %copy-done.11) | copy-start | bytes 6291460
  264.0 18.9 %slice-start.4 = ((s8[8388608]{0:T(1024)(128)(4,1)}), s8[4194304]{0:T(1024)(128)(4,1)S(1)}, s32[]{:S(2)}) async-start(s8[8388608]{0:T(1024)(128)(4,1)} %bitcast.317), calls=%async_computation.8 | async-start | bytes 8388608
  264.0 25.7 %slice-start.6 = ((s8[8388608]{0:T(1024)(128)(4,1)}), s8[4194304]{0:T(1024)(128)(4,1)S(1)}, s32[]{:S(2)}) async-start(s8[8388608]{0:T(1024)(128)(4,1)} %bitcast.321), calls=%async_computation.10 | async-start | bytes 8388608
  264.9 27.7 %copy-start.37 = (f32[276,1024]{1,0:T(8,128)}, f32[276,1024]{1,0:T(8,128)S(1)}, u32[]{:S(2)}) copy-start(f32[276,1024]{1,0:T(8,128)S(1)} %get-tuple-element.201) | copy-start | bytes 3391492
  265.2 17.7 %copy-start.41 = (bf16[1,276,1024]{2,1,0:T(8,128)(2,1)S(1)}, bf16[1,276,1024]{2,1,0:T(8,128)(2,1)}, u32[]{:S(2)}) copy-start(bf16[1,276,1024]{2,1,0:T(8,128)(2,1)} %param.17) | copy-start | bytes 1695748
  265.2 17.7 %slice-start.5 = ((s8[8388608]{0:T(1024)(128)(4,1)}), s8[4194304]{0:T(1024)(128)(4,1)S(1)}, s32[]{:S(2)}) async-start(s8[8388608]{0:T(1024)(128)(4,1)} %bitcast.317), calls=%async_computation.9 | async-start | bytes 8388608
  265.2 24.4 %slice-start.7 = ((s8[8388608]{0:T(1024)(128)(4,1)}), s8[4194304]{0:T(1024)(128)(4,1)S(1)}, s32[]{:S(2)}) async-start(s8[8388608]{0:T(1024)(128)(4,1)} %bitcast.321), calls=%async_computation.11 | async-start | bytes 8388608
  296.7 11.3 %copy-start.1 = (f32[256,3072]{1,0:T(8,128)S(1)}, f32[256,3072]{1,0:T(8,128)}, u32[]{:S(2)}) copy-start(f32[256,3072]{1,0:T(8,128)} %param.19) | copy-start | bytes 9437188
  301.2 19.7 %all-to-all-start.2 = ((bf16[4,276,256]{2,1,0:T(8,128)(2,1)}), bf16[4,276,256]{2,1,0:T(8,128)(2,1)}, u32[]{:S(2)}, u32[]{:S(2)}) async-start(bf16[4,276,256]{2,1,0:T(8,128)(2,1)} %bitcast.285), calls=%async_computation.2 | async-start | bytes 1146880 | tf_op jit(solution)/shard_map/all_to_all | solution.py:605
  322.9 10.1 %copy-start.26 = (bf16[1,1104,3,4,64]{1,4,3,2,0:T(8,128)(2,1)S(1)}, bf16[1,1104,3,4,64]{1,4,3,2,0:T(8,128)(2,1)}, u32[]{:S(2)}) copy-start(bf16[1,1104,3,4,64]{1,4,3,2,0:T(8,128)(2,1)} %copy-done.25) | copy-start | bytes 5087236
  370.4 7.8 %copy-start.51 = (f32[2,11,256]{2,0,1:T(2,128)S(1)}, f32[2,11,256]{2,0,1:T(2,128)}, u32[]{:S(2)}) copy-start(f32[2,11,256]{2,0,1:T(2,128)} %param.29) | copy-start | bytes 67588
  370.4 7.8 %copy-start.47 = (bf16[35,8,4,256]{3,1,2,0:T(8,128)(2,1)S(1)}, bf16[35,8,4,256]{3,1,2,0:T(8,128)(2,1)}, u32[]{:S(2)}) copy-start(bf16[35,8,4,256]{3,1,2,0:T(8,128)(2,1)} %copy-done.46) | copy-start | bytes 1720324
  373.6 44.2 %all-to-all-start.3 = ((bf16[4,276,768]{2,1,0:T(8,128)(2,1)}), bf16[4,276,768]{2,1,0:T(8,128)(2,1)}, u32[]{:S(2)}, u32[]{:S(2)}) async-start(bf16[4,276,768]{2,1,0:T(8,128)(2,1)} %copy.84), calls=%async_computation.3 | async-start | bytes 3440640 | tf_op jit(solution)/shard_map/all_to_all | solution.py:615
  387.6 7.1 copy-start.62
  421.9 8.6 %copy-start.36 = (f32[276,1024]{1,0:T(8,128)S(1)}, f32[276,1024]{1,0:T(8,128)}, u32[]{:S(2)}) copy-start(f32[276,1024]{1,0:T(8,128)} %copy-done.35) | copy-start | bytes 3391492
  421.9 8.6 %copy-start.55 = (f32[276]{0:T(512)S(1)}, f32[276]{0:T(512)}, u32[]{:S(2)}) copy-start(f32[276]{0:T(512)} %copy-done.54) | copy-start | bytes 3316
  421.9 8.6 %copy-start.57 = (f32[1,1024]{1,0:T(1,128)S(1)}, f32[1,1024]{1,0:T(1,128)}, u32[]{:S(2)}) copy-start(f32[1,1024]{1,0:T(1,128)} %copy-done.56) | copy-start | bytes 12292
  421.9 8.6 %copy-start.59 = (f32[276]{0:T(512)S(1)}, f32[276]{0:T(512)}, u32[]{:S(2)}) copy-start(f32[276]{0:T(512)} %copy-done.58) | copy-start | bytes 3316
  624.0 19.7 %slice-start = ((s8[8388608]{0:T(1024)(128)(4,1)}), s8[4194304]{0:T(1024)(128)(4,1)S(1)}, s32[]{:S(2)}) async-start(s8[8388608]{0:T(1024)(128)(4,1)} %bitcast.272), calls=%async_computation.4 | async-start | bytes 8388608
  632.3 7.3 copy-start.33
  632.3 11.4 %slice-start.1 = ((s8[8388608]{0:T(1024)(128)(4,1)}), s8[4194304]{0:T(1024)(128)(4,1)S(1)}, s32[]{:S(2)}) async-start(s8[8388608]{0:T(1024)(128)(4,1)} %bitcast.272), calls=%async_computation.5 | async-start | bytes 8388608
  659.1 11.6 %copy-start.17 = (f32[4,2,2,2,2,16,1024]{6,5,4,3,2,1,0:T(8,128)}, f32[4,2,2,2,2,16,1024]{6,5,4,3,2,1,0:T(8,128)S(1)}, u32[]{:S(2)}) copy-start(f32[4,2,2,2,2,16,1024]{6,5,4,3,2,1,0:T(8,128)S(1)} %convert_element_type.250) | copy-start | bytes 12582916
  677.1 25.2 %copy-start.50 = (f32[11,256]{1,0:T(8,128)}, f32[11,256]{1,0:T(8,128)S(1)}, u32[]{:S(2)}) copy-start(f32[11,256]{1,0:T(8,128)S(1)} %get-tuple-element.140) | copy-start | bytes 33796
  693.0 9.3 %copy-start.63 = (f32[2,6]{1,0:T(2,128)}, f32[2,6]{1,0:T(2,128)S(1)}, u32[]{:S(2)}) copy-start(f32[2,6]{1,0:T(2,128)S(1)} %sqrt.47) | copy-start | bytes 148
  (51 other events, 190.9 us)

commit v3 on v2

--- a/solution.py
+++ b/solution.py
@@ -8,6 +8,8 @@
 from jax.experimental.pallas import tpu as pltpu
 from jax.sharding import PartitionSpec as P
 
+HEADS = 16
+HEAD_DIM = 64
 MESH = pl.DeviceIdType.MESH
 LOW = jnp.bfloat16
 ANY = pl.BlockSpec(memory_space=pl.ANY)
@@ -565,10 +567,6 @@
     return sums, outs[5][: table.shape[0]]
 
 
-HEADS = 16
-HEAD_DIM = 64
-
-
 step_rate = 0.3
 
 
@@ -615,6 +613,408 @@
     rows = lax.all_to_all(rows, "shard", 0, 0, tiled=True)
     rows = rows.reshape(shards, sequences * portion, parts, width).transpose(1, 2, 0, 3)
     return rows.reshape(sequences * portion, parts * shards * width)
+
+
+def weight_tile(whole, shard, group, start, width):
+    return whole[shard, group, :, :, :, :, :, pl.ds(start, width)].reshape(256, width)
+
+
+def product(left, whole, start, width):
+    groups = whole.shape[1]
+    total = None
+    for shard in range(SHARDS):
+        for group in range(groups):
+            first = (shard * groups + group) * 256
+            term = jnp.dot(
+                left[:, first : first + 256],
+                weight_tile(whole, shard, group, start, width),
+                preferred_element_type=jnp.float32,
+            )
+            total = term if total is None else total + term
+    return total
+
+
+def contract(left, right, left_axis, right_axis):
+    return lax.dot_general(
+        left, right, (((left_axis,), (right_axis,)), ((), ())), preferred_element_type=jnp.float32
+    )
+
+
+def norm_rows(source, gain, bias, target, rows):
+    @pl.loop(0, rows // 32)
+    def _(block):
+        where = pl.ds(pl.multiple_of(block * 32, 32), 32)
+        stream = source[where, :]
+        center = stream - jnp.mean(stream, -1, keepdims=True)
+        spread = jnp.mean(center * center, -1, keepdims=True)
+        target[where, :] = (center * lax.rsqrt(spread + 1e-05) * gain + bias).astype(LOW)
+
+
+def forward_kernel(chunks, portion, *refs):
+    joined, vectors = refs[0:2]
+    masters = refs[2:7]
+    keeps = refs[7:12]
+    (entering, first_in, heads, log_total, mixed, middle, second_in, expanded, activated, out) = (
+        refs[12:22]
+    )
+    wholes = refs[22:27]
+    (
+        wide,
+        table_own,
+        table_all,
+        table,
+        outgoing,
+        answer,
+        load_sems,
+        keep_sems,
+        send_sems,
+        recv_sems,
+        more_send,
+        more_recv,
+    ) = refs[27:]
+    place = Place()
+    s, k, x, y = place.shard, place.core, place.x, place.y
+    total = len(chunks)
+    rows = entering.shape[0]
+    width = entering.shape[1]
+    own = width // SHARDS
+    factor = 1.0 / math.sqrt(HEAD_DIM)
+
+    def load(at):
+        index, group, part = chunks[at]
+        return pltpu.make_async_copy(
+            masters[index].at[group, :, :, :, :, :, pl.ds(part * BLOCK, BLOCK)],
+            wide.at[at % 2],
+            load_sems.at[at % 2],
+        )
+
+    def whole(at, shard, *rest):
+        index, group, part = chunks[at]
+        rest = rest + (slice(None),) * (5 - len(rest))
+        return wholes[index].at[(shard, group) + rest + (pl.ds(part * BLOCK, BLOCK),)]
+
+    sent = []
+    arrivals = {}
+
+    def go(at, name, position, ref, device):
+        slot = at * 18 + position
+        copy = pltpu.make_async_remote_copy(
+            src_ref=ref,
+            dst_ref=ref,
+            send_sem=send_sems.at[slot],
+            recv_sem=recv_sems.at[slot],
+            device_id=device,
+            device_id_type=MESH,
+        )
+        copy.start()
+        sent.append(copy)
+        arrivals.setdefault((at, name), []).append(copy)
+
+    def arrived(at, name):
+        for copy in arrivals[(at, name)]:
+            copy.wait_recv()
+
+    def extra(slot, source, target, device):
+        copy = pltpu.make_async_remote_copy(
+            src_ref=source,
+            dst_ref=target,
+            send_sem=more_send.at[slot],
+            recv_sem=more_recv.at[slot],
+            device_id=device,
+            device_id_type=MESH,
+        )
+        copy.start()
+        sent.append(copy)
+        return copy
+
+    kept = []
+
+    def stage_cast(at):
+        index, group, part = chunks[at]
+        load(at).wait()
+
+        @pl.loop(0, 16)
+        def _(row):
+            a, b = row // 8, lax.rem(row // 4, 2)
+            c, d = lax.rem(row // 2, 2), lax.rem(row, 2)
+            wholes[index][s, group, a, b, c, d, :, part * BLOCK : (part + 1) * BLOCK] = wide[
+                at % 2, a, b, c, d
+            ].astype(LOW)
+
+        if at + 2 < total:
+            load(at + 2).start()
+
+    def stage_z(at):
+        for offset in range(1, SHARDS):
+            go(at, "z", offset - 1, whole(at, s, k, slice(None), y, x), place.along(offset))
+
+    def stage_first(at):
+        arrived(at, "z")
+        for offset in range(1, SHARDS):
+            e = place.source(offset)
+            go(at, "first", 3 + 2 * (offset - 1), whole(at, e, k, 0, y, x), place.across("x"))
+            go(at, "first", 4 + 2 * (offset - 1), whole(at, e, k, 1, y, x), place.across("y"))
+
+    def stage_second(at):
+        arrived(at, "first")
+        for offset in range(1, SHARDS):
+            e = place.source(offset)
+            go(at, "second", 9 + 2 * (offset - 1), whole(at, e, k, 0, y), place.across("y"))
+            ref = whole(at, e, k, 1, slice(None), x)
+            go(at, "second", 10 + 2 * (offset - 1), ref, place.across("x"))
+
+    def stage_core(at):
+        arrived(at, "second")
+        for offset in range(1, SHARDS):
+            e = place.source(offset)
+            go(at, "core", 15 + offset - 1, whole(at, e, k), place.across("core"))
+
+    def stage_end(at):
+        arrived(at, "core")
+        index, group, part = chunks[at]
+        copy = pltpu.make_async_copy(
+            whole(at, slice(None)),
+            keeps[index].at[:, group, :, :, :, :, :, pl.ds(part * BLOCK, BLOCK)],
+            keep_sems.at[at],
+        )
+        copy.start()
+        kept.append(copy)
+
+    stages = (stage_z, stage_first, stage_second, stage_core, stage_end)
+    lead = 4
+    step_now = [0]
+
+    def advance():
+        step = step_now[0]
+        if step >= total + 3:
+            return False
+        for position in range(1, 5):
+            at = step - (position - 1)
+            if 0 <= at < total:
+                stages[position](at)
+        if step + lead < total:
+            stage_cast(step + lead)
+            stage_z(step + lead)
+        step_now[0] = step + 1
+        return True
+
+    def until(at):
+        while step_now[0] - 4 < at:
+            advance()
+
+    load(0).start()
+    load(1).start()
+    table_own[...] = vectors[...].astype(LOW)
+    table_all[0] = vectors[...].astype(LOW)
+    greet(place)
+    table_copies = []
+    for at in range(min(lead, total)):
+        stage_cast(at)
+        stage_z(at)
+        if at == 0:
+            for offset in range(1, SHARDS):
+                table_copies.append(
+                    extra(offset - 1, table_own, table_all.at[offset], place.along(offset))
+                )
+    last = {}
+    for at, (index, group, part) in enumerate(chunks):
+        last[index] = at
+
+    until(0)
+    for copy in table_copies:
+        copy.wait_recv()
+    for offset in range(SHARDS):
+        column = pl.multiple_of(place.source(offset) * own, own)
+        table[:, pl.ds(column, own)] = table_all[offset].astype(jnp.float32)
+    until(last[0])
+
+    @pl.loop(0, width // 256)
+    def _(part):
+        start = pl.multiple_of(part * 256, 256)
+        entering[:, pl.ds(start, 256)] = (
+            product(joined, wholes[0], start, 256) + table[0:1, pl.ds(start, 256)]
+        )
+
+    norm_rows(entering, table[1:2, :], table[2:3, :], first_in, rows)
+    until(last[1])
+    live = lax.broadcasted_iota(jnp.int32, (rows, own), 0) < portion
+    for kind in range(3):
+
+        @pl.loop(0, SHARDS)
+        def _(target):
+            start = pl.multiple_of(kind * width + target * own, own)
+            outgoing[target, :, kind * own : (kind + 1) * own] = jnp.where(
+                live, product(first_in, wholes[1], start, own), 0.0
+            ).astype(LOW)
+
+    head_copies = []
+    for offset in range(1, SHARDS):
+        target = lax.rem(s + offset, SHARDS)
+        head_copies.append(
+            extra(
+                2 + offset,
+                outgoing.at[target],
+                heads.at[pl.ds(offset * rows, rows), :],
+                place.along(offset),
+            )
+        )
+
+    @pl.loop(0, rows // 32)
+    def _(block):
+        where = pl.ds(pl.multiple_of(block * 32, 32), 32)
+        heads[where, :] = outgoing[s, where, :]
+
+    advance()
+    advance()
+    for copy in head_copies:
+        copy.wait_recv()
+
+    everyone = SHARDS * rows
+    tile = 384
+    lane = lax.broadcasted_iota(jnp.int32, (tile, 128), 1)
+    key_row = lax.broadcasted_iota(jnp.int32, (everyone, tile), 0)
+    for pair in range(own // 128):
+
+        @pl.loop(0, everyone // tile)
+        def _(block):
+            start = pl.multiple_of(block * tile, 128)
+            where = pl.ds(start, tile)
+            query = heads[where, pair * 128 : (pair + 1) * 128]
+            keys = heads[:, own + pair * 128 : own + (pair + 1) * 128]
+            values = heads[:, 2 * own + pair * 128 : 2 * own + (pair + 1) * 128]
+            parts = []
+            for half in range(2):
+                inside = (lane // 64) == half
+                picked = jnp.where(inside, query.astype(jnp.float32) * factor, 0.0).astype(LOW)
+                scores = contract(keys, picked, 1, 1)
+                scores = jnp.where(lax.rem(key_row, rows) < portion, scores, -1e30)
+                top = jnp.max(scores, 0, keepdims=True)
+                weight = jnp.exp(scores - top)
+                weight_sum = jnp.sum(weight, 0, keepdims=True)
+                log_total[2 * pair + half : 2 * pair + half + 1, pl.ds(start, tile)] = (
+                    top + jnp.log(weight_sum)
+                )
+                weight = (weight * (1.0 / weight_sum)).astype(LOW)
+                summed = contract(values, weight, 0, 0)
+                parts.append(summed[half * 64 : (half + 1) * 64])
+            both = jnp.concatenate(parts, 0)
+            answer[where, pair * 128 : (pair + 1) * 128] = both.T.astype(LOW)
+
+        advance()
+
+    answer_copies = []
+    column = pl.multiple_of(s * own, own)
+    for offset in range(1, SHARDS):
+        answer_copies.append(
+            extra(
+                5 + offset,
+                answer.at[pl.ds(offset * rows, rows), :],
+                mixed.at[:, pl.ds(column, own)],
+                (place.rep, place.source(offset)),
+            )
+        )
+    mixed[:, pl.ds(column, own)] = answer[0:rows, :]
+    until(last[2])
+    for copy in answer_copies:
+        copy.wait_recv()
+
+    @pl.loop(0, width // 256)
+    def _(part):
+        start = pl.multiple_of(part * 256, 256)
+        where = pl.ds(start, 256)
+        middle[:, where] = (
+            entering[:, where] + product(mixed, wholes[2], start, 256) + table[3:4, where]
+        )
+
+    norm_rows(middle, table[4:5, :], table[5:6, :], second_in, rows)
+    per_row = width // 256
+    for part in range(expanded.shape[1] // BLOCK):
+        until(last[2] + 1 + part)
+
+        @pl.loop(0, BLOCK // 256)
+        def _(piece):
+            start = pl.multiple_of(part * BLOCK + piece * 256, 256)
+            bias_at = pl.multiple_of(piece * 256, 256)
+            value = (
+                product(second_in, wholes[3], start, 256)
+                + table[7 + part : 8 + part, pl.ds(bias_at, 256)]
+            )
+            expanded[:, pl.ds(start, 256)] = value
+            activated[:, pl.ds(start, 256)] = (
+                value * (0.5 + 0.5 * lax.erf(value * math.sqrt(0.5)))
+            ).astype(LOW)
+
+    until(last[4])
+
+    @pl.loop(0, width // 256)
+    def _(part):
+        start = pl.multiple_of(part * 256, 256)
+        where = pl.ds(start, 256)
+        out[:, where] = (
+            middle[:, where] + product(activated, wholes[4], start, 256) + table[6:7, where]
+        ).astype(LOW)
+
+    for copy in sent:
+        copy.wait_send()
+    for copy in kept:
+        copy.wait()
+
+
+def forward_pass(joined, vectors, masters, portion):
+    shapes = [(matrix.shape[0] * SHARDS, matrix.shape[1]) for matrix in masters]
+    chunks = chunk_list(shapes)
+    total = len(chunks)
+    rows = joined.shape[0]
+    width = joined.shape[1] // 2
+    own = width // SHARDS
+    hidden = shapes[3][1]
+    everyone = SHARDS * rows
+    split = [
+        matrix.reshape(matrix.shape[0] // 256, 2, 2, 2, 2, UNIT, matrix.shape[1])
+        for matrix in masters
+    ]
+    folds = [(SHARDS, r // SHARDS // 256, 2, 2, 2, 2, UNIT, c) for r, c in shapes]
+    inner = pl.BlockSpec(memory_space=pltpu.VMEM)
+    table = jnp.pad(vectors, ((0, 16 - vectors.shape[0]), (0, 0)))
+    outs = pl.pallas_call(
+        functools.partial(forward_kernel, chunks, portion),
+        out_shape=[jax.ShapeDtypeStruct(fold, LOW) for fold in folds]
+        + [
+            jax.ShapeDtypeStruct((rows, width), jnp.float32),
+            jax.ShapeDtypeStruct((rows, width), LOW),
+            jax.ShapeDtypeStruct((everyone, 3 * own), LOW),
+            jax.ShapeDtypeStruct((8, everyone), jnp.float32),
+            jax.ShapeDtypeStruct((rows, width), LOW),
+            jax.ShapeDtypeStruct((rows, width), jnp.float32),
+            jax.ShapeDtypeStruct((rows, width), LOW),
+            jax.ShapeDtypeStruct((rows, hidden), jnp.float32),
+            jax.ShapeDtypeStruct((rows, hidden), LOW),
+            jax.ShapeDtypeStruct((rows, width), LOW),
+        ],
+        in_specs=[inner] * 2 + [ANY] * 5,
+        out_specs=[ANY] * 5 + [inner] * 10,
+        scratch_shapes=[pltpu.VMEM(fold, LOW) for fold in folds]
+        + [
+            pltpu.VMEM((2, 2, 2, 2, 2, UNIT, BLOCK), jnp.float32),
+            pltpu.VMEM((16, own), LOW),
+            pltpu.VMEM((SHARDS, 16, own), LOW),
+            pltpu.VMEM((16, width), jnp.float32),
+            pltpu.VMEM((SHARDS, rows, 3 * own), LOW),
+            pltpu.VMEM((everyone, own), LOW),
+            pltpu.SemaphoreType.DMA((2,)),
+            pltpu.SemaphoreType.DMA((total,)),
+            pltpu.SemaphoreType.DMA((total * 18,)),
+            pltpu.SemaphoreType.DMA((total * 18,)),
+            pltpu.SemaphoreType.DMA((9,)),
+            pltpu.SemaphoreType.DMA((9,)),
+        ],
+        compiler_params=pltpu.CompilerParams(
+            collective_id=1, has_side_effects=True, vmem_limit_bytes=60 * 2**20
+        ),
+        name="forward_pass",
+    )(joined, table, *split)
+    weights = [out.reshape(shape) for out, shape in zip(outs[:5], shapes)]
+    return weights, outs[5:]
 
 
 def fits(shards, replicas, masters):
@@ -669,43 +1069,78 @@
     row_count = sequences * portion
     factor = 1.0 / math.sqrt(HEAD_DIM)
     masters = (skip_weight, heads_in, heads_out, expand_weight, reduce_weight, vectors)
-    fast = fits(shards, replicas, masters[:5])
-    gathered = gather_weights(masters[:5]) if fast else gather_plain(masters[:5])
-    skip_matrix, in_matrix, out_matrix, expand_matrix, reduce_matrix = gathered
-    table_low = lax.all_gather(vectors.astype(jnp.bfloat16), "shard", axis=1, tiled=True)
-    table_rows = table_low.astype(jnp.float32)
-    source = hidden_in.reshape(row_count, model_width)
-    skip_rows = skip_path.reshape(row_count, model_width)
-    joined = jnp.concatenate([source, skip_rows], 1)
-    entering = matmul(joined, skip_matrix) + table_rows[0]
-    normed_one, norm_back_one = jax.vjp(normalize, entering, table_rows[1], table_rows[2])
-    first_in = normed_one.astype(jnp.bfloat16)
-    triple = matmul(first_in, in_matrix).astype(jnp.bfloat16)
-    heads = to_heads(triple, sequences, portion, shards)
-    queries, keys_full, values_full = heads[:, :, 0], heads[:, :, 1], heads[:, :, 2]
-    scores = (
-        jnp.einsum("sqhd,skhd->shqk", queries, keys_full, preferred_element_type=jnp.float32)
-        * factor
-    )
-    row_max = jnp.max(scores, -1)
-    row_total = jnp.sum(jnp.exp(scores - row_max[..., None]), -1)
-    log_total = row_max + jnp.log(row_total)
-    probability = jnp.exp(scores - log_total[..., None])
-    mixed = jnp.einsum(
-        "shqk,skhd->sqhd",
-        probability.astype(jnp.bfloat16),
-        values_full,
-        preferred_element_type=jnp.float32,
-    )
-    mixed_low = to_tokens(mixed.astype(jnp.bfloat16)[:, :, None], sequences, portion, shards)
-    middle = entering + matmul(mixed_low, out_matrix) + table_rows[3]
-    normed_two, norm_back_two = jax.vjp(normalize, middle, table_rows[4], table_rows[5])
-    second_in = normed_two.astype(jnp.bfloat16)
-    expanded = matmul(second_in, expand_matrix) + table_rows[7:].reshape(-1)
-    activated, gelu_back = jax.vjp(exact_gelu, expanded)
-    activated_low = activated.astype(jnp.bfloat16)
-    block_result = middle + matmul(activated_low, reduce_matrix) + table_rows[6]
-    block_out = block_result.astype(jnp.bfloat16).reshape(sequences, portion, model_width)
+    fast = sequences == 1 and fits(shards, replicas, masters[:5])
+    joined = jnp.concatenate(
+        [hidden_in.reshape(row_count, model_width), skip_path.reshape(row_count, model_width)], 1
+    )
+    if fast:
+        padded = -(-portion // 32) * 32
+        gathered, kept = forward_pass(
+            jnp.pad(joined, ((0, padded - portion), (0, 0))), vectors, masters[:5], portion
+        )
+        entering, first_in, heads, log_total = kept[:4]
+        mixed_low, middle, second_in, expanded, activated_low, block_out = [
+            rows[:portion] for rows in kept[4:]
+        ]
+        entering, first_in = entering[:portion], first_in[:portion]
+        block_out = block_out.reshape(sequences, portion, model_width)
+        own = HEADS * HEAD_DIM // shards
+        heads = heads.reshape(shards, padded, 3 * own)[:, :portion]
+        order = lax.rem(lax.axis_index("shard") + shards - jnp.arange(shards), shards)
+        heads = jnp.zeros_like(heads).at[order].set(heads)
+        heads = heads.reshape(1, shards * portion, 3, own // HEAD_DIM, HEAD_DIM)
+        queries, keys_full, values_full = heads[:, :, 0], heads[:, :, 1], heads[:, :, 2]
+        log_total = log_total[: own // HEAD_DIM].reshape(-1, shards, padded)[:, :, :portion]
+        log_total = jnp.zeros_like(log_total).at[:, order].set(log_total)
+        log_total = log_total.reshape(1, -1, shards * portion)
+        scores = (
+            jnp.einsum("sqhd,skhd->shqk", queries, keys_full, preferred_element_type=jnp.float32)
+            * factor
+        )
+        probability = jnp.exp(scores - log_total[..., None])
+        table_low = lax.all_gather(vectors.astype(LOW), "shard", axis=1, tiled=True)
+        table_rows = table_low.astype(jnp.float32)
+        norm_back_one = jax.vjp(normalize, entering, table_rows[1], table_rows[2])[1]
+        norm_back_two = jax.vjp(normalize, middle, table_rows[4], table_rows[5])[1]
+        gelu_back = jax.vjp(exact_gelu, expanded)[1]
+        skip_matrix, in_matrix, out_matrix, expand_matrix, reduce_matrix = gathered
+    else:
+        gathered = gather_plain(masters[:5])
+        skip_matrix, in_matrix, out_matrix, expand_matrix, reduce_matrix = gathered
+        table_low = lax.all_gather(vectors.astype(jnp.bfloat16), "shard", axis=1, tiled=True)
+        table_rows = table_low.astype(jnp.float32)
+        source = hidden_in.reshape(row_count, model_width)
+        skip_rows = skip_path.reshape(row_count, model_width)
+        joined = jnp.concatenate([source, skip_rows], 1)
+        entering = matmul(joined, skip_matrix) + table_rows[0]
+        normed_one, norm_back_one = jax.vjp(normalize, entering, table_rows[1], table_rows[2])
+        first_in = normed_one.astype(jnp.bfloat16)
+        triple = matmul(first_in, in_matrix).astype(jnp.bfloat16)
+        heads = to_heads(triple, sequences, portion, shards)
+        queries, keys_full, values_full = heads[:, :, 0], heads[:, :, 1], heads[:, :, 2]
+        scores = (
+            jnp.einsum("sqhd,skhd->shqk", queries, keys_full, preferred_element_type=jnp.float32)
+            * factor
+        )
+        row_max = jnp.max(scores, -1)
+        row_total = jnp.sum(jnp.exp(scores - row_max[..., None]), -1)
+        log_total = row_max + jnp.log(row_total)
+        probability = jnp.exp(scores - log_total[..., None])
+        mixed = jnp.einsum(
+            "shqk,skhd->sqhd",
+            probability.astype(jnp.bfloat16),
+            values_full,
+            preferred_element_type=jnp.float32,
+        )
+        mixed_low = to_tokens(mixed.astype(jnp.bfloat16)[:, :, None], sequences, portion, shards)
+        middle = entering + matmul(mixed_low, out_matrix) + table_rows[3]
+        normed_two, norm_back_two = jax.vjp(normalize, middle, table_rows[4], table_rows[5])
+        second_in = normed_two.astype(jnp.bfloat16)
+        expanded = matmul(second_in, expand_matrix) + table_rows[7:].reshape(-1)
+        activated, gelu_back = jax.vjp(exact_gelu, expanded)
+        activated_low = activated.astype(jnp.bfloat16)
+        block_result = middle + matmul(activated_low, reduce_matrix) + table_rows[6]
+        block_out = block_result.astype(jnp.bfloat16).reshape(sequences, portion, model_width)
     grad_out = cotangent.reshape(row_count, model_width)
     grad_reduce = matmul(activated_low.T, grad_out)
     grad_act = matmul(grad_out, reduce_matrix.T)

time: 747 us -> 690 us (0.924)
  Pallas kernels: 284 us -> 354 us
  blocking collectives: 76.1 us -> 24.6 us
  matrix products: 121 us -> 91.1 us
  waiting for transfers between devices: 35 us -> 13.7 us
  local copies, waits for them, and re-layouts: 86.5 us -> 67.5 us
    pallas_call x1, Pallas kernels: 114 us -> 182 us  [forward_pass(): pl.pallas_call(functools.partial(forward_kernel, chunks, portion), out_sh...]
    all_to_all x1 -> x0, blocking collectives: 50.1 us -> none  [to_heads(): blocks = lax.all_to_all(blocks, 'shard', 0, 0, tiled=True)]
    dot_general x15 -> x10, matrix products: 74.7 us -> 54.7 us  [matmul(): return jnp.dot(left, right, preferred_element_type=jnp.float32)]
    all_to_all x2 -> x1, waiting for transfers between devices: 30.9 us -> 13.7 us  [to_tokens(): rows = lax.all_to_all(rows, 'shard', 0, 0, tiled=True)]
    dot_general x1 -> x0, matrix products: 10.8 us -> none  [on_device(): jnp.einsum('shqk,skhd->sqhd', probability.astype(jnp.bfloat16), values_fu...]
    reduce_sum x1 -> x0, other arithmetic: 9.51 us -> none  [on_device(): row_total = jnp.sum(jnp.exp(scores - row_max[..., None]), -1)]
    unnamed x165 -> x114, local copies, waits for them, and re-layouts: 28.3 us -> 19.1 us
    another operation x4 -> x1, local copies, waits for them, and re-layouts: 9.37 us -> 0.52 us  [the longest x2 5.17 us: to_tokens(): rows = rows.reshape(shards, sequences * portion, parts * width)]
  transfers between devices with their start and end apart: 3 -> 2, of which waited for: 3 -> 1; matrix products, arithmetic and copies ran while one was open for 5% -> 6% of each run, Pallas kernels for 0% -> 0%
where the time goes in v3:
time: 690 us; the launch traced here: 680 us
  Pallas kernels  354 us (51%)
  other arithmetic  115 us (17%)
  matrix products  91.1 us (13%)
  local copies, waits for them, and re-layouts  67.5 us (10%)
  blocking collectives  24.6 us (4%)
  waiting for transfers between devices  13.7 us (2%)
  starting transfers between devices  9.74 us (1%)
    pallas_call x1, Pallas kernels, forward_pass(): pl.pallas_call(functools.partial(forward_kernel, chunks, portion), out_sh...  182 us
    pallas_call x1, Pallas kernels, reduce_gradients(): pl.pallas_call(functools.partial(reduce_kernel, chunks), out_shape=[jax.S...  171 us
    dot_general x10, matrix products, matmul(): return jnp.dot(left, right, preferred_element_type=jnp.float32)  54.7 us
    reduce_sum x6, other arithmetic, on_device(): jnp.sum(direction * direction)  24.8 us
    add x5, other arithmetic, moment_step(): first_moment = 0.5 * moments[0] + 0.5 * gradient  23.5 us
    another operation x7, other arithmetic, moment_step(): return (jnp.stack([first_moment, root_square]), direction)  19.2 us
    unnamed x114, local copies, waits for them, and re-layouts  19.1 us
  transfers between devices with their start and end apart: 2, of which 1 were waited for; matrix products, arithmetic and copies ran while one was open for 6% of the time, Pallas kernels for 0%

profile of v3, /device:TPU:0, one launch (start us, length us, event | category | flops | bytes accessed | tf_op | source)
XLA Modules:
  0.0 680.4 jit_solution(13106636739951048665)
XLA Ops:
  5.8 182.2 %forward_pass.1 = (bf16[4,2,2,2,2,2,16,1024]{7,6,5,4,3,2,1,0:T(8,128)(2,1)}, bf16[4,1,2,2,2,2,16,3072]{7,6,5,4,3,2,1,0:T(8,128)(2,1)}, bf16[4,1,2,2,2,2,16,1024]...) custom-call(bf16[288,2048]{1,0:T(8,128)(2,1)} %pad.12.refs_0_, ...), custom_call_target="tpu_custom_call" | custom-call | tf_op jit(solution)/shard_map/forward_pass/pallas_call | solution.py:979
  191.0 13.3 %all_gather.3 = bf16[11,1024]{1,0:T(8,128)(2,1)S(1)} all-gather(bf16[11,256]{1,0:T(8,128)(2,1)S(1)} %get-tuple-element.200), channel_id=1, replica_groups=mesh['rep'=8,'shard'=4] {'shard'}, dimensions={1}, use_global_device_ids=true | all-gather | bytes 28160 | tf_op jit(solution)/shard_map/all_gather | solution.py:1101
  206.5 15.9 %convert_reduce_fusion = (f32[4096]{0:T(1024)S(1)}, bf16[276,4096]{1,0:T(8,128)(2,1)S(1)}) fusion(bf16[4096,1024]{1,0:T(8,128)(2,1)} %bitcast.268, bf16[1,276,1024]{2,1,0:T(8,128)(2,1)S(1)} %copy-done.30, f32[288,4096]{1,0:T(8,128)} %get-tuple-element.44), kind=kOutput, calls=%fused_computation.36 | convolution fusion | flops 2398908416 | bytes 15753216 | tf_op jit(solution)/shard_map/dot_general | solution.py:584
  231.2 4.5 all-to-all-start
  241.8 4.8 reshape.498
  255.6 8.4 %fusion.58 = f32[4,1104,1104]{1,2,0:T(8,128)} fusion(bf16[1104,4,64]{0,2,1:T(8,128)(2,1)S(1)} %reshape.505, bf16[1,1104,3,4,64]{1,4,3,2,0:T(8,128)(2,1)S(1)} %copy-done.18), kind=kOutput, calls=%fused_computation.154 | convolution fusion | flops 624033792 | bytes 20680704 | tf_op jit(solution)/shard_map/sqhd,skhd->shqk/dot_general | solution.py:1156
  264.0 13.1 %multiply_reduce_fusion = (f32[4,1104]{1,0:T(4,128)S(1)}, f32[4,1104,1104]{1,2,0:T(8,128)}) fusion(f32[4,1104,1104]{1,2,0:T(8,128)} %fusion.58, f32[4,1104]{1,0:T(4,128)S(1)} %sub.71, bf16[1,1104,3,4,64]{1,4,3,2,0:T(8,128)(2,1)S(1)} %copy-done.18), kind=kOutput, calls=%fused_computation.6 | convolution fusion | flops 643530432 | bytes 40217856 | tf_op jit(solution)/shard_map/sqhd,skhd->shqk/dot_general | solution.py:1097
  277.1 9.9 %fusion.41 = bf16[1,1104,1,4,64]{1,4,3,2,0:T(8,128)(2,1)S(1)} fusion(bf16[1104,4,64]{0,2,1:T(8,128)(2,1)S(1)} %reshape.505, f32[4,1104,1104]{1,2,0:T(8,128)} %get-tuple-element.211), kind=kOutput, calls=%fused_computation.102 | convolution fusion | flops 629191680 | bytes 20631552 | tf_op jit(solution)/shard_map/shqk,sqhd->skhd/dot_general | solution.py:1169
  287.0 13.6 %multiply_convert_fusion = bf16[4,1104,1104]{1,2,0:T(8,128)(2,1)S(1)} fusion(f32[4,1104,1104]{1,2,0:T(8,128)} %get-tuple-element.211, f32[4,1104,1104]{1,2,0:T(8,128)} %fusion.58, f32[4,1104]{1,0:T(4,128)S(1)} %get-tuple-element.210), kind=kLoop, calls=%fused_computation.5 | loop fusion | flops 14625792 | bytes 48770304 | tf_op jit(solution)/shard_map/convert_element_type | solution.py:1160
  307.0 4.6 convert_element_type.187
  314.8 5.2 all-to-all-start.1
  324.8 4.0 stack.131
  332.1 6.9 %convolution_convert_fusion.1 = bf16[1024,4096]{1,0:T(8,128)(2,1)} fusion(bf16[276,4096]{1,0:T(8,128)(2,1)S(1)} %copy-done.49, bf16[288,1024]{1,0:T(8,128)(2,1)S(1)} %copy-done.47), kind=kOutput, calls=%fused_computation.12 | convolution fusion | flops 2319450112 | bytes 11255808 | tf_op jit(solution)/shard_map/dot_general | solution.py:584
  339.0 6.8 %convolution_convert_fusion = bf16[4096,1024]{1,0:T(8,128)(2,1)} fusion(bf16[288,4096]{1,0:T(8,128)(2,1)S(1)} %copy-done.44, bf16[1,276,1024]{2,1,0:T(8,128)(2,1)S(1)} %copy-done.31), kind=kOutput, calls=%fused_computation.11 | convolution fusion | flops 2319450112 | bytes 11255808 | tf_op jit(solution)/shard_map/dot_general | solution.py:584
  345.8 13.7 %all-to-all-done.1 = bf16[4,276,768]{2,1,0:T(8,128)(2,1)} async-done(((bf16[4,276,768]{2,1,0:T(8,128)(2,1)}), bf16[4,276,768]{2,1,0:T(8,128)(2,1)}, u32[]{:S(2)}, u32[]{:S(2)}) %all-to-all-start.1) | async-done | bytes 1695776 | tf_op jit(solution)/shard_map/all_to_all | solution.py:613
  359.5 4.1 reshape.507
  363.6 4.2 copy.80
  367.8 4.3 reshape.508
  372.2 5.7 multiply_reduce_fusion.10
  379.5 4.4 convolution_convert_fusion.3
  384.0 5.4 convolution_convert_fusion.2
  391.8 171.4 %reduce_gradients.1 = (bf16[2,2,2,2,2,16,1024]{6,5,4,3,2,1,0:T(8,128)(2,1)S(1)}, bf16[1,2,2,2,2,16,3072]{6,5,4,3,2,1,0:T(8,128)(2,1)S(1)}, bf16[1,2,2,2,2,16,102...) custom-call(bf16[4,2,2,2,2,2,16,1024]{7,6,5,4,3,2,1,0:T(8,128)(2,1)S, ...), custom_call_target="tpu_custom_call" | custom-call | tf_op jit(solution)/shard_map/reduce_gradients/pallas_call | solution.py:533
  563.2 8.3 %multiply_reduce_fusion.5 = (f32[]{:T(128)}, f32[256,3072]{1,0:T(8,128)}, f32[256,3072]{1,0:T(8,128)}) fusion(f32[2,256,3072]{2,1,0:T(8,128)} %param.25, bf16[1,2,2,2,2,16,3072]{6,5,4,3,2,1,0:T(8,128)(2,1)S(1)} %get-tuple-element.59), kind=kLoop, calls=%fused_computation.85 | loop fusion | flops 9437183 | bytes 14155780 | tf_op jit(solution)/shard_map/reduce_sum | solution.py:1226
  571.5 7.2 %multiply_add_fusion.5 = (f32[1,256,3072]{2,1,0:T(8,128)}, f32[1,256,3072]{2,1,0:T(8,128)}) fusion(f32[2,256,3072]{2,1,0:T(8,128)} %param.25, bf16[1,2,2,2,2,16,3072]{6,5,4,3,2,1,0:T(8,128)(2,1)S(1)} %get-tuple-element.59), kind=kLoop, calls=%fused_computation.55 | loop fusion | flops 6291456 | bytes 14155776 | tf_op jit(solution)/shard_map/add | solution.py:592
  582.9 5.6 multiply_reduce_fusion.2
  588.5 5.5 multiply_add_fusion.3
  608.2 4.7 multiply_reduce_fusion.1
  612.8 5.9 multiply_add_fusion.2
  623.9 11.3 %psum.7 = f32[2,6]{1,0:T(2,128)S(1)} all-reduce(f32[2,6]{1,0:T(2,128)S(1)} %pad_maximum_fusion.8), channel_id=1, replica_groups=mesh['rep'=8,'shard'=4] {'shard'}, use_global_device_ids=true, to_apply=%region_31.32 | all-reduce | flops 12 | bytes 96 | tf_op jit(solution)/shard_map/psum | solution.py:1229
  639.8 5.0 pad_maximum_fusion.3
  652.0 4.8 pad_maximum_fusion
  658.5 4.2 pad_maximum_fusion.1
  (195 shorter events, 106.1 us)
Async XLA Ops:
  188.1 18.4 %copy-start.30 = (bf16[1,276,1024]{2,1,0:T(8,128)(2,1)S(1)}, bf16[1,276,1024]{2,1,0:T(8,128)(2,1)}, u32[]{:S(2)}) copy-start(bf16[1,276,1024]{2,1,0:T(8,128)(2,1)} %param.17) | copy-start | bytes 1695748
  204.3 19.4 %slice-start.4 = ((s8[8388608]{0:T(1024)(128)(4,1)}), s8[4194304]{0:T(1024)(128)(4,1)S(1)}, s32[]{:S(2)}) async-start(s8[8388608]{0:T(1024)(128)(4,1)} %bitcast.265), calls=%async_computation.6 | async-start | bytes 8388608
  206.5 17.3 %copy-start.22 = (f32[288,1024]{1,0:T(8,128)S(1)}, f32[288,1024]{1,0:T(8,128)}, u32[]{:S(2)}) copy-start(f32[288,1024]{1,0:T(8,128)} %get-tuple-element.47) | copy-start | bytes 3538948
  206.5 17.3 %slice-start.5 = ((s8[8388608]{0:T(1024)(128)(4,1)}), s8[4194304]{0:T(1024)(128)(4,1)S(1)}, s32[]{:S(2)}) async-start(s8[8388608]{0:T(1024)(128)(4,1)} %bitcast.265), calls=%async_computation.7 | async-start | bytes 8388608
  231.2 22.3 %all-to-all-start = ((bf16[4,276,256]{2,1,0:T(8,128)(2,1)}), bf16[4,276,256]{2,1,0:T(8,128)(2,1)}, u32[]{:S(2)}, u32[]{:S(2)}) async-start(bf16[4,276,256]{2,1,0:T(8,128)(2,1)} %bitcast.219), calls=%async_computation | async-start | bytes 1146880 | tf_op jit(solution)/shard_map/all_to_all | solution.py:603
  238.5 8.1 %copy-start.42 = (f32[8,1152]{1,0:T(8,128)S(1)}, f32[8,1152]{1,0:T(8,128)}, u32[]{:S(2)}) copy-start(f32[8,1152]{1,0:T(8,128)} %get-tuple-element.49) | copy-start | bytes 110596
  241.8 8.6 %copy-start.4 = (f32[256,3072]{1,0:T(8,128)S(1)}, f32[256,3072]{1,0:T(8,128)}, u32[]{:S(2)}) copy-start(f32[256,3072]{1,0:T(8,128)} %param.19) | copy-start | bytes 9437188
  311.6 8.4 %copy-start.23 = (f32[256,1024]{1,0:T(8,128)S(1)}, f32[256,1024]{1,0:T(8,128)}, u32[]{:S(2)}) copy-start(f32[256,1024]{1,0:T(8,128)} %param.20) | copy-start | bytes 3145732
  314.8 14.0 %copy-start.41 = (f32[2,11,256]{2,0,1:T(2,128)S(1)}, f32[2,11,256]{2,0,1:T(2,128)}, u32[]{:S(2)}) copy-start(f32[2,11,256]{2,0,1:T(2,128)} %param.29) | copy-start | bytes 67588
  314.8 14.0 %copy-start.38 = (bf16[288,1024]{1,0:T(8,128)(2,1)S(1)}, bf16[288,1024]{1,0:T(8,128)(2,1)}, u32[]{:S(2)}) copy-start(bf16[288,1024]{1,0:T(8,128)(2,1)} %get-tuple-element.43) | copy-start | bytes 1769476
  314.8 14.9 %copy-start.37 = (bf16[276,1024]{1,0:T(8,128)(2,1)S(1)}, bf16[276,1024]{1,0:T(8,128)(2,1)}, u32[]{:S(2)}) copy-start(bf16[276,1024]{1,0:T(8,128)(2,1)} %copy-done.36) | copy-start | bytes 1695748
  314.8 44.7 %all-to-all-start.1 = ((bf16[4,276,768]{2,1,0:T(8,128)(2,1)}), bf16[4,276,768]{2,1,0:T(8,128)(2,1)}, u32[]{:S(2)}, u32[]{:S(2)}) async-start(bf16[4,276,768]{2,1,0:T(8,128)(2,1)} %copy.79), calls=%async_computation.1 | async-start | bytes 3440640 | tf_op jit(solution)/shard_map/all_to_all | solution.py:613
  320.9 11.2 %copy-start.47 = (bf16[288,1024]{1,0:T(8,128)(2,1)S(1)}, bf16[288,1024]{1,0:T(8,128)(2,1)}, u32[]{:S(2)}) copy-start(bf16[288,1024]{1,0:T(8,128)(2,1)} %get-tuple-element.56) | copy-start | bytes 1769476
  332.1 6.9 %copy-start.31 = (bf16[1,276,1024]{2,1,0:T(8,128)(2,1)S(1)}, bf16[1,276,1024]{2,1,0:T(8,128)(2,1)}, u32[]{:S(2)}) copy-start(bf16[1,276,1024]{2,1,0:T(8,128)(2,1)} %param.17) | copy-start | bytes 1695748
  332.1 6.9 %copy-start.44 = (bf16[288,4096]{1,0:T(8,128)(2,1)S(1)}, bf16[288,4096]{1,0:T(8,128)(2,1)}, u32[]{:S(2)}) copy-start(bf16[288,4096]{1,0:T(8,128)(2,1)} %get-tuple-element.57) | copy-start | bytes 7077892
  363.6 8.6 %copy-start.21 = (f32[288,1024]{1,0:T(8,128)S(1)}, f32[288,1024]{1,0:T(8,128)}, u32[]{:S(2)}) copy-start(f32[288,1024]{1,0:T(8,128)} %get-tuple-element.52) | copy-start | bytes 3538948
  372.2 6.2 copy-start.32
  563.2 19.7 %slice-start = ((s8[8388608]{0:T(1024)(128)(4,1)}), s8[4194304]{0:T(1024)(128)(4,1)S(1)}, s32[]{:S(2)}) async-start(s8[8388608]{0:T(1024)(128)(4,1)} %bitcast.229), calls=%async_computation.2 | async-start | bytes 8388608
  571.5 7.3 %copy-start.26 = (f32[2,256,1024]{2,1,0:T(8,128)S(1)}, f32[2,256,1024]{2,1,0:T(8,128)}, u32[]{:S(2)}) copy-start(f32[2,256,1024]{2,1,0:T(8,128)} %param.26) | copy-start | bytes 6291460
  571.5 11.4 %slice-start.1 = ((s8[8388608]{0:T(1024)(128)(4,1)}), s8[4194304]{0:T(1024)(128)(4,1)S(1)}, s32[]{:S(2)}) async-start(s8[8388608]{0:T(1024)(128)(4,1)} %bitcast.229), calls=%async_computation.3 | async-start | bytes 8388608
  598.8 6.1 copy-start.25
  601.6 11.3 %copy-start.7 = (f32[4,2,2,2,2,16,1024]{6,5,4,3,2,1,0:T(8,128)}, f32[4,2,2,2,2,16,1024]{6,5,4,3,2,1,0:T(8,128)S(1)}, u32[]{:S(2)}) copy-start(f32[4,2,2,2,2,16,1024]{6,5,4,3,2,1,0:T(8,128)S(1)} %convert_element_type.221) | copy-start | bytes 12582916
  601.6 6.4 slice-start.2
  619.4 25.4 %copy-start.40 = (f32[11,256]{1,0:T(8,128)}, f32[11,256]{1,0:T(8,128)S(1)}, u32[]{:S(2)}) copy-start(f32[11,256]{1,0:T(8,128)S(1)} %get-tuple-element.160) | copy-start | bytes 33796
  635.2 9.5 %copy-start.43 = (f32[2,6]{1,0:T(2,128)}, f32[2,6]{1,0:T(2,128)S(1)}, u32[]{:S(2)}) copy-start(f32[2,6]{1,0:T(2,128)S(1)} %sqrt.47) | copy-start | bytes 148
  639.7 5.0 copy-start.15
  639.8 5.0 copy-start.16
  644.8 5.7 copy-start.14
  652.0 4.8 copy-start.10
  652.0 6.5 copy-start.11
  666.4 5.3 copy-start.12
  671.6 5.0 copy-start.8
  (26 other events, 77.4 us)

commit v4 on v1

--- a/solution.py
+++ b/solution.py
@@ -1,12 +1,62 @@
+import functools
 import math
 
 import jax
 import jax.numpy as jnp
 from jax import lax
+from jax.experimental import pallas as pl
+from jax.experimental.pallas import tpu as pltpu
 from jax.sharding import PartitionSpec as P
 
 HEADS = 16
 HEAD_DIM = 64
+MESH = pl.DeviceIdType.MESH
+LOW = jnp.bfloat16
+ANY = pl.BlockSpec(memory_space=pl.ANY)
+SHARDS, REPLICAS = 4, 8
+UNIT = 16
+BLOCK = 1024
+
+
+class Place:
+    def __init__(self):
+        self.rep = lax.axis_index("rep")
+        self.shard = lax.axis_index("shard")
+        self.core = lax.rem(self.rep, 2)
+        self.x = lax.rem(self.rep // 2, 2)
+        self.y = self.rep // 4
+
+    def across(self, axis):
+        own, step = {"core": (self.core, 1), "x": (self.x, 2), "y": (self.y, 4)}[axis]
+        return (self.rep + step - 2 * step * own, self.shard)
+
+    def along(self, offset):
+        return (self.rep, lax.rem(self.shard + offset, SHARDS))
+
+    def source(self, offset):
+        return lax.rem(self.shard + SHARDS - offset, SHARDS)
+
+    def partners(self):
+        return [self.across("core"), self.across("x"), self.across("y")] + [
+            self.along(offset) for offset in range(1, SHARDS)
+        ]
+
+
+def greet(place):
+    barrier = pltpu.get_barrier_semaphore()
+    partners = place.partners()
+    for partner in partners:
+        pl.semaphore_signal(barrier, inc=1, device_id=partner, device_id_type=MESH)
+    pl.semaphore_wait(barrier, len(partners))
+
+
+def chunk_list(shapes):
+    chunks = []
+    for index, (rows, columns) in enumerate(shapes):
+        for group in range(rows // SHARDS // 256):
+            for part in range(columns // BLOCK):
+                chunks.append((index, group, part))
+    return chunks
 
 
 step_rate = 0.3
@@ -57,7 +107,1157 @@
     return rows.reshape(sequences * portion, parts * shards * width)
 
 
-def on_device(
+def weight_tile(whole, shard, group, start, width):
+    return whole[shard, group, :, :, :, :, :, pl.ds(start, width)].reshape(256, width)
+
+
+def product(left, whole, start, width):
+    groups = whole.shape[1]
+    total = None
+    for shard in range(SHARDS):
+        for group in range(groups):
+            first = (shard * groups + group) * 256
+            term = jnp.dot(
+                left[:, first : first + 256],
+                weight_tile(whole, shard, group, start, width),
+                preferred_element_type=jnp.float32,
+            )
+            total = term if total is None else total + term
+    return total
+
+
+def contract(left, right, left_axis, right_axis):
+    return lax.dot_general(
+        left, right, (((left_axis,), (right_axis,)), ((), ())), preferred_element_type=jnp.float32
+    )
+
+
+def norm_rows(source, gain, bias, target, rows):
+    @pl.loop(0, rows // 32)
+    def _(block):
+        where = pl.ds(pl.multiple_of(block * 32, 32), 32)
+        stream = source[where, :]
+        center = stream - jnp.mean(stream, -1, keepdims=True)
+        spread = jnp.mean(center * center, -1, keepdims=True)
+        target[where, :] = (center * lax.rsqrt(spread + 1e-05) * gain + bias).astype(LOW)
+
+
+def forward_kernel(chunks, portion, *refs):
+    joined, vectors = refs[0:2]
+    masters = refs[2:7]
+    keeps = refs[7:12]
+    (
+        entering,
+        first_in,
+        heads,
+        log_total,
+        mixed,
+        middle,
+        second_in,
+        expanded,
+        activated,
+        out,
+        table,
+    ) = refs[12:23]
+    wholes = refs[23:28]
+    (
+        wide,
+        table_own,
+        table_all,
+        outgoing,
+        answer,
+        load_sems,
+        keep_sems,
+        send_sems,
+        recv_sems,
+        more_send,
+        more_recv,
+    ) = refs[28:]
+    place = Place()
+    s, k, x, y = place.shard, place.core, place.x, place.y
+    total = len(chunks)
+    rows = entering.shape[0]
+    width = entering.shape[1]
+    own = width // SHARDS
+    factor = 1.0 / math.sqrt(HEAD_DIM)
+
+    def load(at):
+        index, group, part = chunks[at]
+        return pltpu.make_async_copy(
+            masters[index].at[group, :, :, :, :, :, pl.ds(part * BLOCK, BLOCK)],
+            wide.at[at % 2],
+            load_sems.at[at % 2],
+        )
+
+    def whole(at, shard, *rest):
+        index, group, part = chunks[at]
+        rest = rest + (slice(None),) * (5 - len(rest))
+        return wholes[index].at[(shard, group) + rest + (pl.ds(part * BLOCK, BLOCK),)]
+
+    sent = []
+    arrivals = {}
+
+    def go(at, name, position, ref, device):
+        slot = at * 18 + position
+        copy = pltpu.make_async_remote_copy(
+            src_ref=ref,
+            dst_ref=ref,
+            send_sem=send_sems.at[slot],
+            recv_sem=recv_sems.at[slot],
+            device_id=device,
+            device_id_type=MESH,
+        )
+        copy.start()
+        sent.append(copy)
+        arrivals.setdefault((at, name), []).append(copy)
+
+    def arrived(at, name):
+        for copy in arrivals[(at, name)]:
+            copy.wait_recv()
+
+    def extra(slot, source, target, device):
+        copy = pltpu.make_async_remote_copy(
+            src_ref=source,
+            dst_ref=target,
+            send_sem=more_send.at[slot],
+            recv_sem=more_recv.at[slot],
+            device_id=device,
+            device_id_type=MESH,
+        )
+        copy.start()
+        sent.append(copy)
+        return copy
+
+    kept = []
+
+    def stage_cast(at):
+        index, group, part = chunks[at]
+        load(at).wait()
+
+        @pl.loop(0, 16)
+        def _(row):
+            a, b = row // 8, lax.rem(row // 4, 2)
+            c, d = lax.rem(row // 2, 2), lax.rem(row, 2)
+            wholes[index][s, group, a, b, c, d, :, part * BLOCK : (part + 1) * BLOCK] = wide[
+                at % 2, a, b, c, d
+            ].astype(LOW)
+
+        if at + 2 < total:
+            load(at + 2).start()
+
+    def stage_z(at):
+        for offset in range(1, SHARDS):
+            go(at, "z", offset - 1, whole(at, s, k, slice(None), y, x), place.along(offset))
+
+    def stage_first(at):
+        arrived(at, "z")
+        for offset in range(1, SHARDS):
+            e = place.source(offset)
+            go(at, "first", 3 + 2 * (offset - 1), whole(at, e, k, 0, y, x), place.across("x"))
+            go(at, "first", 4 + 2 * (offset - 1), whole(at, e, k, 1, y, x), place.across("y"))
+
+    def stage_second(at):
+        arrived(at, "first")
+        for offset in range(1, SHARDS):
+            e = place.source(offset)
+            go(at, "second", 9 + 2 * (offset - 1), whole(at, e, k, 0, y), place.across("y"))
+            ref = whole(at, e, k, 1, slice(None), x)
+            go(at, "second", 10 + 2 * (offset - 1), ref, place.across("x"))
+
+    def stage_core(at):
+        arrived(at, "second")
+        for offset in range(1, SHARDS):
+            e = place.source(offset)
+            go(at, "core", 15 + offset - 1, whole(at, e, k), place.across("core"))
+
+    def stage_end(at):
+        arrived(at, "core")
+        index, group, part = chunks[at]
+        copy = pltpu.make_async_copy(
+            whole(at, slice(None)),
+            keeps[index].at[:, group, :, :, :, :, :, pl.ds(part * BLOCK, BLOCK)],
+            keep_sems.at[at],
+        )
+        copy.start()
+        kept.append(copy)
+
+    stages = (stage_z, stage_first, stage_second, stage_core, stage_end)
+    lead = 4
+    step_now = [0]
+
+    def advance():
+        step = step_now[0]
+        if step >= total + 3:
+            return False
+        for position in range(1, 5):
+            at = step - (position - 1)
+            if 0 <= at < total:
+                stages[position](at)
+        if step + lead < total:
+            stage_cast(step + lead)
+            stage_z(step + lead)
+        step_now[0] = step + 1
+        return True
+
+    def until(at):
+        while step_now[0] - 4 < at:
+            advance()
+
+    load(0).start()
+    load(1).start()
+    table_own[...] = vectors[...].astype(LOW)
+    table_all[0] = vectors[...].astype(LOW)
+    greet(place)
+    table_copies = []
+    for at in range(min(lead, total)):
+        stage_cast(at)
+        stage_z(at)
+        if at == 0:
+            for offset in range(1, SHARDS):
+                table_copies.append(
+                    extra(offset - 1, table_own, table_all.at[offset], place.along(offset))
+                )
+    last = {}
+    for at, (index, group, part) in enumerate(chunks):
+        last[index] = at
+
+    until(0)
+    for copy in table_copies:
+        copy.wait_recv()
+    for offset in range(SHARDS):
+        column = pl.multiple_of(place.source(offset) * own, own)
+        table[:, pl.ds(column, own)] = table_all[offset].astype(jnp.float32)
+    until(last[0])
+
+    @pl.loop(0, width // 256)
+    def _(part):
+        start = pl.multiple_of(part * 256, 256)
+        entering[:, pl.ds(start, 256)] = (
+            product(joined, wholes[0], start, 256) + table[0:1, pl.ds(start, 256)]
+        )
+
+    norm_rows(entering, table[1:2, :], table[2:3, :], first_in, rows)
+    until(last[1])
+    live = lax.broadcasted_iota(jnp.int32, (rows, own), 0) < portion
+    for kind in range(3):
+
+        @pl.loop(0, SHARDS)
+        def _(target):
+            start = pl.multiple_of(kind * width + target * own, own)
+            outgoing[target, :, kind * own : (kind + 1) * own] = jnp.where(
+                live, product(first_in, wholes[1], start, own), 0.0
+            ).astype(LOW)
+
+    head_copies = []
+    for offset in range(1, SHARDS):
+        target = lax.rem(s + offset, SHARDS)
+        head_copies.append(
+            extra(
+                2 + offset,
+                outgoing.at[target],
+                heads.at[pl.ds(offset * rows, rows), :],
+                place.along(offset),
+            )
+        )
+
+    @pl.loop(0, rows // 32)
+    def _(block):
+        where = pl.ds(pl.multiple_of(block * 32, 32), 32)
+        heads[where, :] = outgoing[s, where, :]
+
+    advance()
+    advance()
+    for copy in head_copies:
+        copy.wait_recv()
+
+    everyone = SHARDS * rows
+    tile = 384
+    lane = lax.broadcasted_iota(jnp.int32, (tile, 128), 1)
+    key_row = lax.broadcasted_iota(jnp.int32, (everyone, tile), 0)
+    for pair in range(own // 128):
+
+        @pl.loop(0, everyone // tile)
+        def _(block):
+            start = pl.multiple_of(block * tile, 128)
+            where = pl.ds(start, tile)
+            query = heads[where, pair * 128 : (pair + 1) * 128]
+            keys = heads[:, own + pair * 128 : own + (pair + 1) * 128]
+            values = heads[:, 2 * own + pair * 128 : 2 * own + (pair + 1) * 128]
+            parts = []
+            for half in range(2):
+                inside = (lane // 64) == half
+                picked = jnp.where(inside, query.astype(jnp.float32) * factor, 0.0).astype(LOW)
+                scores = contract(keys, picked, 1, 1)
+                scores = jnp.where(lax.rem(key_row, rows) < portion, scores, -1e30)
+                top = jnp.max(scores, 0, keepdims=True)
+                weight = jnp.exp(scores - top)
+                weight_sum = jnp.sum(weight, 0, keepdims=True)
+                log_total[2 * pair + half : 2 * pair + half + 1, pl.ds(start, tile)] = (
+                    top + jnp.log(weight_sum)
+                )
+                weight = (weight * (1.0 / weight_sum)).astype(LOW)
+                summed = contract(values, weight, 0, 0)
+                parts.append(summed[half * 64 : (half + 1) * 64])
+            both = jnp.concatenate(parts, 0)
+            answer[where, pair * 128 : (pair + 1) * 128] = both.T.astype(LOW)
+
+        advance()
+
+    answer_copies = []
+    column = pl.multiple_of(s * own, own)
+    for offset in range(1, SHARDS):
+        answer_copies.append(
+            extra(
+                5 + offset,
+                answer.at[pl.ds(offset * rows, rows), :],
+                mixed.at[:, pl.ds(column, own)],
+                (place.rep, place.source(offset)),
+            )
+        )
+    mixed[:, pl.ds(column, own)] = answer[0:rows, :]
+    until(last[2])
+    for copy in answer_copies:
+        copy.wait_recv()
+
+    @pl.loop(0, width // 256)
+    def _(part):
+        start = pl.multiple_of(part * 256, 256)
+        where = pl.ds(start, 256)
+        middle[:, where] = (
+            entering[:, where] + product(mixed, wholes[2], start, 256) + table[3:4, where]
+        )
+
+    norm_rows(middle, table[4:5, :], table[5:6, :], second_in, rows)
+    per_row = width // 256
+    for part in range(expanded.shape[1] // BLOCK):
+        until(last[2] + 1 + part)
+
+        @pl.loop(0, BLOCK // 256)
+        def _(piece):
+            start = pl.multiple_of(part * BLOCK + piece * 256, 256)
+            bias_at = pl.multiple_of(piece * 256, 256)
+            value = (
+                product(second_in, wholes[3], start, 256)
+                + table[7 + part : 8 + part, pl.ds(bias_at, 256)]
+            )
+            expanded[:, pl.ds(start, 256)] = value
+            activated[:, pl.ds(start, 256)] = (
+                value * (0.5 + 0.5 * lax.erf(value * math.sqrt(0.5)))
+            ).astype(LOW)
+
+    until(last[4])
+
+    @pl.loop(0, width // 256)
+    def _(part):
+        start = pl.multiple_of(part * 256, 256)
+        where = pl.ds(start, 256)
+        out[:, where] = (
+            middle[:, where] + product(activated, wholes[4], start, 256) + table[6:7, where]
+        ).astype(LOW)
+
+    for copy in sent:
+        copy.wait_send()
+    for copy in kept:
+        copy.wait()
+
+
+def forward_pass(joined, vectors, masters, portion):
+    shapes = [(matrix.shape[0] * SHARDS, matrix.shape[1]) for matrix in masters]
+    chunks = chunk_list(shapes)
+    total = len(chunks)
+    rows = joined.shape[0]
+    width = joined.shape[1] // 2
+    own = width // SHARDS
+    hidden = shapes[3][1]
+    everyone = SHARDS * rows
+    split = [
+        matrix.reshape(matrix.shape[0] // 256, 2, 2, 2, 2, UNIT, matrix.shape[1])
+        for matrix in masters
+    ]
+    folds = [(SHARDS, r // SHARDS // 256, 2, 2, 2, 2, UNIT, c) for r, c in shapes]
+    inner = pl.BlockSpec(memory_space=pltpu.VMEM)
+    table = jnp.pad(vectors, ((0, 16 - vectors.shape[0]), (0, 0)))
+    outs = pl.pallas_call(
+        functools.partial(forward_kernel, chunks, portion),
+        out_shape=[jax.ShapeDtypeStruct(fold, LOW) for fold in folds]
+        + [
+            jax.ShapeDtypeStruct((rows, width), jnp.float32),
+            jax.ShapeDtypeStruct((rows, width), LOW),
+            jax.ShapeDtypeStruct((everyone, 3 * own), LOW),
+            jax.ShapeDtypeStruct((8, everyone), jnp.float32),
+            jax.ShapeDtypeStruct((rows, width), LOW),
+            jax.ShapeDtypeStruct((rows, width), jnp.float32),
+            jax.ShapeDtypeStruct((rows, width), LOW),
+            jax.ShapeDtypeStruct((rows, hidden), jnp.float32),
+            jax.ShapeDtypeStruct((rows, hidden), LOW),
+            jax.ShapeDtypeStruct((rows, width), LOW),
+            jax.ShapeDtypeStruct((16, width), jnp.float32),
+        ],
+        in_specs=[inner] * 2 + [ANY] * 5,
+        out_specs=[ANY] * 5 + [inner] * 11,
+        scratch_shapes=[pltpu.VMEM(fold, LOW) for fold in folds]
+        + [
+            pltpu.VMEM((2, 2, 2, 2, 2, UNIT, BLOCK), jnp.float32),
+            pltpu.VMEM((16, own), LOW),
+            pltpu.VMEM((SHARDS, 16, own), LOW),
+            pltpu.VMEM((SHARDS, rows, 3 * own), LOW),
+            pltpu.VMEM((everyone, own), LOW),
+            pltpu.SemaphoreType.DMA((2,)),
+            pltpu.SemaphoreType.DMA((total,)),
+            pltpu.SemaphoreType.DMA((total * 18,)),
+            pltpu.SemaphoreType.DMA((total * 18,)),
+            pltpu.SemaphoreType.DMA((9,)),
+            pltpu.SemaphoreType.DMA((9,)),
+        ],
+        compiler_params=pltpu.CompilerParams(
+            collective_id=1, has_side_effects=True, vmem_limit_bytes=60 * 2**20
+        ),
+        name="forward_pass",
+    )(joined, table, *split)
+    weights = [out.reshape(shape) for out, shape in zip(outs[:5], shapes)]
+    return weights, outs[5:]
+
+
+def norm_back(source, gain, incoming, residual, wide_out, low_out, rows):
+    columns = source.shape[1]
+
+    def body(block, carry):
+        where = pl.ds(pl.multiple_of(block * 32, 32), 32)
+        stream = source[where, :]
+        center = stream - jnp.mean(stream, -1, keepdims=True)
+        spread = jnp.mean(center * center, -1, keepdims=True)
+        scale = lax.rsqrt(spread + 1e-05)
+        hat = center * scale
+        grad = incoming[where, :]
+        scaled = grad * gain
+        slope = scale * (
+            scaled
+            - jnp.mean(scaled, -1, keepdims=True)
+            - hat * jnp.mean(scaled * hat, -1, keepdims=True)
+        )
+        value = residual[where, :].astype(jnp.float32) + slope
+        low = value.astype(LOW)
+        if wide_out is not None:
+            wide_out[where, :] = value
+        low_out[where, :] = low
+        terms = (grad * hat, grad, low.astype(jnp.float32))
+        return tuple(kept + jnp.sum(term, 0, keepdims=True) for kept, term in zip(carry, terms))
+
+    zero = jnp.zeros((1, columns), jnp.float32)
+    return lax.fori_loop(0, rows // 32, body, (zero, zero, zero))
+
+
+def backward_kernel(chunks, portion, *refs):
+    (
+        cotangent,
+        joined,
+        vectors,
+        entering,
+        first_in,
+        heads,
+        log_total,
+        mixed,
+        middle,
+        second_in,
+        expanded,
+        activated,
+    ) = refs[:12]
+    weights = refs[12:17]
+    masters = refs[17:22]
+    states = refs[22:27]
+    own_vectors, own_states = refs[27:29]
+    sums = refs[29:34]
+    table_sum, norms, grad_joined = refs[34:37]
+    (
+        ring,
+        theirs,
+        mine,
+        from_core,
+        from_first,
+        from_second,
+        final,
+        from_z,
+        ready,
+        state_in,
+        master_in,
+        squares,
+        square_in,
+        square_z,
+        table_own,
+        table_in,
+        table_z,
+        grad_inner,
+        grad_second,
+        grad_middle,
+        grad_middle_low,
+        outgoing,
+        grad_mixed,
+        grad_key,
+        grad_value,
+        grad_heads,
+        grad_triple,
+        grad_entering,
+        ring_sems,
+        state_sems,
+        ready_sems,
+        send_sems,
+        recv_sems,
+        more_send,
+        more_recv,
+    ) = refs[37:]
+    place = Place()
+    s, k, x, y = place.shard, place.core, place.x, place.y
+    rows, width = entering.shape
+    own = width // SHARDS
+    factor = 1.0 / math.sqrt(HEAD_DIM)
+    depth = ring.shape[0]
+
+    def tiles(index):
+        parts = weights[index].shape[7] // BLOCK
+        return weights[index].shape[1], parts, SHARDS * weights[index].shape[1] * parts
+
+    def fetch(index, at):
+        groups, parts, _ = tiles(index)
+        shard, rest = at // (groups * parts), lax.rem(at, groups * parts)
+        group, part = rest // parts, lax.rem(rest, parts)
+        start = pl.multiple_of(part * BLOCK, BLOCK)
+        return pltpu.make_async_copy(
+            weights[index].at[shard, group, :, :, :, :, :, pl.ds(start, BLOCK)],
+            ring.at[lax.rem(at, depth)],
+            ring_sems.at[lax.rem(at, depth)],
+        )
+
+    def prime(index):
+        @pl.loop(0, min(depth, tiles(index)[2]))
+        def _(at):
+            fetch(index, at).start()
+
+    def take(index, at):
+        fetch(index, at).wait()
+        return ring[lax.rem(at, depth)].reshape(256, BLOCK)
+
+    def give(index, at):
+        @pl.when(at + depth < tiles(index)[2])
+        def _():
+            fetch(index, at + depth).start()
+
+    copies = {}
+
+    def go(at, name, position, source, target, device):
+        slot = at * 14 + position
+        copy = pltpu.make_async_remote_copy(
+            src_ref=source,
+            dst_ref=target,
+            send_sem=send_sems.at[slot],
+            recv_sem=recv_sems.at[slot],
+            device_id=device,
+            device_id_type=MESH,
+        )
+        copy.start()
+        copies.setdefault((at, name), []).append(copy)
+
+    sent = []
+
+    def extra(slot, source, target, device):
+        copy = pltpu.make_async_remote_copy(
+            src_ref=source,
+            dst_ref=target,
+            send_sem=more_send.at[slot],
+            recv_sem=more_recv.at[slot],
+            device_id=device,
+            device_id_type=MESH,
+        )
+        copy.start()
+        sent.append(copy)
+        return copy
+
+    def arrived(at, name):
+        for copy in copies[(at, name)]:
+            copy.wait_recv()
+
+    def left(at, name):
+        for copy in copies.pop((at, name), []):
+            copy.wait_send()
+
+    def gradient_half(at, core):
+        index, group, part = chunks[at]
+        lefts = (joined, first_in, mixed, second_in, activated)[index]
+        pitch = lefts.shape[1] // SHARDS
+        columns = [
+            lefts[:, pl.ds(pl.multiple_of(shard * pitch + group * 256 + core * 128, 128), 128)]
+            for shard in range(SHARDS)
+        ]
+        if index == 0:
+            right = grad_entering[...]
+        elif index == 1:
+            right = jnp.concatenate(
+                [grad_triple[shard, :, part * own : (part + 1) * own] for shard in range(SHARDS)],
+                1,
+            )
+        elif index == 2:
+            right = grad_middle_low[...]
+        elif index == 3:
+            right = grad_inner[:, part * BLOCK : (part + 1) * BLOCK]
+        else:
+            right = cotangent[...]
+        return contract(jnp.concatenate(columns, 1), right, 0, 0)
+
+    def stage_core(at):
+        slot = at % 2
+        value = gradient_half(at, 1 - k).astype(LOW)
+        theirs[slot] = value.reshape(SHARDS, 2, 2, 2, UNIT, BLOCK)
+        go(at, "core", 0, theirs.at[slot], from_core.at[slot], place.across("core"))
+
+    def stage_first(at):
+        slot = at % 3
+        value = gradient_half(at, k).reshape(SHARDS, 2, 2, 2, UNIT, BLOCK)
+        arrived(at, "core")
+        left(at, "core")
+        mine[slot] = (value + from_core[at % 2].astype(jnp.float32)).astype(LOW)
+        target = from_first.at[at % 2]
+        go(at, "first", 1, mine.at[slot, :, 0, :, 1 - x], target.at[0], place.across("x"))
+        go(at, "first", 2, mine.at[slot, :, 1, 1 - y], target.at[1], place.across("y"))
+
+    def stage_second(at):
+        slot = at % 3
+        arrived(at, "first")
+        left(at, "first")
+
+        @pl.loop(0, SHARDS)
+        def _(shard):
+            for i in range(2):
+                mine[slot, shard, 0, i, x] = (
+                    mine[slot, shard, 0, i, x].astype(jnp.float32)
+                    + from_first[at % 2, 0, shard, i].astype(jnp.float32)
+                ).astype(LOW)
+                mine[slot, shard, 1, y, i] = (
+                    mine[slot, shard, 1, y, i].astype(jnp.float32)
+                    + from_first[at % 2, 1, shard, i].astype(jnp.float32)
+                ).astype(LOW)
+
+        target = from_second.at[at % 2]
+        go(at, "second", 3, mine.at[slot, :, 0, 1 - y, x], target.at[0], place.across("y"))
+        go(at, "second", 4, mine.at[slot, :, 1, y, 1 - x], target.at[1], place.across("x"))
+
+    def piece_loads(at):
+        index, group, part = chunks[at]
+        slot = at % 2
+        where = pl.ds(part * BLOCK, BLOCK)
+        return (
+            pltpu.make_async_copy(
+                states[index].at[:, group, k, :, y, x, :, where],
+                state_in.at[slot],
+                state_sems.at[slot, 0],
+            ),
+            pltpu.make_async_copy(
+                masters[index].at[group, k, :, y, x, :, where],
+                master_in.at[slot],
+                state_sems.at[slot, 1],
+            ),
+        )
+
+    def stage_z(at):
+        slot = at % 3
+        arrived(at, "second")
+        left(at, "second")
+
+        @pl.loop(0, SHARDS)
+        def _(shard):
+            for h in range(2):
+                final[at % 2, shard, h] = (
+                    mine[slot, shard, h, y, x].astype(jnp.float32)
+                    + from_second[at % 2, h, shard].astype(jnp.float32)
+                ).astype(LOW)
+
+        for copy in piece_loads(at):
+            copy.start()
+        for offset in range(1, SHARDS):
+            target = lax.rem(s + offset, SHARDS)
+            go(
+                at,
+                "z",
+                5 + offset - 1,
+                final.at[at % 2, target],
+                from_z.at[at % 2, offset - 1],
+                place.along(offset),
+            )
+
+    def summed(at, *where):
+        index, group, part = chunks[at]
+        rest = where + (slice(None),) * (5 - len(where))
+        return sums[index].at[(group,) + rest + (pl.ds(part * BLOCK, BLOCK),)]
+
+    def own_piece(at):
+        return pltpu.make_async_copy(
+            ready.at[at % 2], summed(at, k, slice(None), y, x), ready_sems.at[at % 2]
+        )
+
+    def direction_of(gradient, first, second):
+        moment = 0.5 * first + 0.5 * gradient
+        root = jnp.sqrt(0.5 * second * second + 0.5 * gradient * gradient)
+        return moment / (root + 1e-06)
+
+    def lanes(square):
+        total = jnp.sum(square, 0, keepdims=True)
+        parts = [total[:, i * 128 : (i + 1) * 128] for i in range(total.shape[1] // 128)]
+        return sum(parts[1:], parts[0])
+
+    def stage_back(at):
+        index = chunks[at][0]
+        slot = at % 2
+        for copy in piece_loads(at):
+            copy.wait()
+        arrived(at, "z")
+        left(at, "z")
+        for h in range(2):
+            value = final[slot, s, h].astype(jnp.float32)
+            for offset in range(1, SHARDS):
+                value = value + from_z[slot, offset - 1, h].astype(jnp.float32)
+            low = value.astype(LOW)
+            ready[slot, h] = low
+            direction = direction_of(
+                low.astype(jnp.float32), state_in[slot, 0, h], state_in[slot, 1, h]
+            )
+            master = master_in[slot, h]
+            squares[0, index : index + 1, :] += lanes(master * master)
+            squares[0, 8 + index : 9 + index, :] += lanes(direction * direction)
+        own_piece(at).start()
+        target = summed(at, k, 0, y, x)
+        go(at, "back", 8, ready.at[slot, 0], target, place.across("y"))
+        target = summed(at, k, 1, y, x)
+        go(at, "back", 9, ready.at[slot, 1], target, place.across("x"))
+
+    def stage_wide(at):
+        own_piece(at).wait()
+        arrived(at, "back")
+        left(at, "back")
+        ref = summed(at, k, 0, slice(None), x)
+        go(at, "wide", 10, ref, ref, place.across("x"))
+        ref = summed(at, k, 1, y)
+        go(at, "wide", 11, ref, ref, place.across("y"))
+
+    def stage_twin(at):
+        arrived(at, "wide")
+        ref = summed(at, k)
+        go(at, "twin", 12, ref, ref, place.across("core"))
+
+    def stage_end(at):
+        arrived(at, "twin")
+
+    stages = (
+        stage_core,
+        stage_first,
+        stage_second,
+        stage_z,
+        stage_back,
+        stage_wide,
+        stage_twin,
+        stage_end,
+    )
+    ages = {}
+    upcoming = [0]
+
+    def tick(start=False):
+        for at in sorted(ages):
+            stages[ages[at]](at)
+            ages[at] += 1
+            if ages[at] == len(stages):
+                del ages[at]
+        if start:
+            at = upcoming[0]
+            stages[0](at)
+            ages[at] = 1
+            upcoming[0] = at + 1
+
+    prime(4)
+    squares[...] = jnp.zeros_like(squares)
+    table_own[...] = jnp.zeros_like(table_own)
+    greet(place)
+    tick(True)
+
+    def put_row(row, value):
+        for shard in range(SHARDS):
+            table_own[0, shard, row : row + 1, :] = value[:, shard * own : (shard + 1) * own]
+
+    put_row(6, jnp.sum(cotangent[...].astype(jnp.float32), 0, keepdims=True))
+
+    groups = tiles(4)[0]
+    for quarter in range(SHARDS):
+
+        @pl.loop(0, groups)
+        def _(group):
+            at = quarter * groups + group
+            act = contract(cotangent[...], take(4, at), 1, 1)
+            give(4, at)
+            where = pl.ds(pl.multiple_of(at * 256, 256), 256)
+            value = expanded[:, where]
+            slope = 0.5 + 0.5 * lax.erf(value * math.sqrt(0.5))
+            slope = slope + value * jnp.exp(-0.5 * value * value) * (1.0 / math.sqrt(2.0 * math.pi))
+            low = (act * slope).astype(LOW)
+            grad_inner[:, where] = low
+            table_own[0, group, 7 + quarter : 8 + quarter, :] = jnp.sum(
+                low.astype(jnp.float32), 0, keepdims=True
+            )
+
+        if quarter % 2:
+            tick(True)
+    prime(3)
+    parts = tiles(3)[1]
+
+    @pl.loop(0, SHARDS)
+    def _(shard):
+        where = pl.ds(pl.multiple_of(shard * 256, 256), 256)
+        total = None
+        for part in range(parts):
+            at = shard * parts + part
+            term = contract(grad_inner[:, part * BLOCK : (part + 1) * BLOCK], take(3, at), 1, 1)
+            give(3, at)
+            total = term if total is None else total + term
+        grad_second[:, where] = total
+
+    prime(2)
+    tick(True)
+    gain_sum, bias_sum, low_sum = norm_back(
+        middle, vectors[4:5, :], grad_second, cotangent, grad_middle, grad_middle_low, rows
+    )
+    put_row(4, gain_sum)
+    put_row(5, bias_sum)
+    put_row(3, low_sum)
+
+    @pl.loop(0, SHARDS)
+    def _(shard):
+        outgoing[shard, :, 0:own] = contract(grad_middle_low[...], take(2, shard), 1, 1).astype(LOW)
+
+    prime(1)
+    mixed_copies = []
+    for offset in range(1, SHARDS):
+        mixed_copies.append(
+            extra(
+                offset - 1,
+                outgoing.at[lax.rem(s + offset, SHARDS), :, pl.ds(0, own)],
+                grad_mixed.at[pl.ds(offset * rows, rows), :],
+                place.along(offset),
+            )
+        )
+
+    @pl.loop(0, rows // 32)
+    def _(block):
+        where = pl.ds(pl.multiple_of(block * 32, 32), 32)
+        grad_mixed[where, :] = outgoing[s, where, 0:own]
+
+    tick(True)
+    for copy in mixed_copies:
+        copy.wait_recv()
+
+    everyone = SHARDS * rows
+    tile = 384
+    lane = lax.broadcasted_iota(jnp.int32, (tile, 128), 1)
+    key_row = lax.broadcasted_iota(jnp.int32, (everyone, tile), 0)
+    for pair in range(own // 128):
+        grad_key[...] = jnp.zeros_like(grad_key)
+        grad_value[...] = jnp.zeros_like(grad_value)
+        low, high = pair * 128, (pair + 1) * 128
+
+        @pl.loop(0, everyone // tile)
+        def _(block):
+            start = pl.multiple_of(block * tile, 128)
+            where = pl.ds(start, tile)
+            query = heads[where, low:high]
+            keys = heads[:, own + low : own + high]
+            values = heads[:, 2 * own + low : 2 * own + high]
+            incoming = grad_mixed[where, low:high]
+            parts = []
+            for half in range(2):
+                inside = (lane // 64) == half
+                picked = jnp.where(inside, query.astype(jnp.float32) * factor, 0.0).astype(LOW)
+                grads = jnp.where(inside, incoming.astype(jnp.float32), 0.0).astype(LOW)
+                scores = contract(keys, picked, 1, 1)
+                scores = jnp.where(lax.rem(key_row, rows) < portion, scores, -1e30)
+                at = 2 * pair + half
+                weight = jnp.exp(scores - log_total[at : at + 1, pl.ds(start, tile)])
+                slope = contract(values, grads, 1, 1)
+                delta = jnp.sum(weight * slope, 0, keepdims=True)
+                grad_scores = (weight * (slope - delta)).astype(LOW)
+                grad_key[...] += jnp.dot(
+                    grad_scores, picked, preferred_element_type=jnp.float32
+                )
+                grad_value[...] += jnp.dot(
+                    weight.astype(LOW), grads, preferred_element_type=jnp.float32
+                )
+                turned = contract(keys, grad_scores, 0, 0)
+                parts.append(turned[half * 64 : (half + 1) * 64])
+            both = jnp.concatenate(parts, 0) * factor
+            grad_heads[where, low:high] = both.T.astype(LOW)
+
+        grad_heads[:, own + low : own + high] = grad_key[...].astype(LOW)
+        grad_heads[:, 2 * own + low : 2 * own + high] = grad_value[...].astype(LOW)
+        tick(True)
+
+    triple_copies = []
+    for offset in range(1, SHARDS):
+        triple_copies.append(
+            extra(
+                2 + offset,
+                grad_heads.at[pl.ds(offset * rows, rows), :],
+                grad_triple.at[s],
+                (place.rep, place.source(offset)),
+            )
+        )
+
+    @pl.loop(0, rows // 32)
+    def _(block):
+        where = pl.ds(pl.multiple_of(block * 32, 32), 32)
+        grad_triple[s, where, :] = grad_heads[where, :]
+
+    tick(True)
+    tick(True)
+    for copy in triple_copies:
+        copy.wait_recv()
+    parts_in = tiles(1)[1]
+
+    @pl.loop(0, SHARDS)
+    def _(shard):
+        where = pl.ds(pl.multiple_of(shard * 256, 256), 256)
+        total = None
+        for part in range(parts_in):
+            at = shard * parts_in + part
+            left_side = jnp.concatenate(
+                [grad_triple[g, :, part * own : (part + 1) * own] for g in range(SHARDS)], 1
+            )
+            term = contract(left_side, take(1, at), 1, 1)
+            give(1, at)
+            total = term if total is None else total + term
+        grad_second[:, where] = total
+
+    prime(0)
+    gain_sum, bias_sum, low_sum = norm_back(
+        entering, vectors[1:2, :], grad_second, grad_middle, None, grad_entering, rows
+    )
+    put_row(1, gain_sum)
+    put_row(2, bias_sum)
+    put_row(0, low_sum)
+    table_copies = []
+
+    def table_step(position, axis):
+        if position:
+            table_copies[-1].wait_recv()
+            table_own[position] = table_own[position - 1] + table_in[position - 1]
+        if axis:
+            table_copies.append(
+                extra(
+                    6 + position,
+                    table_own.at[position],
+                    table_in.at[position],
+                    place.across(axis),
+                )
+            )
+
+    table_step(0, "core")
+    tick(True)
+    table_step(1, "x")
+
+    @pl.loop(0, tiles(0)[2])
+    def _(at):
+        where = pl.ds(pl.multiple_of(at * 256, 256), 256)
+        grad_joined[:, where] = contract(grad_entering[...], take(0, at), 1, 1).astype(LOW)
+        give(0, at)
+
+    table_step(2, "y")
+    tick(True)
+    table_step(3, None)
+    for offset in range(1, SHARDS):
+        table_copies.append(
+            extra(
+                8 + offset,
+                table_own.at[3, lax.rem(s + offset, SHARDS)],
+                table_z.at[offset - 1],
+                place.along(offset),
+            )
+        )
+    tick(True)
+    for copy in table_copies[3:]:
+        copy.wait_recv()
+    value = table_own[3, s]
+    for offset in range(1, SHARDS):
+        value = value + table_z[offset - 1]
+    table_sum[...] = value
+    direction = direction_of(value, own_states[0], own_states[1])
+    share = 1.0 / REPLICAS
+    squares[0, 5:6, :] = share * lanes(own_vectors[...] * own_vectors[...])
+    squares[0, 13:14, :] = share * lanes(direction * direction)
+    while upcoming[0] < len(chunks):
+        tick(True)
+    square_copies = []
+    square_axes = ("core", "x", "y")
+    position = 0
+    while ages or position < 4:
+        if ages:
+            tick()
+        waiting = [at for at in ages if ages[at] <= 4]
+        if not waiting and position < 4:
+            if position:
+                square_copies[-1].wait_recv()
+                squares[position] = squares[position - 1] + square_in[position - 1]
+            if position < 3:
+                square_copies.append(
+                    extra(
+                        12 + position,
+                        squares.at[position],
+                        square_in.at[position],
+                        place.across(square_axes[position]),
+                    )
+                )
+            position += 1
+    for offset in range(1, SHARDS):
+        square_copies.append(
+            extra(14 + offset, squares.at[3], square_z.at[offset], place.along(offset))
+        )
+    square_z[0] = squares[3]
+    for copy in square_copies[3:]:
+        copy.wait_recv()
+    value = square_z[s]
+    for shard in range(1, SHARDS):
+        value = value + square_z[lax.rem(s + SHARDS - shard, SHARDS)]
+    norms[...] = jnp.sqrt(jnp.sum(value, 1, keepdims=True)) + jnp.zeros_like(value)
+    for key in sorted(copies):
+        for copy in copies[key]:
+            copy.wait_send()
+    for copy in sent:
+        copy.wait_send()
+
+
+def backward_pass(cotangent, joined, table, kept, weights, masters, states, vectors, vector_states, portion):
+    entering, first_in, heads, log_total, mixed, middle, second_in, expanded, activated = kept[:9]
+    shapes = [(matrix.shape[0] * SHARDS, matrix.shape[1]) for matrix in masters]
+    order = chunk_list(shapes)
+    chunks = [chunk for index in (4, 3, 2, 1, 0) for chunk in order if chunk[0] == index]
+    total = len(chunks)
+    rows, width = entering.shape
+    own = width // SHARDS
+    hidden = expanded.shape[1]
+    everyone = SHARDS * rows
+    piece = (UNIT, BLOCK)
+    inner = pl.BlockSpec(memory_space=pltpu.VMEM)
+    folds = [(SHARDS, r // SHARDS // 256, 2, 2, 2, 2, UNIT, c) for r, c in shapes]
+    extra_rows = 16 - vectors.shape[0]
+    own_vectors = jnp.pad(vectors, ((0, extra_rows), (0, 0)))
+    own_states = jnp.pad(vector_states, ((0, 0), (0, extra_rows), (0, 0)))
+    outs = pl.pallas_call(
+        functools.partial(backward_kernel, chunks, portion),
+        out_shape=[jax.ShapeDtypeStruct(fold[1:], LOW) for fold in folds]
+        + [
+            jax.ShapeDtypeStruct((16, own), jnp.float32),
+            jax.ShapeDtypeStruct((16, 128), jnp.float32),
+            jax.ShapeDtypeStruct((rows, 2 * width), LOW),
+        ],
+        in_specs=[inner] * 12 + [ANY] * 15 + [inner] * 2,
+        out_specs=[ANY] * 5 + [inner] * 3,
+        scratch_shapes=[
+            pltpu.VMEM((8, 2, 2, 2, 2) + piece, LOW),
+            pltpu.VMEM((2, SHARDS, 2, 2, 2) + piece, LOW),
+            pltpu.VMEM((3, SHARDS, 2, 2, 2) + piece, LOW),
+            pltpu.VMEM((2, SHARDS, 2, 2, 2) + piece, LOW),
+            pltpu.VMEM((2, 2, SHARDS, 2) + piece, LOW),
+            pltpu.VMEM((2, 2, SHARDS) + piece, LOW),
+            pltpu.VMEM((2, SHARDS, 2) + piece, LOW),
+            pltpu.VMEM((2, SHARDS - 1, 2) + piece, LOW),
+            pltpu.VMEM((2, 2) + piece, LOW),
+            pltpu.VMEM((2, 2, 2) + piece, jnp.float32),
+            pltpu.VMEM((2, 2) + piece, jnp.float32),
+            pltpu.VMEM((4, 16, 128), jnp.float32),
+            pltpu.VMEM((3, 16, 128), jnp.float32),
+            pltpu.VMEM((SHARDS, 16, 128), jnp.float32),
+            pltpu.VMEM((4, SHARDS, 16, own), jnp.float32),
+            pltpu.VMEM((3, SHARDS, 16, own), jnp.float32),
+            pltpu.VMEM((SHARDS - 1, 16, own), jnp.float32),
+            pltpu.VMEM((rows, hidden), LOW),
+            pltpu.VMEM((rows, width), jnp.float32),
+            pltpu.VMEM((rows, width), jnp.float32),
+            pltpu.VMEM((rows, width), LOW),
+            pltpu.VMEM((SHARDS, rows, own), LOW),
+            pltpu.VMEM((everyone, own), LOW),
+            pltpu.VMEM((everyone, 128), jnp.float32),
+            pltpu.VMEM((everyone, 128), jnp.float32),
+            pltpu.VMEM((everyone, 3 * own), LOW),
+            pltpu.VMEM((SHARDS, rows, 3 * own), LOW),
+            pltpu.VMEM((rows, width), LOW),
+            pltpu.SemaphoreType.DMA((8,)),
+            pltpu.SemaphoreType.DMA((2, 2)),
+            pltpu.SemaphoreType.DMA((2,)),
+            pltpu.SemaphoreType.DMA((total * 14,)),
+            pltpu.SemaphoreType.DMA((total * 14,)),
+            pltpu.SemaphoreType.DMA((18,)),
+            pltpu.SemaphoreType.DMA((18,)),
+        ],
+        compiler_params=pltpu.CompilerParams(
+            collective_id=2, has_side_effects=True, vmem_limit_bytes=60 * 2**20
+        ),
+        name="backward_pass",
+    )(
+        cotangent,
+        joined,
+        table,
+        entering,
+        first_in,
+        heads,
+        log_total,
+        mixed,
+        middle,
+        second_in,
+        expanded,
+        activated,
+        *[matrix.reshape(fold) for matrix, fold in zip(weights, folds)],
+        *[matrix.reshape(fold[1:]) for matrix, fold in zip(masters, folds)],
+        *[state.reshape((2,) + fold[1:]) for state, fold in zip(states, folds)],
+        own_vectors,
+        own_states,
+    )
+    lows = [low.reshape(r // SHARDS, c) for low, (r, c) in zip(outs[:5], shapes)]
+    return lows, outs[5][: vectors.shape[0]], outs[6], outs[7]
+
+
+def update_kernel(position, norms, gradient, state, master, wide, new_state, new_master):
+    grad = gradient[...].astype(jnp.float32)
+    moment = 0.5 * state[0] + 0.5 * grad
+    root = jnp.sqrt(0.5 * state[1] * state[1] + 0.5 * grad * grad)
+    wide[...] = grad
+    new_state[0] = moment
+    new_state[1] = root
+    ratio = norms[position : position + 1, 0:1] / (
+        norms[8 + position : 9 + position, 0:1] + 1e-06
+    )
+    new_master[...] = master[...] - (step_rate * ratio) * (moment / (root + 1e-06))
+
+
+def update_weight(position, norms, gradient, state, master):
+    rows, columns = master.shape
+    block = 256 if columns <= BLOCK else 64
+    plain = pl.BlockSpec((block, columns), lambda i: (i, 0))
+    paired = pl.BlockSpec((2, block, columns), lambda i: (0, i, 0))
+    return pl.pallas_call(
+        functools.partial(update_kernel, position),
+        grid=(rows // block,),
+        out_shape=[
+            jax.ShapeDtypeStruct(master.shape, jnp.float32),
+            jax.ShapeDtypeStruct(state.shape, jnp.float32),
+            jax.ShapeDtypeStruct(master.shape, jnp.float32),
+        ],
+        in_specs=[pl.BlockSpec((16, 128), lambda i: (0, 0)), plain, paired, plain],
+        out_specs=[plain, paired, plain],
+        name="update_weight",
+    )(norms, gradient, state, master)
+
+
+def fits(masters):
+    return (
+        lax.axis_size("shard") == SHARDS
+        and lax.axis_size("rep") == REPLICAS
+        and all(m.shape[0] % 256 == 0 and m.shape[1] % BLOCK == 0 for m in masters)
+        and masters[0].shape[1] == HEADS * HEAD_DIM == BLOCK
+    )
+
+
+def plain_device(
     hidden_in,
     skip_path,
     cotangent,
@@ -227,6 +1427,59 @@
     )
 
 
+def on_device(
+    hidden_in,
+    skip_path,
+    cotangent,
+    skip_weight,
+    heads_in,
+    heads_out,
+    expand_weight,
+    reduce_weight,
+    vectors,
+    moments_skip,
+    moments_in,
+    moments_out,
+    moments_expand,
+    moments_reduce,
+    moments_vectors,
+):
+    sequences, portion, model_width = hidden_in.shape
+    masters = (skip_weight, heads_in, heads_out, expand_weight, reduce_weight)
+    states = (moments_skip, moments_in, moments_out, moments_expand, moments_reduce)
+    if not (sequences == 1 and fits(masters)):
+        return plain_device(
+            hidden_in, skip_path, cotangent, *masters, vectors, *states, moments_vectors
+        )
+    more = -portion % 32
+    joined = jnp.concatenate([hidden_in[0], skip_path[0]], 1)
+    joined = jnp.pad(joined, ((0, more), (0, 0)))
+    incoming = jnp.pad(cotangent[0], ((0, more), (0, 0)))
+    weights, kept = forward_pass(joined, vectors, masters, portion)
+    block_out, table = kept[9], kept[10]
+    lows, vector_total, norms, grad_joined = backward_pass(
+        incoming, joined, table, kept, weights, masters, states, vectors, moments_vectors, portion
+    )
+    steps = [
+        update_weight(position, norms, lows[position], states[position], masters[position])
+        for position in range(5)
+    ]
+    vector_state, direction = moment_step(vector_total, moments_vectors)
+    ratio = norms[5, 0] / (norms[13, 0] + 1e-06)
+    return (
+        block_out[None, :portion],
+        grad_joined[None, :portion, :model_width],
+        grad_joined[None, :portion, model_width:],
+        *(step[0] for step in steps),
+        vector_total,
+        *(step[1] for step in steps),
+        vector_state,
+        *(step[2] for step in steps),
+        vectors - step_rate * ratio * direction,
+        jnp.stack([norms[:6, 0], norms[8:14, 0]]),
+    )
+
+
 def solution(mesh):
     placed = (
         P("rep", "shard", None),

time: 1410 us -> 484 us (0.34)
  waiting for transfers between devices: 844 us -> 0 us
  Pallas kernels: 0 us -> 462 us
  blocking collectives: 195 us -> 0 us
  matrix products: 140 us -> 0 us
  other arithmetic: 130 us -> 4.3 us
  local copies, waits for them, and re-layouts: 72.8 us -> 6.05 us
  between operations: 18.8 us -> 2.47 us
    reduce_scatter x5 -> x0, waiting for transfers between devices: 585 us -> none  [on_device(): lax.psum_scatter(partial.astype(jnp.bfloat16), ('shard', 'rep'), scatter_...]
    pallas_call x0 -> x7, Pallas kernels: none -> 462 us  [the longest x1 234 us: backward_pass(): pl.pallas_call(functools.partial(backward_kernel, chunks, portion), out_s...]
    all_gather x9 -> x0, waiting for transfers between devices: 232 us -> none  [the longest x5 182 us: on_device(): gathered.append(lax.all_gather(piece, ('shard', 'rep'), axis=0, tiled=True))]
    dot_general x21 -> x0, matrix products: 140 us -> none  [the longest x15 94 us: matmul(): return jnp.dot(left, right, preferred_element_type=jnp.float32)]
    all_to_all x3 -> x0, blocking collectives: 116 us -> none  [the longest x2 72.9 us: to_heads(): blocks = lax.all_to_all(blocks, 'shard', 0, 0, tiled=True)]
    reduce_sum x19 -> x0, other arithmetic: 58.8 us -> none  [the longest x6 34.5 us: on_device(): jnp.sum(direction * direction)]
    psum x2 -> x0, blocking collectives: 53.6 us -> none  [the longest x1 42 us: on_device(): grad_table = lax.psum(grad_table, ('rep', 'shard'))]
    another operation x12 -> x2, other arithmetic: 45.8 us -> 0.02 us  [moment_step(): return (jnp.stack([first_moment, root_square]), direction)]
  transfers between devices with their start and end apart: 15 -> 0, of which waited for: 14 -> 0; matrix products, arithmetic and copies ran while one was open for 13% -> 0% of each run, Pallas kernels for 0% -> 0%
where the time goes in v4:
time: 484 us; the launch traced here: 475 us
  Pallas kernels  462 us (95%)
  local copies, waits for them, and re-layouts  6.05 us (1%)
    pallas_call x1, Pallas kernels, backward_pass(): pl.pallas_call(functools.partial(backward_kernel, chunks, portion), out_s...  234 us
    pallas_call x1, Pallas kernels, forward_pass(): pl.pallas_call(functools.partial(forward_kernel, chunks, portion), out_sh...  182 us
    pallas_call x5, Pallas kernels, update_weight(): pl.pallas_call(functools.partial(update_kernel, position), grid=(rows //...  46 us

profile of v4, /device:TPU:0, one launch (start us, length us, event | category | flops | bytes accessed | tf_op | source)
XLA Modules:
  0.0 475.3 jit_solution(5106554407135581537)
XLA Ops:
  0.7 2.3 fusion.2.refs_0_.refs_1_
  3.0 1.3 pad.18.refs_1_.refs_27_
  4.3 0.0 copy-start.6
  4.3 0.0 copy-start.1
  4.3 182.2 %forward_pass.1 = (bf16[4,2,2,2,2,2,16,1024]{7,6,5,4,3,2,1,0:T(8,128)(2,1)}, bf16[4,1,2,2,2,2,16,3072]{7,6,5,4,3,2,1,0:T(8,128)(2,1)}, bf16[4,1,2,2,2,2,16,1024]...) custom-call(bf16[288,2048]{1,0:T(8,128)(2,1)} %fusion.2.refs_0_.refs, ...), custom_call_target="tpu_custom_call" | custom-call | tf_op jit(solution)/shard_map/forward_pass/pallas_call | solution.py:480
  186.5 0.0 copy-done.6
  186.6 0.6 pad.20.refs_28_
  187.2 0.0 copy-done.1
  187.2 0.9 pad.19.refs_0_
  188.1 0.0 copy-start.5
  188.1 234.2 %backward_pass.1 = (bf16[2,2,2,2,2,16,1024]{6,5,4,3,2,1,0:T(8,128)(2,1)}, bf16[1,2,2,2,2,16,3072]{6,5,4,3,2,1,0:T(8,128)(2,1)}, bf16[1,2,2,2,2,16,1024]{6,5,4,3,...) custom-call(bf16[288,1024]{1,0:T(8,128)(2,1)} %pad.19.refs_0_, ...), custom_call_target="tpu_custom_call" | custom-call | tf_op jit(solution)/shard_map/backward_pass/pallas_call | solution.py:1145
  422.3 1.2 fusion.8
  424.8 0.0 copy-done.5
  424.8 1.3 multiply_subtract_fusion
  426.2 0.0 copy-start.4
  426.2 0.6 copy.44
  426.8 0.0 copy-start.3
  426.8 13.0 %update_weight.9 = (f32[1024,1024]{1,0:T(8,128)}, f32[2,1024,1024]{2,1,0:T(8,128)}, f32[1024,1024]{1,0:T(8,128)}) custom-call(f32[16,128]{1,0:T(8,128)} %get-tuple-element.78.norms, bf16[1024,1024]{1,0:T(8,128)(2,1)} %bitcast.63, f32[2,1024,1024]{2,1,0:T(8,128)} %state.9, f32[1024,1024]{1,0:T(8,128)} %master.9), custom_call_target="tpu_custom_call" | custom-call | tf_op jit(solution)/shard_map/update_weight/pallas_call | solution.py:1237
  439.8 0.0 copy-done.4
  439.8 0.0 copy-done.3
  439.9 0.1 slice_reduce_fusion.1
  440.0 0.6 pad_maximum_fusion.1
  440.6 12.1 %update_weight.8 = (f32[256,4096]{1,0:T(8,128)}, f32[2,256,4096]{2,1,0:T(8,128)}, f32[256,4096]{1,0:T(8,128)}) custom-call(f32[16,128]{1,0:T(8,128)} %get-tuple-element.78.norms, bf16[256,4096]{1,0:T(8,128)(2,1)} %bitcast.62, f32[2,256,4096]{2,1,0:T(8,128)} %state.8, f32[256,4096]{1,0:T(8,128)} %master.8), custom_call_target="tpu_custom_call" | custom-call | tf_op jit(solution)/shard_map/update_weight/pallas_call | solution.py:1237
  452.6 5.0 %update_weight.7 = (f32[256,1024]{1,0:T(8,128)}, f32[2,256,1024]{2,1,0:T(8,128)}, f32[256,1024]{1,0:T(8,128)}) custom-call(f32[16,128]{1,0:T(8,128)} %get-tuple-element.78.norms, bf16[256,1024]{1,0:T(8,128)(2,1)} %bitcast.69, f32[2,256,1024]{2,1,0:T(8,128)} %state.7, f32[256,1024]{1,0:T(8,128)} %master.7), custom_call_target="tpu_custom_call" | custom-call | tf_op jit(solution)/shard_map/update_weight/pallas_call | solution.py:1237
  457.6 9.6 %update_weight.6 = (f32[256,3072]{1,0:T(8,128)}, f32[2,256,3072]{2,1,0:T(8,128)}, f32[256,3072]{1,0:T(8,128)}) custom-call(f32[16,128]{1,0:T(8,128)} %get-tuple-element.78.norms, bf16[256,3072]{1,0:T(8,128)(2,1)} %bitcast.64, f32[2,256,3072]{2,1,0:T(8,128)} %state.6, f32[256,3072]{1,0:T(8,128)} %master.6), custom_call_target="tpu_custom_call" | custom-call | tf_op jit(solution)/shard_map/update_weight/pallas_call | solution.py:1237
  467.2 0.0 copy-start
  467.2 0.0 copy-start.2
  467.2 6.4 %update_weight.5 = (f32[512,1024]{1,0:T(8,128)}, f32[2,512,1024]{2,1,0:T(8,128)}, f32[512,1024]{1,0:T(8,128)}) custom-call(f32[16,128]{1,0:T(8,128)} %get-tuple-element.78.norms, bf16[512,1024]{1,0:T(8,128)(2,1)} %bitcast.65, f32[2,512,1024]{2,1,0:T(8,128)} %state.5, f32[512,1024]{1,0:T(8,128)} %master.5), custom_call_target="tpu_custom_call" | custom-call | tf_op jit(solution)/shard_map/update_weight/pallas_call | solution.py:1237
  473.6 0.0 copy-done
  473.6 0.0 copy-done.2
  473.6 1.2 slice_bitcast_fusion
  (3 shorter events, 0.0 us)
Async XLA Ops:
  4.3 182.2 %copy-start.6 = (f32[2,11,256]{2,0,1:T(2,128)S(1)}, f32[2,11,256]{2,0,1:T(2,128)}, u32[]{:S(2)}) copy-start(f32[2,11,256]{2,0,1:T(2,128)} %param.29) | copy-start | bytes 67588
  4.3 182.9 %copy-start.1 = (bf16[1,276,1024]{2,1,0:T(8,128)(2,1)S(1)}, bf16[1,276,1024]{2,1,0:T(8,128)(2,1)}, u32[]{:S(2)}) copy-start(bf16[1,276,1024]{2,1,0:T(8,128)(2,1)} %param.17) | copy-start | bytes 1695748
  188.1 236.8 %copy-start.5 = (f32[11,256]{1,0:T(8,128)S(1)}, f32[11,256]{1,0:T(8,128)}, u32[]{:S(2)}) copy-start(f32[11,256]{1,0:T(8,128)} %param.23) | copy-start | bytes 33796
  426.2 13.7 %copy-start.4 = (f32[11,256]{1,0:T(8,128)}, f32[11,256]{1,0:T(8,128)S(1)}, u32[]{:S(2)}) copy-start(f32[11,256]{1,0:T(8,128)S(1)} %get-tuple-element.147) | copy-start | bytes 33796
  426.8 13.0 %copy-start.3 = (f32[16,128]{1,0:T(8,128)S(1)}, f32[16,128]{1,0:T(8,128)}, u32[]{:S(2)}) copy-start(f32[16,128]{1,0:T(8,128)} %get-tuple-element.78.norms) | copy-start | bytes 24580
  467.2 6.4 %copy-start = (bf16[288,2048]{1,0:T(8,128)(2,1)S(1)}, bf16[288,2048]{1,0:T(8,128)(2,1)}, u32[]{:S(2)}) copy-start(bf16[288,2048]{1,0:T(8,128)(2,1)} %get-tuple-element.77) | copy-start | bytes 3538948
  467.2 6.4 %copy-start.2 = (bf16[288,1024]{1,0:T(8,128)(2,1)S(1)}, bf16[288,1024]{1,0:T(8,128)(2,1)}, u32[]{:S(2)}) copy-start(bf16[288,1024]{1,0:T(8,128)(2,1)} %get-tuple-element.61) | copy-start | bytes 1769476

commit v5 on v4

--- a/solution.py
+++ b/solution.py
@@ -59,6 +59,59 @@
     return chunks
 
 
+class Plan:
+    def __init__(self, latency=1.5):
+        self.now, self.latency = 0.0, latency
+        self.free = {}
+        self.agents = []
+
+    def transfer(self, link, length):
+        self.free[link] = max(self.now, self.free.get(link, 0.0)) + length
+        return self.free[link] + self.latency
+
+    def backlog(self, link):
+        return self.free.get(link, 0.0) - self.now
+
+    def add(self, steps):
+        agent = [steps, 0.0, None]
+        self.agents.append(agent)
+        self.resume(agent)
+
+    def resume(self, agent):
+        try:
+            agent[1], agent[2] = next(agent[0])
+        except StopIteration:
+            self.agents.remove(agent)
+
+    def ready(self):
+        return [a for a in self.agents if a[2] is None or a[2]()]
+
+    def pump(self):
+        while True:
+            able = [agent for agent in self.ready() if agent[1] <= self.now]
+            if not able:
+                return
+            self.resume(able[0])
+
+    def spend(self, length):
+        self.now += length
+        self.pump()
+
+    def until(self, moment):
+        self.pump()
+        while self.now < moment:
+            times = [agent[1] for agent in self.ready() if agent[1] > self.now]
+            self.now = min(times + [moment])
+            self.pump()
+
+    def finish(self, test):
+        self.pump()
+        while not test():
+            times = [agent[1] for agent in self.ready()]
+            self.now = max(self.now, min(times))
+            self.pump()
+
+
 step_rate = 0.3
 
 
@@ -105,6 +158,11 @@
     rows = lax.all_to_all(rows, "shard", 0, 0, tiled=True)
     rows = rows.reshape(shards, sequences * portion, parts, width).transpose(1, 2, 0, 3)
     return rows.reshape(sequences * portion, parts * shards * width)
+
+
+SLOTS = 19
+LINK_RATE = 45e3
+Z_BACKLOG = 5.0
 
 
 def weight_tile(whole, shard, group, start, width):
@@ -154,7 +212,7 @@
         mixed,
         middle,
         second_in,
-        expanded,
+        slope,
         activated,
         out,
         table,
@@ -179,6 +237,7 @@
     rows = entering.shape[0]
     width = entering.shape[1]
     own = width // SHARDS
+    pairs = own // 128
     factor = 1.0 / math.sqrt(HEAD_DIM)
 
     def load(at):
@@ -195,10 +254,24 @@
         return wholes[index].at[(shard, group) + rest + (pl.ds(part * BLOCK, BLOCK),)]
 
     sent = []
+    far = []
     arrivals = {}
 
+    def relay_copy(at):
+        up = s == SHARDS - 2
+        ref = whole(at, place.source(2), k, slice(None), y, x)
+        target = jnp.where(up, SHARDS - 1, 0)
+        return pltpu.make_async_remote_copy(
+            src_ref=ref,
+            dst_ref=ref,
+            send_sem=send_sems.at[at * SLOTS + SLOTS - 1],
+            recv_sem=recv_sems.at[at * SLOTS + jnp.where(up, SHARDS - 2, 0)],
+            device_id=(place.rep, target),
+            device_id_type=MESH,
+        )
+
     def go(at, name, position, ref, device):
-        slot = at * 18 + position
+        slot = at * SLOTS + position
         copy = pltpu.make_async_remote_copy(
             src_ref=ref,
             dst_ref=ref,
@@ -247,10 +320,42 @@
 
     def stage_z(at):
         for offset in range(1, SHARDS):
-            go(at, "z", offset - 1, whole(at, s, k, slice(None), y, x), place.along(offset))
+            ref = whole(at, s, k, slice(None), y, x)
+            slot = at * SLOTS + offset - 1
+            target = lax.rem(s + offset, SHARDS)
+            copy = pltpu.make_async_remote_copy(
+                src_ref=ref,
+                dst_ref=ref,
+                send_sem=send_sems.at[slot],
+                recv_sem=recv_sems.at[slot],
+                device_id=(place.rep, target),
+                device_id_type=MESH,
+            )
+            arrivals[(at, "z", offset)] = copy
+            if offset == 2:
+                copy.start()
+                sent.append(copy)
+            else:
+                near = s != (0 if offset == SHARDS - 1 else SHARDS - 1)
+                far.append((near, copy))
+
+                @pl.when(near)
+                def _(copy=copy):
+                    copy.start()
+
+    def stage_relay(at):
+        arrivals[(at, "z", 2)].wait_recv()
+        inner = (s > 0) & (s < SHARDS - 1)
+        copy = relay_copy(at)
+        far.append((inner, copy))
+
+        @pl.when(inner)
+        def _():
+            copy.start()
 
     def stage_first(at):
-        arrived(at, "z")
+        arrivals[(at, "z", 1)].wait_recv()
+        arrivals[(at, "z", 3)].wait_recv()
         for offset in range(1, SHARDS):
             e = place.source(offset)
             go(at, "first", 3 + 2 * (offset - 1), whole(at, e, k, 0, y, x), place.across("x"))
@@ -281,27 +386,39 @@
         copy.start()
         kept.append(copy)
 
-    stages = (stage_z, stage_first, stage_second, stage_core, stage_end)
-    lead = 4
-    step_now = [0]
-
-    def advance():
-        step = step_now[0]
-        if step >= total + 3:
-            return False
-        for position in range(1, 5):
-            at = step - (position - 1)
-            if 0 <= at < total:
-                stages[position](at)
-        if step + lead < total:
-            stage_cast(step + lead)
-            stage_z(step + lead)
-        step_now[0] = step + 1
-        return True
+    plan = Plan()
+    done = [0] * total
+    unit = UNIT * BLOCK * 2 / LINK_RATE
+
+    def chunk_steps(at):
+        yield 0.0, lambda: (at == 0 or done[at - 1] >= 1) and plan.backlog("z") < Z_BACKLOG
+        stage_cast(at)
+        plan.now += 0.6
+        stage_z(at)
+        start = plan.transfer("z", 6 * unit)
+        done[at] = 1
+        yield start - 2 * unit, None
+        stage_relay(at)
+        yield start + 1.0, None
+        stage_first(at)
+        moment = max(plan.transfer("x", 3 * unit), plan.transfer("y", 3 * unit))
+        yield moment, None
+        stage_second(at)
+        moment = max(plan.transfer("x", 6 * unit), plan.transfer("y", 6 * unit))
+        yield moment, None
+        stage_core(at)
+        plan.now += 0.2
+        yield plan.transfer("core", 24 * unit / 6), None
+        stage_end(at)
+        done[at] = 2
 
     def until(at):
-        while step_now[0] - 4 < at:
-            advance()
+        plan.finish(lambda: done[at] == 2)
+
+    def arrive(copies, moment):
+        plan.until(moment)
+        for copy in copies:
+            copy.wait_recv()
 
     load(0).start()
     load(1).start()
@@ -309,14 +426,10 @@
     table_all[0] = vectors[...].astype(LOW)
     greet(place)
     table_copies = []
-    for at in range(min(lead, total)):
-        stage_cast(at)
-        stage_z(at)
-        if at == 0:
-            for offset in range(1, SHARDS):
-                table_copies.append(
-                    extra(offset - 1, table_own, table_all.at[offset], place.along(offset))
-                )
+    for offset in range(1, SHARDS):
+        table_copies.append(extra(offset - 1, table_own, table_all.at[offset], place.along(offset)))
+    for at in range(total):
+        plan.add(chunk_steps(at))
     last = {}
     for at, (index, group, part) in enumerate(chunks):
         last[index] = at
@@ -336,7 +449,9 @@
             product(joined, wholes[0], start, 256) + table[0:1, pl.ds(start, 256)]
         )
 
+    plan.spend(2.5)
     norm_rows(entering, table[1:2, :], table[2:3, :], first_in, rows)
+    plan.spend(2.0)
     until(last[1])
     live = lax.broadcasted_iota(jnp.int32, (rows, own), 0) < portion
     for kind in range(3):
@@ -344,55 +459,62 @@
         @pl.loop(0, SHARDS)
         def _(target):
             start = pl.multiple_of(kind * width + target * own, own)
-            outgoing[target, :, kind * own : (kind + 1) * own] = jnp.where(
-                live, product(first_in, wholes[1], start, own), 0.0
-            ).astype(LOW)
+            value = jnp.where(live, product(first_in, wholes[1], start, own), 0.0).astype(LOW)
+            for pair in range(pairs):
+                first = (3 * pair + kind) * 128
+                outgoing[target, :, first : first + 128] = value[:, pair * 128 : (pair + 1) * 128]
+
+        plan.spend(1.5)
 
     head_copies = []
-    for offset in range(1, SHARDS):
-        target = lax.rem(s + offset, SHARDS)
-        head_copies.append(
-            extra(
-                2 + offset,
-                outgoing.at[target],
-                heads.at[pl.ds(offset * rows, rows), :],
-                place.along(offset),
+    moments = []
+    for pair in range(pairs):
+        moments.append(plan.transfer("z", 4 * rows * 384 * 2 / LINK_RATE))
+        for offset in range(1, SHARDS):
+            target = lax.rem(s + offset, SHARDS)
+            columns = pl.ds(pair * 384, 384)
+            head_copies.append(
+                extra(
+                    3 * pair + 2 + offset,
+                    outgoing.at[target, :, columns],
+                    heads.at[pl.ds(offset * rows, rows), columns],
+                    place.along(offset),
+                )
             )
-        )
 
     @pl.loop(0, rows // 32)
     def _(block):
         where = pl.ds(pl.multiple_of(block * 32, 32), 32)
         heads[where, :] = outgoing[s, where, :]
 
-    advance()
-    advance()
-    for copy in head_copies:
-        copy.wait_recv()
-
+    plan.spend(0.5)
     everyone = SHARDS * rows
     tile = 384
     lane = lax.broadcasted_iota(jnp.int32, (tile, 128), 1)
-    key_row = lax.broadcasted_iota(jnp.int32, (everyone, tile), 0)
-    for pair in range(own // 128):
-
-        @pl.loop(0, everyone // tile)
-        def _(block):
-            start = pl.multiple_of(block * tile, 128)
-            where = pl.ds(start, tile)
-            query = heads[where, pair * 128 : (pair + 1) * 128]
-            keys = heads[:, own + pair * 128 : own + (pair + 1) * 128]
-            values = heads[:, 2 * own + pair * 128 : 2 * own + (pair + 1) * 128]
+    key_row = lax.rem(lax.broadcasted_iota(jnp.int32, (everyone, 1), 0), rows)
+    key_bias = jnp.where(key_row < portion, 0.0, -1e30)
+    answer_copies = []
+    column = pl.multiple_of(s * own, own)
+    for pair in range(pairs):
+        arrive(head_copies[3 * pair : 3 * pair + 3], moments[pair])
+        base = pair * 384
+
+        for block in range(everyone // tile):
+            start = block * tile
+            where = slice(start, start + tile)
+            query = heads[where, base : base + 128]
+            keys = heads[:, base + 128 : base + 256]
+            values = heads[:, base + 256 : base + 384]
             parts = []
             for half in range(2):
                 inside = (lane // 64) == half
                 picked = jnp.where(inside, query.astype(jnp.float32) * factor, 0.0).astype(LOW)
                 scores = contract(keys, picked, 1, 1)
-                scores = jnp.where(lax.rem(key_row, rows) < portion, scores, -1e30)
+                scores = scores + key_bias
                 top = jnp.max(scores, 0, keepdims=True)
                 weight = jnp.exp(scores - top)
                 weight_sum = jnp.sum(weight, 0, keepdims=True)
-                log_total[2 * pair + half : 2 * pair + half + 1, pl.ds(start, tile)] = (
+                log_total[2 * pair + half : 2 * pair + half + 1, where] = (
                     top + jnp.log(weight_sum)
                 )
                 weight = (weight * (1.0 / weight_sum)).astype(LOW)
@@ -400,24 +522,23 @@
                 parts.append(summed[half * 64 : (half + 1) * 64])
             both = jnp.concatenate(parts, 0)
             answer[where, pair * 128 : (pair + 1) * 128] = both.T.astype(LOW)
-
-        advance()
-
-    answer_copies = []
-    column = pl.multiple_of(s * own, own)
-    for offset in range(1, SHARDS):
-        answer_copies.append(
-            extra(
-                5 + offset,
-                answer.at[pl.ds(offset * rows, rows), :],
-                mixed.at[:, pl.ds(column, own)],
-                (place.rep, place.source(offset)),
+            plan.spend(2.0)
+
+        answer_moment = plan.transfer("z", 4 * rows * 128 * 2 / LINK_RATE)
+        columns = pl.ds(pair * 128, 128)
+        for offset in range(1, SHARDS):
+            answer_copies.append(
+                extra(
+                    3 * (pairs + pair) + 2 + offset,
+                    answer.at[pl.ds(offset * rows, rows), columns],
+                    mixed.at[:, pl.ds(column + pair * 128, 128)],
+                    (place.rep, place.source(offset)),
+                )
             )
-        )
+
     mixed[:, pl.ds(column, own)] = answer[0:rows, :]
     until(last[2])
-    for copy in answer_copies:
-        copy.wait_recv()
+    arrive(answer_copies, answer_moment)
 
     @pl.loop(0, width // 256)
     def _(part):
@@ -427,9 +548,11 @@
             entering[:, where] + product(mixed, wholes[2], start, 256) + table[3:4, where]
         )
 
+    plan.spend(1.5)
     norm_rows(middle, table[4:5, :], table[5:6, :], second_in, rows)
+    plan.spend(2.0)
     per_row = width // 256
-    for part in range(expanded.shape[1] // BLOCK):
+    for part in range(slope.shape[1] // BLOCK):
         until(last[2] + 1 + part)
 
         @pl.loop(0, BLOCK // 256)
@@ -440,10 +563,12 @@
                 product(second_in, wholes[3], start, 256)
                 + table[7 + part : 8 + part, pl.ds(bias_at, 256)]
             )
-            expanded[:, pl.ds(start, 256)] = value
-            activated[:, pl.ds(start, 256)] = (
-                value * (0.5 + 0.5 * lax.erf(value * math.sqrt(0.5)))
-            ).astype(LOW)
+            below = 0.5 + 0.5 * lax.erf(value * math.sqrt(0.5))
+            bell = jnp.exp(-0.5 * value * value) * (1.0 / math.sqrt(2.0 * math.pi))
+            slope[:, pl.ds(start, 256)] = below + value * bell
+            activated[:, pl.ds(start, 256)] = (value * below).astype(LOW)
+
+        plan.spend(4.0)
 
     until(last[4])
 
@@ -457,6 +582,12 @@
 
     for copy in sent:
         copy.wait_send()
+    for used, copy in far:
+
+        @pl.when(used)
+        def _(copy=copy):
+            copy.wait_send()
+
     for copy in kept:
         copy.wait()
 
@@ -504,10 +635,10 @@
             pltpu.VMEM((everyone, own), LOW),
             pltpu.SemaphoreType.DMA((2,)),
             pltpu.SemaphoreType.DMA((total,)),
-            pltpu.SemaphoreType.DMA((total * 18,)),
-            pltpu.SemaphoreType.DMA((total * 18,)),
-            pltpu.SemaphoreType.DMA((9,)),
-            pltpu.SemaphoreType.DMA((9,)),
+            pltpu.SemaphoreType.DMA((total * SLOTS,)),
+            pltpu.SemaphoreType.DMA((total * SLOTS,)),
+            pltpu.SemaphoreType.DMA((3 + 6 * (own // 128),)),
+            pltpu.SemaphoreType.DMA((3 + 6 * (own // 128),)),
         ],
         compiler_params=pltpu.CompilerParams(
             collective_id=1, has_side_effects=True, vmem_limit_bytes=60 * 2**20
@@ -550,18 +681,11 @@
 def backward_kernel(chunks, portion, *refs):
     (
         cotangent,
-        joined,
         vectors,
-        entering,
-        first_in,
-        heads,
         log_total,
-        mixed,
-        middle,
-        second_in,
-        expanded,
         activated,
-    ) = refs[:12]
+    ) = refs[:4]
+    outside = refs[4:12]
     weights = refs[12:17]
     masters = refs[17:22]
     states = refs[22:27]
@@ -597,6 +721,15 @@
         grad_heads,
         grad_triple,
         grad_entering,
+        second_in,
+        slope,
+        middle,
+        mixed,
+        heads,
+        first_in,
+        entering,
+        joined,
+        load_sems,
         ring_sems,
         state_sems,
         ready_sems,
@@ -612,6 +745,18 @@
     factor = 1.0 / math.sqrt(HEAD_DIM)
     depth = ring.shape[0]
 
+    inside = (second_in, slope, middle, mixed, heads, first_in, entering, joined)
+    loads = [
+        pltpu.make_async_copy(source, target, load_sems.at[position])
+        for position, (source, target) in enumerate(zip(outside, inside))
+    ]
+    names = ["second_in", "slope", "middle", "mixed", "heads", "first_in", "entering", "joined"]
+    waiting_for = dict(zip(names, loads))
+
+    def need(name):
+        if name in waiting_for:
+            waiting_for.pop(name).wait()
+
     def tiles(index):
         parts = weights[index].shape[7] // BLOCK
         return weights[index].shape[1], parts, SHARDS * weights[index].shape[1] * parts
@@ -657,6 +802,7 @@
         copies.setdefault((at, name), []).append(copy)
 
     sent = []
+    more = 18
 
     def extra(slot, source, target, device):
         copy = pltpu.make_async_remote_copy(
@@ -679,8 +825,22 @@
         for copy in copies.pop((at, name), []):
             copy.wait_send()
 
+    pairs = own // 128
+
+    def triple_part(part):
+        return jnp.concatenate(
+            [
+                grad_triple[shard, :, (3 * pair + part) * 128 : (3 * pair + part + 1) * 128]
+                for shard in range(SHARDS)
+                for pair in range(pairs)
+            ],
+            1,
+        )
+
     def gradient_half(at, core):
         index, group, part = chunks[at]
+        if index < 4:
+            need(("joined", "first_in", "mixed", "second_in")[index])
         lefts = (joined, first_in, mixed, second_in, activated)[index]
         pitch = lefts.shape[1] // SHARDS
         columns = [
@@ -690,10 +850,7 @@
         if index == 0:
             right = grad_entering[...]
         elif index == 1:
-            right = jnp.concatenate(
-                [grad_triple[shard, :, part * own : (part + 1) * own] for shard in range(SHARDS)],
-                1,
-            )
+            right = triple_part(part)
         elif index == 2:
             right = grad_middle_low[...]
         elif index == 3:
@@ -854,26 +1011,56 @@
         stage_twin,
         stage_end,
     )
-    ages = {}
-    upcoming = [0]
-
-    def tick(start=False):
-        for at in sorted(ages):
-            stages[ages[at]](at)
-            ages[at] += 1
-            if ages[at] == len(stages):
-                del ages[at]
-        if start:
-            at = upcoming[0]
-            stages[0](at)
-            ages[at] = 1
-            upcoming[0] = at + 1
+    plan = Plan()
+    total = len(chunks)
+    at_stage = [0] * total
+    allowed = [0]
+    unit = UNIT * BLOCK * 2 / LINK_RATE
+    costs = (0.8, 1.8, 0.6, 0.4, 0.4, 0.2, 0.1, 0.0)
+    lengths = (
+        (("core", 32 * unit / 6),),
+        (("x", 8 * unit), ("y", 8 * unit)),
+        (("x", 4 * unit), ("y", 4 * unit)),
+        (("z", 8 * unit),),
+        (("x", unit), ("y", unit)),
+        (("x", 2 * unit), ("y", 2 * unit)),
+        (("core", 8 * unit / 6),),
+        (),
+    )
+
+    def chunk_steps(at):
+        moment = 0.0
+        for number, stage in enumerate(stages):
+            def free(number=number):
+                if number == 0 and at >= allowed[0]:
+                    return False
+                return at == 0 or at_stage[at - 1] >= min(number + 2, len(stages))
+
+            yield moment, free
+            stage(at)
+            plan.now += costs[number]
+            at_stage[at] = number + 1
+            moment = max([plan.transfer(link, length) for link, length in lengths[number]] + [0.0])
+
+    for at in range(total):
+        plan.add(chunk_steps(at))
+
+    def allow(index):
+        allowed[0] = sum(1 for chunk in chunks if chunk[0] >= index)
+        plan.pump()
+
+    def arrive(copies, moment):
+        plan.until(moment)
+        for copy in copies:
+            copy.wait_recv()
 
     prime(4)
+    for copy in loads:
+        copy.start()
     squares[...] = jnp.zeros_like(squares)
     table_own[...] = jnp.zeros_like(table_own)
     greet(place)
-    tick(True)
+    allow(4)
 
     def put_row(row, value):
         for shard in range(SHARDS):
@@ -882,6 +1069,7 @@
     put_row(6, jnp.sum(cotangent[...].astype(jnp.float32), 0, keepdims=True))
 
     groups = tiles(4)[0]
+    need("slope")
     for quarter in range(SHARDS):
 
         @pl.loop(0, groups)
@@ -890,18 +1078,15 @@
             act = contract(cotangent[...], take(4, at), 1, 1)
             give(4, at)
             where = pl.ds(pl.multiple_of(at * 256, 256), 256)
-            value = expanded[:, where]
-            slope = 0.5 + 0.5 * lax.erf(value * math.sqrt(0.5))
-            slope = slope + value * jnp.exp(-0.5 * value * value) * (1.0 / math.sqrt(2.0 * math.pi))
-            low = (act * slope).astype(LOW)
+            low = (act * slope[:, where]).astype(LOW)
             grad_inner[:, where] = low
             table_own[0, group, 7 + quarter : 8 + quarter, :] = jnp.sum(
                 low.astype(jnp.float32), 0, keepdims=True
             )
 
-        if quarter % 2:
-            tick(True)
+        plan.spend(1.5)
     prime(3)
+    allow(3)
     parts = tiles(3)[1]
 
     @pl.loop(0, SHARDS)
@@ -916,55 +1101,64 @@
         grad_second[:, where] = total
 
     prime(2)
-    tick(True)
+    plan.spend(3.0)
+    need("middle")
     gain_sum, bias_sum, low_sum = norm_back(
         middle, vectors[4:5, :], grad_second, cotangent, grad_middle, grad_middle_low, rows
     )
     put_row(4, gain_sum)
     put_row(5, bias_sum)
     put_row(3, low_sum)
+    plan.spend(3.0)
+    allow(2)
 
     @pl.loop(0, SHARDS)
     def _(shard):
         outgoing[shard, :, 0:own] = contract(grad_middle_low[...], take(2, shard), 1, 1).astype(LOW)
 
     prime(1)
+    plan.spend(1.0)
     mixed_copies = []
-    for offset in range(1, SHARDS):
-        mixed_copies.append(
-            extra(
-                offset - 1,
-                outgoing.at[lax.rem(s + offset, SHARDS), :, pl.ds(0, own)],
-                grad_mixed.at[pl.ds(offset * rows, rows), :],
-                place.along(offset),
+    moments = []
+    for pair in range(pairs):
+        moments.append(plan.transfer("z", 4 * rows * 128 * 2 / LINK_RATE))
+        columns = pl.ds(pair * 128, 128)
+        for offset in range(1, SHARDS):
+            mixed_copies.append(
+                extra(
+                    more + 3 * pair + offset - 1,
+                    outgoing.at[lax.rem(s + offset, SHARDS), :, columns],
+                    grad_mixed.at[pl.ds(offset * rows, rows), columns],
+                    place.along(offset),
+                )
             )
-        )
 
     @pl.loop(0, rows // 32)
     def _(block):
         where = pl.ds(pl.multiple_of(block * 32, 32), 32)
         grad_mixed[where, :] = outgoing[s, where, 0:own]
 
-    tick(True)
-    for copy in mixed_copies:
-        copy.wait_recv()
-
+    plan.spend(0.5)
+    need("heads")
     everyone = SHARDS * rows
     tile = 384
     lane = lax.broadcasted_iota(jnp.int32, (tile, 128), 1)
-    key_row = lax.broadcasted_iota(jnp.int32, (everyone, tile), 0)
-    for pair in range(own // 128):
+    key_row = lax.rem(lax.broadcasted_iota(jnp.int32, (everyone, 128), 0), rows)
+    live = key_row < portion
+    triple_copies = []
+    for pair in range(pairs):
+        arrive(mixed_copies[3 * pair : 3 * pair + 3], moments[pair])
+        base = pair * 384
         grad_key[...] = jnp.zeros_like(grad_key)
         grad_value[...] = jnp.zeros_like(grad_value)
         low, high = pair * 128, (pair + 1) * 128
 
-        @pl.loop(0, everyone // tile)
-        def _(block):
-            start = pl.multiple_of(block * tile, 128)
-            where = pl.ds(start, tile)
-            query = heads[where, low:high]
-            keys = heads[:, own + low : own + high]
-            values = heads[:, 2 * own + low : 2 * own + high]
+        for block in range(everyone // tile):
+            start = block * tile
+            where = slice(start, start + tile)
+            query = heads[where, base : base + 128]
+            keys = heads[:, base + 128 : base + 256]
+            values = heads[:, base + 256 : base + 384]
             incoming = grad_mixed[where, low:high]
             parts = []
             for half in range(2):
@@ -972,12 +1166,12 @@
                 picked = jnp.where(inside, query.astype(jnp.float32) * factor, 0.0).astype(LOW)
                 grads = jnp.where(inside, incoming.astype(jnp.float32), 0.0).astype(LOW)
                 scores = contract(keys, picked, 1, 1)
-                scores = jnp.where(lax.rem(key_row, rows) < portion, scores, -1e30)
                 at = 2 * pair + half
-                weight = jnp.exp(scores - log_total[at : at + 1, pl.ds(start, tile)])
-                slope = contract(values, grads, 1, 1)
-                delta = jnp.sum(weight * slope, 0, keepdims=True)
-                grad_scores = (weight * (slope - delta)).astype(LOW)
+                below = scores - log_total[at : at + 1, where]
+                weight = jnp.exp(jnp.minimum(below, 0.0))
+                into = contract(values, grads, 1, 1)
+                delta = jnp.sum(weight * into, 0, keepdims=True)
+                grad_scores = (weight * (into - delta)).astype(LOW)
                 grad_key[...] += jnp.dot(
                     grad_scores, picked, preferred_element_type=jnp.float32
                 )
@@ -987,32 +1181,31 @@
                 turned = contract(keys, grad_scores, 0, 0)
                 parts.append(turned[half * 64 : (half + 1) * 64])
             both = jnp.concatenate(parts, 0) * factor
-            grad_heads[where, low:high] = both.T.astype(LOW)
-
-        grad_heads[:, own + low : own + high] = grad_key[...].astype(LOW)
-        grad_heads[:, 2 * own + low : 2 * own + high] = grad_value[...].astype(LOW)
-        tick(True)
-
-    triple_copies = []
-    for offset in range(1, SHARDS):
-        triple_copies.append(
-            extra(
-                2 + offset,
-                grad_heads.at[pl.ds(offset * rows, rows), :],
-                grad_triple.at[s],
-                (place.rep, place.source(offset)),
+            grad_heads[where, base : base + 128] = both.T.astype(LOW)
+            plan.spend(4.0)
+
+        grad_heads[:, base + 128 : base + 256] = jnp.where(live, grad_key[...], 0.0).astype(LOW)
+        grad_heads[:, base + 256 : base + 384] = jnp.where(live, grad_value[...], 0.0).astype(LOW)
+        columns = pl.ds(base, 384)
+        triple_moment = plan.transfer("z", 4 * rows * 384 * 2 / LINK_RATE)
+        for offset in range(1, SHARDS):
+            triple_copies.append(
+                extra(
+                    more + 3 * (pairs + pair) + offset - 1,
+                    grad_heads.at[pl.ds(offset * rows, rows), columns],
+                    grad_triple.at[s, :, columns],
+                    (place.rep, place.source(offset)),
+                )
             )
-        )
+        plan.pump()
 
     @pl.loop(0, rows // 32)
     def _(block):
         where = pl.ds(pl.multiple_of(block * 32, 32), 32)
         grad_triple[s, where, :] = grad_heads[where, :]
 
-    tick(True)
-    tick(True)
-    for copy in triple_copies:
-        copy.wait_recv()
+    arrive(triple_copies, triple_moment)
+    allow(1)
     parts_in = tiles(1)[1]
 
     @pl.loop(0, SHARDS)
@@ -1021,21 +1214,22 @@
         total = None
         for part in range(parts_in):
             at = shard * parts_in + part
-            left_side = jnp.concatenate(
-                [grad_triple[g, :, part * own : (part + 1) * own] for g in range(SHARDS)], 1
-            )
-            term = contract(left_side, take(1, at), 1, 1)
+            term = contract(triple_part(part), take(1, at), 1, 1)
             give(1, at)
             total = term if total is None else total + term
         grad_second[:, where] = total
 
     prime(0)
+    need("entering")
+    plan.spend(3.0)
     gain_sum, bias_sum, low_sum = norm_back(
         entering, vectors[1:2, :], grad_second, grad_middle, None, grad_entering, rows
     )
     put_row(1, gain_sum)
     put_row(2, bias_sum)
     put_row(0, low_sum)
+    plan.spend(3.0)
+    allow(0)
     table_copies = []
 
     def table_step(position, axis):
@@ -1052,73 +1246,79 @@
                 )
             )
 
-    table_step(0, "core")
-    tick(True)
-    table_step(1, "x")
-
     @pl.loop(0, tiles(0)[2])
     def _(at):
         where = pl.ds(pl.multiple_of(at * 256, 256), 256)
         grad_joined[:, where] = contract(grad_entering[...], take(0, at), 1, 1).astype(LOW)
         give(0, at)
 
-    table_step(2, "y")
-    tick(True)
-    table_step(3, None)
-    for offset in range(1, SHARDS):
-        table_copies.append(
-            extra(
-                8 + offset,
-                table_own.at[3, lax.rem(s + offset, SHARDS)],
-                table_z.at[offset - 1],
-                place.along(offset),
+    plan.spend(1.5)
+
+    def table_steps():
+        for position, axis in enumerate(("core", "x", "y", None)):
+            table_step(position, axis)
+            if axis:
+                yield plan.transfer(axis, 1.5), None
+        for offset in range(1, SHARDS):
+            table_copies.append(
+                extra(
+                    8 + offset,
+                    table_own.at[3, lax.rem(s + offset, SHARDS)],
+                    table_z.at[offset - 1],
+                    place.along(offset),
+                )
             )
-        )
-    tick(True)
-    for copy in table_copies[3:]:
-        copy.wait_recv()
-    value = table_own[3, s]
-    for offset in range(1, SHARDS):
-        value = value + table_z[offset - 1]
-    table_sum[...] = value
-    direction = direction_of(value, own_states[0], own_states[1])
-    share = 1.0 / REPLICAS
-    squares[0, 5:6, :] = share * lanes(own_vectors[...] * own_vectors[...])
-    squares[0, 13:14, :] = share * lanes(direction * direction)
-    while upcoming[0] < len(chunks):
-        tick(True)
-    square_copies = []
-    square_axes = ("core", "x", "y")
-    position = 0
-    while ages or position < 4:
-        if ages:
-            tick()
-        waiting = [at for at in ages if ages[at] <= 4]
-        if not waiting and position < 4:
+        yield plan.transfer("z", 2.0), None
+        for copy in table_copies[3:]:
+            copy.wait_recv()
+        value = table_own[3, s]
+        for offset in range(1, SHARDS):
+            value = value + table_z[offset - 1]
+        table_sum[...] = value
+        direction = direction_of(value, own_states[0], own_states[1])
+        share = 1.0 / REPLICAS
+        squares[0, 5:6, :] = share * lanes(own_vectors[...] * own_vectors[...])
+        squares[0, 13:14, :] = share * lanes(direction * direction)
+        table_done[0] = True
+
+    table_done = [False]
+    squares_done = [False]
+
+    def square_steps():
+        yield 0.0, lambda: table_done[0] and min(at_stage) >= 5
+        hops = []
+        for position, axis in enumerate(("core", "x", "y", None)):
             if position:
-                square_copies[-1].wait_recv()
+                hops[-1].wait_recv()
                 squares[position] = squares[position - 1] + square_in[position - 1]
-            if position < 3:
-                square_copies.append(
+            if axis:
+                hops.append(
                     extra(
                         12 + position,
                         squares.at[position],
                         square_in.at[position],
-                        place.across(square_axes[position]),
+                        place.across(axis),
                     )
                 )
-            position += 1
-    for offset in range(1, SHARDS):
-        square_copies.append(
-            extra(14 + offset, squares.at[3], square_z.at[offset], place.along(offset))
-        )
-    square_z[0] = squares[3]
-    for copy in square_copies[3:]:
-        copy.wait_recv()
-    value = square_z[s]
-    for shard in range(1, SHARDS):
-        value = value + square_z[lax.rem(s + SHARDS - shard, SHARDS)]
-    norms[...] = jnp.sqrt(jnp.sum(value, 1, keepdims=True)) + jnp.zeros_like(value)
+                yield plan.transfer(axis, 0.5), None
+        hops = []
+        for offset in range(1, SHARDS):
+            hops.append(
+                extra(14 + offset, squares.at[3], square_z.at[offset], place.along(offset))
+            )
+        square_z[0] = squares[3]
+        yield plan.transfer("z", 0.5), None
+        for copy in hops:
+            copy.wait_recv()
+        value = square_z[s]
+        for shard in range(1, SHARDS):
+            value = value + square_z[lax.rem(s + SHARDS - shard, SHARDS)]
+        norms[...] = jnp.sqrt(jnp.sum(value, 1, keepdims=True)) + jnp.zeros_like(value)
+        squares_done[0] = True
+
+    plan.add(table_steps())
+    plan.add(square_steps())
+    plan.finish(lambda: squares_done[0] and min(at_stage) == len(stages))
     for key in sorted(copies):
         for copy in copies[key]:
             copy.wait_send()
@@ -1127,14 +1327,15 @@
 
 
 def backward_pass(cotangent, joined, table, kept, weights, masters, states, vectors, vector_states, portion):
-    entering, first_in, heads, log_total, mixed, middle, second_in, expanded, activated = kept[:9]
+    entering, first_in, heads, log_total, mixed, middle, second_in, slope, activated = kept[:9]
     shapes = [(matrix.shape[0] * SHARDS, matrix.shape[1]) for matrix in masters]
     order = chunk_list(shapes)
     chunks = [chunk for index in (4, 3, 2, 1, 0) for chunk in order if chunk[0] == index]
     total = len(chunks)
     rows, width = entering.shape
     own = width // SHARDS
-    hidden = expanded.shape[1]
+    hidden = slope.shape[1]
+    loaded = (second_in, slope, middle, mixed, heads, first_in, entering, joined)
     everyone = SHARDS * rows
     piece = (UNIT, BLOCK)
     inner = pl.BlockSpec(memory_space=pltpu.VMEM)
@@ -1150,7 +1351,7 @@
             jax.ShapeDtypeStruct((16, 128), jnp.float32),
             jax.ShapeDtypeStruct((rows, 2 * width), LOW),
         ],
-        in_specs=[inner] * 12 + [ANY] * 15 + [inner] * 2,
+        in_specs=[inner] * 4 + [ANY] * 23 + [inner] * 2,
         out_specs=[ANY] * 5 + [inner] * 3,
         scratch_shapes=[
             pltpu.VMEM((8, 2, 2, 2, 2) + piece, LOW),
@@ -1181,13 +1382,15 @@
             pltpu.VMEM((everyone, 3 * own), LOW),
             pltpu.VMEM((SHARDS, rows, 3 * own), LOW),
             pltpu.VMEM((rows, width), LOW),
+            *[pltpu.VMEM(array.shape, array.dtype) for array in loaded],
+            pltpu.SemaphoreType.DMA((8,)),
             pltpu.SemaphoreType.DMA((8,)),
             pltpu.SemaphoreType.DMA((2, 2)),
             pltpu.SemaphoreType.DMA((2,)),
             pltpu.SemaphoreType.DMA((total * 14,)),
             pltpu.SemaphoreType.DMA((total * 14,)),
-            pltpu.SemaphoreType.DMA((18,)),
-            pltpu.SemaphoreType.DMA((18,)),
+            pltpu.SemaphoreType.DMA((18 + 6 * (own // 128),)),
+            pltpu.SemaphoreType.DMA((18 + 6 * (own // 128),)),
         ],
         compiler_params=pltpu.CompilerParams(
             collective_id=2, has_side_effects=True, vmem_limit_bytes=60 * 2**20
@@ -1195,17 +1398,10 @@
         name="backward_pass",
     )(
         cotangent,
-        joined,
         table,
-        entering,
-        first_in,
-        heads,
         log_total,
-        mixed,
-        middle,
-        second_in,
-        expanded,
         activated,
+        *loaded,
         *[matrix.reshape(fold) for matrix, fold in zip(weights, folds)],
         *[matrix.reshape(fold[1:]) for matrix, fold in zip(masters, folds)],
         *[state.reshape((2,) + fold[1:]) for state, fold in zip(states, folds)],

time: 484 us -> 436 us (0.901); the launches traced: 475 us -> 433 us
  Pallas kernels: 462 us -> 420 us
    pallas_call x1, Pallas kernels: 182 us -> 147 us  [forward_pass(): pl.pallas_call(functools.partial(forward_kernel, chunks, portion), out_sh...]
    pallas_call x1, Pallas kernels: 234 us -> 227 us  [backward_pass(): pl.pallas_call(functools.partial(backward_kernel, chunks, portion), out_s...]
where the time goes in v5:
time: 436 us; the launch traced here: 433 us
  Pallas kernels  420 us (96%)
  local copies, waits for them, and re-layouts  6.05 us (1%)
    pallas_call x1, Pallas kernels, backward_pass(): pl.pallas_call(functools.partial(backward_kernel, chunks, portion), out_s...  227 us
    pallas_call x1, Pallas kernels, forward_pass(): pl.pallas_call(functools.partial(forward_kernel, chunks, portion), out_sh...  147 us
    pallas_call x5, Pallas kernels, update_weight(): pl.pallas_call(functools.partial(update_kernel, position), grid=(rows //...  45.8 us

profile of v5, /device:TPU:0, one launch (start us, length us, event | category | flops | bytes accessed | tf_op | source)
XLA Modules:
  0.0 432.5 jit_solution(1650407337605050113)
XLA Ops:
  0.7 2.3 fusion.2.refs_0_.refs_11_
  3.0 1.3 pad.18.refs_1_.refs_27_
  4.3 0.0 copy-start.6
  4.3 0.0 copy-start.1
  4.3 146.8 %forward_pass.1 = (bf16[4,2,2,2,2,2,16,1024]{7,6,5,4,3,2,1,0:T(8,128)(2,1)}, bf16[4,1,2,2,2,2,16,3072]{7,6,5,4,3,2,1,0:T(8,128)(2,1)}, bf16[4,1,2,2,2,2,16,1024]...) custom-call(bf16[288,2048]{1,0:T(8,128)(2,1)} %fusion.2.refs_0_.refs, ...), custom_call_target="tpu_custom_call" | custom-call | tf_op jit(solution)/shard_map/forward_pass/pallas_call | solution.py:611
  151.2 0.0 copy-done.6
  151.2 0.6 pad.20.refs_28_
  151.8 0.0 copy-done.1
  151.8 0.9 pad.19.refs_0_
  152.7 0.0 copy-start.5
  152.7 227.1 %backward_pass.1 = (bf16[2,2,2,2,2,16,1024]{6,5,4,3,2,1,0:T(8,128)(2,1)}, bf16[1,2,2,2,2,16,3072]{6,5,4,3,2,1,0:T(8,128)(2,1)}, bf16[1,2,2,2,2,16,1024]{6,5,4,3,...) custom-call(bf16[288,1024]{1,0:T(8,128)(2,1)} %pad.19.refs_0_, ...), custom_call_target="tpu_custom_call" | custom-call | tf_op jit(solution)/shard_map/backward_pass/pallas_call | solution.py:1346
  379.8 1.2 fusion.8
  382.3 0.0 copy-done.5
  382.3 1.3 multiply_subtract_fusion
  383.6 0.0 copy-start.4
  383.7 0.6 copy.44
  384.3 0.0 copy-start.3
  384.3 12.8 %update_weight.9 = (f32[1024,1024]{1,0:T(8,128)}, f32[2,1024,1024]{2,1,0:T(8,128)}, f32[1024,1024]{1,0:T(8,128)}) custom-call(f32[16,128]{1,0:T(8,128)} %get-tuple-element.78.norms, bf16[1024,1024]{1,0:T(8,128)(2,1)} %bitcast.63, f32[2,1024,1024]{2,1,0:T(8,128)} %state.9, f32[1024,1024]{1,0:T(8,128)} %master.9), custom_call_target="tpu_custom_call" | custom-call | tf_op jit(solution)/shard_map/update_weight/pallas_call | solution.py:1433
  397.1 0.0 copy-done.4
  397.1 0.0 copy-done.3
  397.1 0.1 slice_reduce_fusion.1
  397.2 0.6 pad_maximum_fusion.1
  397.8 12.1 %update_weight.8 = (f32[256,4096]{1,0:T(8,128)}, f32[2,256,4096]{2,1,0:T(8,128)}, f32[256,4096]{1,0:T(8,128)}) custom-call(f32[16,128]{1,0:T(8,128)} %get-tuple-element.78.norms, bf16[256,4096]{1,0:T(8,128)(2,1)} %bitcast.62, f32[2,256,4096]{2,1,0:T(8,128)} %state.8, f32[256,4096]{1,0:T(8,128)} %master.8), custom_call_target="tpu_custom_call" | custom-call | tf_op jit(solution)/shard_map/update_weight/pallas_call | solution.py:1433
  409.9 5.0 %update_weight.7 = (f32[256,1024]{1,0:T(8,128)}, f32[2,256,1024]{2,1,0:T(8,128)}, f32[256,1024]{1,0:T(8,128)}) custom-call(f32[16,128]{1,0:T(8,128)} %get-tuple-element.78.norms, bf16[256,1024]{1,0:T(8,128)(2,1)} %bitcast.69, f32[2,256,1024]{2,1,0:T(8,128)} %state.7, f32[256,1024]{1,0:T(8,128)} %master.7), custom_call_target="tpu_custom_call" | custom-call | tf_op jit(solution)/shard_map/update_weight/pallas_call | solution.py:1433
  414.8 9.6 %update_weight.6 = (f32[256,3072]{1,0:T(8,128)}, f32[2,256,3072]{2,1,0:T(8,128)}, f32[256,3072]{1,0:T(8,128)}) custom-call(f32[16,128]{1,0:T(8,128)} %get-tuple-element.78.norms, bf16[256,3072]{1,0:T(8,128)(2,1)} %bitcast.64, f32[2,256,3072]{2,1,0:T(8,128)} %state.6, f32[256,3072]{1,0:T(8,128)} %master.6), custom_call_target="tpu_custom_call" | custom-call | tf_op jit(solution)/shard_map/update_weight/pallas_call | solution.py:1433
  424.5 0.0 copy-start
  424.5 0.0 copy-start.2
  424.5 6.4 %update_weight.5 = (f32[512,1024]{1,0:T(8,128)}, f32[2,512,1024]{2,1,0:T(8,128)}, f32[512,1024]{1,0:T(8,128)}) custom-call(f32[16,128]{1,0:T(8,128)} %get-tuple-element.78.norms, bf16[512,1024]{1,0:T(8,128)(2,1)} %bitcast.65, f32[2,512,1024]{2,1,0:T(8,128)} %state.5, f32[512,1024]{1,0:T(8,128)} %master.5), custom_call_target="tpu_custom_call" | custom-call | tf_op jit(solution)/shard_map/update_weight/pallas_call | solution.py:1433
  430.8 0.0 copy-done
  430.8 0.0 copy-done.2
  430.9 1.2 slice_bitcast_fusion
  (3 shorter events, 0.0 us)
Async XLA Ops:
  4.3 146.8 %copy-start.6 = (f32[2,11,256]{2,0,1:T(2,128)S(1)}, f32[2,11,256]{2,0,1:T(2,128)}, u32[]{:S(2)}) copy-start(f32[2,11,256]{2,0,1:T(2,128)} %param.29) | copy-start | bytes 67588
  4.3 147.5 %copy-start.1 = (bf16[1,276,1024]{2,1,0:T(8,128)(2,1)S(1)}, bf16[1,276,1024]{2,1,0:T(8,128)(2,1)}, u32[]{:S(2)}) copy-start(bf16[1,276,1024]{2,1,0:T(8,128)(2,1)} %param.17) | copy-start | bytes 1695748
  152.7 229.6 %copy-start.5 = (f32[11,256]{1,0:T(8,128)S(1)}, f32[11,256]{1,0:T(8,128)}, u32[]{:S(2)}) copy-start(f32[11,256]{1,0:T(8,128)} %param.23) | copy-start | bytes 33796
  383.6 13.4 %copy-start.4 = (f32[11,256]{1,0:T(8,128)}, f32[11,256]{1,0:T(8,128)S(1)}, u32[]{:S(2)}) copy-start(f32[11,256]{1,0:T(8,128)S(1)} %get-tuple-element.147) | copy-start | bytes 33796
  384.3 12.8 %copy-start.3 = (f32[16,128]{1,0:T(8,128)S(1)}, f32[16,128]{1,0:T(8,128)}, u32[]{:S(2)}) copy-start(f32[16,128]{1,0:T(8,128)} %get-tuple-element.78.norms) | copy-start | bytes 24580
  424.5 6.4 %copy-start = (bf16[288,2048]{1,0:T(8,128)(2,1)S(1)}, bf16[288,2048]{1,0:T(8,128)(2,1)}, u32[]{:S(2)}) copy-start(bf16[288,2048]{1,0:T(8,128)(2,1)} %get-tuple-element.77) | copy-start | bytes 3538948
  424.5 6.4 %copy-start.2 = (bf16[288,1024]{1,0:T(8,128)(2,1)S(1)}, bf16[288,1024]{1,0:T(8,128)(2,1)}, u32[]{:S(2)}) copy-start(bf16[288,1024]{1,0:T(8,128)(2,1)} %get-tuple-element.61) | copy-start | bytes 1769476

commit v6 on v5

--- a/solution.py
+++ b/solution.py
@@ -94,7 +94,7 @@
             self.resume(able[0])
 
     def spend(self, length):
-        self.now += length
+        self.now += 0.8 * length
         self.pump()
 
     def until(self, moment):
@@ -863,20 +863,20 @@
         slot = at % 2
         value = gradient_half(at, 1 - k).astype(LOW)
         theirs[slot] = value.reshape(SHARDS, 2, 2, 2, UNIT, BLOCK)
-        go(at, "core", 0, theirs.at[slot], from_core.at[slot], place.across("core"))
+        go(at, "core", 0, theirs.at[slot], from_core.at[at % 4], place.across("core"))
 
     def stage_first(at):
-        slot = at % 3
+        slot = at % 5
         value = gradient_half(at, k).reshape(SHARDS, 2, 2, 2, UNIT, BLOCK)
         arrived(at, "core")
         left(at, "core")
-        mine[slot] = (value + from_core[at % 2].astype(jnp.float32)).astype(LOW)
-        target = from_first.at[at % 2]
+        mine[slot] = (value + from_core[at % 4].astype(jnp.float32)).astype(LOW)
+        target = from_first.at[at % 4]
         go(at, "first", 1, mine.at[slot, :, 0, :, 1 - x], target.at[0], place.across("x"))
         go(at, "first", 2, mine.at[slot, :, 1, 1 - y], target.at[1], place.across("y"))
 
     def stage_second(at):
-        slot = at % 3
+        slot = at % 5
         arrived(at, "first")
         left(at, "first")
 
@@ -885,14 +885,14 @@
             for i in range(2):
                 mine[slot, shard, 0, i, x] = (
                     mine[slot, shard, 0, i, x].astype(jnp.float32)
-                    + from_first[at % 2, 0, shard, i].astype(jnp.float32)
+                    + from_first[at % 4, 0, shard, i].astype(jnp.float32)
                 ).astype(LOW)
                 mine[slot, shard, 1, y, i] = (
                     mine[slot, shard, 1, y, i].astype(jnp.float32)
-                    + from_first[at % 2, 1, shard, i].astype(jnp.float32)
+                    + from_first[at % 4, 1, shard, i].astype(jnp.float32)
                 ).astype(LOW)
 
-        target = from_second.at[at % 2]
+        target = from_second.at[at % 4]
         go(at, "second", 3, mine.at[slot, :, 0, 1 - y, x], target.at[0], place.across("y"))
         go(at, "second", 4, mine.at[slot, :, 1, y, 1 - x], target.at[1], place.across("x"))
 
@@ -914,7 +914,7 @@
         )
 
     def stage_z(at):
-        slot = at % 3
+        slot = at % 5
         arrived(at, "second")
         left(at, "second")
 
@@ -923,7 +923,7 @@
             for h in range(2):
                 final[at % 2, shard, h] = (
                     mine[slot, shard, h, y, x].astype(jnp.float32)
-                    + from_second[at % 2, h, shard].astype(jnp.float32)
+                    + from_second[at % 4, h, shard].astype(jnp.float32)
                 ).astype(LOW)
 
         for copy in piece_loads(at):
@@ -935,7 +935,7 @@
                 "z",
                 5 + offset - 1,
                 final.at[at % 2, target],
-                from_z.at[at % 2, offset - 1],
+                from_z.at[at % 4, offset - 1],
                 place.along(offset),
             )
 
@@ -969,7 +969,7 @@
         for h in range(2):
             value = final[slot, s, h].astype(jnp.float32)
             for offset in range(1, SHARDS):
-                value = value + from_z[slot, offset - 1, h].astype(jnp.float32)
+                value = value + from_z[at % 4, offset - 1, h].astype(jnp.float32)
             low = value.astype(LOW)
             ready[slot, h] = low
             direction = direction_of(
@@ -1016,7 +1016,7 @@
     at_stage = [0] * total
     allowed = [0]
     unit = UNIT * BLOCK * 2 / LINK_RATE
-    costs = (0.8, 1.8, 0.6, 0.4, 0.4, 0.2, 0.1, 0.0)
+    costs = (0.5, 1.1, 0.4, 0.25, 0.25, 0.1, 0.1, 0.0)
     lengths = (
         (("core", 32 * unit / 6),),
         (("x", 8 * unit), ("y", 8 * unit)),
@@ -1034,7 +1034,11 @@
             def free(number=number):
                 if number == 0 and at >= allowed[0]:
                     return False
-                return at == 0 or at_stage[at - 1] >= min(number + 2, len(stages))
+                if number == 1 and at >= 5 and at_stage[at - 5] < 4:
+                    return False
+                if at and at_stage[at - 1] <= number:
+                    return False
+                return at < 2 or at_stage[at - 2] >= min(number + 2, len(stages))
 
             yield moment, free
             stage(at)
@@ -1356,12 +1360,12 @@
         scratch_shapes=[
             pltpu.VMEM((8, 2, 2, 2, 2) + piece, LOW),
             pltpu.VMEM((2, SHARDS, 2, 2, 2) + piece, LOW),
-            pltpu.VMEM((3, SHARDS, 2, 2, 2) + piece, LOW),
-            pltpu.VMEM((2, SHARDS, 2, 2, 2) + piece, LOW),
-            pltpu.VMEM((2, 2, SHARDS, 2) + piece, LOW),
-            pltpu.VMEM((2, 2, SHARDS) + piece, LOW),
+            pltpu.VMEM((5, SHARDS, 2, 2, 2) + piece, LOW),
+            pltpu.VMEM((4, SHARDS, 2, 2, 2) + piece, LOW),
+            pltpu.VMEM((4, 2, SHARDS, 2) + piece, LOW),
+            pltpu.VMEM((4, 2, SHARDS) + piece, LOW),
             pltpu.VMEM((2, SHARDS, 2) + piece, LOW),
-            pltpu.VMEM((2, SHARDS - 1, 2) + piece, LOW),
+            pltpu.VMEM((4, SHARDS - 1, 2) + piece, LOW),
             pltpu.VMEM((2, 2) + piece, LOW),
             pltpu.VMEM((2, 2, 2) + piece, jnp.float32),
             pltpu.VMEM((2, 2) + piece, jnp.float32),

time: 436 us -> 414 us (0.950)
  Pallas kernels: 420 us -> 399 us
    pallas_call x1, Pallas kernels: 227 us -> 206 us  [backward_pass(): pl.pallas_call(functools.partial(backward_kernel, chunks, portion), out_s...]
where the time goes in v6:
time: 414 us; the launch traced here: 411 us
  Pallas kernels  399 us (96%)
  local copies, waits for them, and re-layouts  6.05 us (1%)
  other arithmetic  4.3 us (1%)
    pallas_call x1, Pallas kernels, backward_pass(): pl.pallas_call(functools.partial(backward_kernel, chunks, portion), out_s...  206 us
    pallas_call x1, Pallas kernels, forward_pass(): pl.pallas_call(functools.partial(forward_kernel, chunks, portion), out_sh...  147 us
    pallas_call x5, Pallas kernels, update_weight(): pl.pallas_call(functools.partial(update_kernel, position), grid=(rows //...  45.8 us

profile of v6, /device:TPU:0, one launch (start us, length us, event | category | flops | bytes accessed | tf_op | source)
XLA Modules:
  0.0 411.5 jit_solution(10578948667322353879)
XLA Ops:
  0.7 2.3 fusion.2.refs_0_.refs_11_
  3.0 1.3 pad.18.refs_1_.refs_27_
  4.3 0.0 copy-start.6
  4.3 0.0 copy-start.1
  4.3 146.5 %forward_pass.1 = (bf16[4,2,2,2,2,2,16,1024]{7,6,5,4,3,2,1,0:T(8,128)(2,1)}, bf16[4,1,2,2,2,2,16,3072]{7,6,5,4,3,2,1,0:T(8,128)(2,1)}, bf16[4,1,2,2,2,2,16,1024]...) custom-call(bf16[288,2048]{1,0:T(8,128)(2,1)} %fusion.2.refs_0_.refs, ...), custom_call_target="tpu_custom_call" | custom-call | tf_op jit(solution)/shard_map/forward_pass/pallas_call | solution.py:611
  150.9 0.0 copy-done.6
  150.9 0.6 pad.20.refs_28_
  151.5 0.0 copy-done.1
  151.5 0.9 pad.19.refs_0_
  152.4 0.0 copy-start.5
  152.4 206.3 %backward_pass.1 = (bf16[2,2,2,2,2,16,1024]{6,5,4,3,2,1,0:T(8,128)(2,1)}, bf16[1,2,2,2,2,16,3072]{6,5,4,3,2,1,0:T(8,128)(2,1)}, bf16[1,2,2,2,2,16,1024]{6,5,4,3,...) custom-call(bf16[288,1024]{1,0:T(8,128)(2,1)} %pad.19.refs_0_, ...), custom_call_target="tpu_custom_call" | custom-call | tf_op jit(solution)/shard_map/backward_pass/pallas_call | solution.py:1350
  358.7 1.2 fusion.8
  361.2 0.0 copy-done.5
  361.2 1.3 multiply_subtract_fusion
  362.6 0.0 copy-start.4
  362.6 0.6 copy.44
  363.2 0.0 copy-start.3
  363.2 12.8 %update_weight.9 = (f32[1024,1024]{1,0:T(8,128)}, f32[2,1024,1024]{2,1,0:T(8,128)}, f32[1024,1024]{1,0:T(8,128)}) custom-call(f32[16,128]{1,0:T(8,128)} %get-tuple-element.78.norms, bf16[1024,1024]{1,0:T(8,128)(2,1)} %bitcast.63, f32[2,1024,1024]{2,1,0:T(8,128)} %state.9, f32[1024,1024]{1,0:T(8,128)} %master.9), custom_call_target="tpu_custom_call" | custom-call | tf_op jit(solution)/shard_map/update_weight/pallas_call | solution.py:1437
  376.0 0.0 copy-done.4
  376.0 0.0 copy-done.3
  376.0 0.1 slice_reduce_fusion.1
  376.2 0.6 pad_maximum_fusion.1
  376.7 12.1 %update_weight.8 = (f32[256,4096]{1,0:T(8,128)}, f32[2,256,4096]{2,1,0:T(8,128)}, f32[256,4096]{1,0:T(8,128)}) custom-call(f32[16,128]{1,0:T(8,128)} %get-tuple-element.78.norms, bf16[256,4096]{1,0:T(8,128)(2,1)} %bitcast.62, f32[2,256,4096]{2,1,0:T(8,128)} %state.8, f32[256,4096]{1,0:T(8,128)} %master.8), custom_call_target="tpu_custom_call" | custom-call | tf_op jit(solution)/shard_map/update_weight/pallas_call | solution.py:1437
  388.8 5.0 %update_weight.7 = (f32[256,1024]{1,0:T(8,128)}, f32[2,256,1024]{2,1,0:T(8,128)}, f32[256,1024]{1,0:T(8,128)}) custom-call(f32[16,128]{1,0:T(8,128)} %get-tuple-element.78.norms, bf16[256,1024]{1,0:T(8,128)(2,1)} %bitcast.69, f32[2,256,1024]{2,1,0:T(8,128)} %state.7, f32[256,1024]{1,0:T(8,128)} %master.7), custom_call_target="tpu_custom_call" | custom-call | tf_op jit(solution)/shard_map/update_weight/pallas_call | solution.py:1437
  393.8 9.6 %update_weight.6 = (f32[256,3072]{1,0:T(8,128)}, f32[2,256,3072]{2,1,0:T(8,128)}, f32[256,3072]{1,0:T(8,128)}) custom-call(f32[16,128]{1,0:T(8,128)} %get-tuple-element.78.norms, bf16[256,3072]{1,0:T(8,128)(2,1)} %bitcast.64, f32[2,256,3072]{2,1,0:T(8,128)} %state.6, f32[256,3072]{1,0:T(8,128)} %master.6), custom_call_target="tpu_custom_call" | custom-call | tf_op jit(solution)/shard_map/update_weight/pallas_call | solution.py:1437
  403.4 0.0 copy-start
  403.4 0.0 copy-start.2
  403.4 6.4 %update_weight.5 = (f32[512,1024]{1,0:T(8,128)}, f32[2,512,1024]{2,1,0:T(8,128)}, f32[512,1024]{1,0:T(8,128)}) custom-call(f32[16,128]{1,0:T(8,128)} %get-tuple-element.78.norms, bf16[512,1024]{1,0:T(8,128)(2,1)} %bitcast.65, f32[2,512,1024]{2,1,0:T(8,128)} %state.5, f32[512,1024]{1,0:T(8,128)} %master.5), custom_call_target="tpu_custom_call" | custom-call | tf_op jit(solution)/shard_map/update_weight/pallas_call | solution.py:1437
  409.8 0.0 copy-done
  409.8 0.0 copy-done.2
  409.8 1.2 slice_bitcast_fusion
  (3 shorter events, 0.0 us)
Async XLA Ops:
  4.3 146.6 %copy-start.6 = (f32[2,11,256]{2,0,1:T(2,128)S(1)}, f32[2,11,256]{2,0,1:T(2,128)}, u32[]{:S(2)}) copy-start(f32[2,11,256]{2,0,1:T(2,128)} %param.29) | copy-start | bytes 67588
  4.3 147.2 %copy-start.1 = (bf16[1,276,1024]{2,1,0:T(8,128)(2,1)S(1)}, bf16[1,276,1024]{2,1,0:T(8,128)(2,1)}, u32[]{:S(2)}) copy-start(bf16[1,276,1024]{2,1,0:T(8,128)(2,1)} %param.17) | copy-start | bytes 1695748
  152.4 208.8 %copy-start.5 = (f32[11,256]{1,0:T(8,128)S(1)}, f32[11,256]{1,0:T(8,128)}, u32[]{:S(2)}) copy-start(f32[11,256]{1,0:T(8,128)} %param.23) | copy-start | bytes 33796
  362.6 13.4 %copy-start.4 = (f32[11,256]{1,0:T(8,128)}, f32[11,256]{1,0:T(8,128)S(1)}, u32[]{:S(2)}) copy-start(f32[11,256]{1,0:T(8,128)S(1)} %get-tuple-element.147) | copy-start | bytes 33796
  363.2 12.8 %copy-start.3 = (f32[16,128]{1,0:T(8,128)S(1)}, f32[16,128]{1,0:T(8,128)}, u32[]{:S(2)}) copy-start(f32[16,128]{1,0:T(8,128)} %get-tuple-element.78.norms) | copy-start | bytes 24580
  403.4 6.4 %copy-start = (bf16[288,2048]{1,0:T(8,128)(2,1)S(1)}, bf16[288,2048]{1,0:T(8,128)(2,1)}, u32[]{:S(2)}) copy-start(bf16[288,2048]{1,0:T(8,128)(2,1)} %get-tuple-element.77) | copy-start | bytes 3538948
  403.4 6.4 %copy-start.2 = (bf16[288,1024]{1,0:T(8,128)(2,1)S(1)}, bf16[288,1024]{1,0:T(8,128)(2,1)}, u32[]{:S(2)}) copy-start(bf16[288,1024]{1,0:T(8,128)(2,1)} %get-tuple-element.61) | copy-start | bytes 1769476

commit v7 on v6

--- a/solution.py
+++ b/solution.py
@@ -60,8 +60,8 @@
 
 
 class Plan:
-    def __init__(self, latency=1.5):
-        self.now, self.latency = 0.0, latency
+    def __init__(self, latency, rate, pace):
+        self.now, self.latency, self.rate, self.pace = 0.0, latency, rate, pace
         self.free = {}
         self.agents = []
 
@@ -94,7 +94,7 @@
             self.resume(able[0])
 
     def spend(self, length):
-        self.now += 0.8 * length
+        self.now += self.pace * length
         self.pump()
 
     def until(self, moment):
@@ -161,7 +161,6 @@
 
 
 SLOTS = 19
-LINK_RATE = 45e3
 Z_BACKLOG = 5.0
 
 
@@ -386,9 +385,9 @@
         copy.start()
         kept.append(copy)
 
-    plan = Plan()
+    plan = Plan(latency=1.5, rate=45e3, pace=0.8)
     done = [0] * total
-    unit = UNIT * BLOCK * 2 / LINK_RATE
+    unit = UNIT * BLOCK * 2 / plan.rate
 
     def chunk_steps(at):
         yield 0.0, lambda: (at == 0 or done[at - 1] >= 1) and plan.backlog("z") < Z_BACKLOG
@@ -469,7 +468,7 @@
     head_copies = []
     moments = []
     for pair in range(pairs):
-        moments.append(plan.transfer("z", 4 * rows * 384 * 2 / LINK_RATE))
+        moments.append(plan.transfer("z", 4 * rows * 384 * 2 / plan.rate))
         for offset in range(1, SHARDS):
             target = lax.rem(s + offset, SHARDS)
             columns = pl.ds(pair * 384, 384)
@@ -524,7 +523,7 @@
             answer[where, pair * 128 : (pair + 1) * 128] = both.T.astype(LOW)
             plan.spend(2.0)
 
-        answer_moment = plan.transfer("z", 4 * rows * 128 * 2 / LINK_RATE)
+        answer_moment = plan.transfer("z", 4 * rows * 128 * 2 / plan.rate)
         columns = pl.ds(pair * 128, 128)
         for offset in range(1, SHARDS):
             answer_copies.append(
@@ -647,6 +646,10 @@
     )(joined, table, *split)
     weights = [out.reshape(shape) for out, shape in zip(outs[:5], shapes)]
     return weights, outs[5:]
+
+
+UPDATE_ROWS, UPDATE_SLOTS = 256, 3
+Z_LIMIT = 1000.0
 
 
 def norm_back(source, gain, incoming, residual, wide_out, low_out, rows):
@@ -1011,11 +1014,11 @@
         stage_twin,
         stage_end,
     )
-    plan = Plan()
+    plan = Plan(latency=1.5, rate=45e3, pace=0.8)
     total = len(chunks)
     at_stage = [0] * total
     allowed = [0]
-    unit = UNIT * BLOCK * 2 / LINK_RATE
+    unit = UNIT * BLOCK * 2 / plan.rate
     costs = (0.5, 1.1, 0.4, 0.25, 0.25, 0.1, 0.1, 0.0)
     lengths = (
         (("core", 32 * unit / 6),),
@@ -1033,6 +1036,8 @@
         for number, stage in enumerate(stages):
             def free(number=number):
                 if number == 0 and at >= allowed[0]:
+                    return False
+                if number == 3 and plan.backlog("z") > Z_LIMIT:
                     return False
                 if number == 1 and at >= 5 and at_stage[at - 5] < 4:
                     return False
@@ -1125,7 +1130,7 @@
     mixed_copies = []
     moments = []
     for pair in range(pairs):
-        moments.append(plan.transfer("z", 4 * rows * 128 * 2 / LINK_RATE))
+        moments.append(plan.transfer("z", 4 * rows * 128 * 2 / plan.rate))
         columns = pl.ds(pair * 128, 128)
         for offset in range(1, SHARDS):
             mixed_copies.append(
@@ -1191,7 +1196,7 @@
         grad_heads[:, base + 128 : base + 256] = jnp.where(live, grad_key[...], 0.0).astype(LOW)
         grad_heads[:, base + 256 : base + 384] = jnp.where(live, grad_value[...], 0.0).astype(LOW)
         columns = pl.ds(base, 384)
-        triple_moment = plan.transfer("z", 4 * rows * 384 * 2 / LINK_RATE)
+        triple_moment = plan.transfer("z", 4 * rows * 384 * 2 / plan.rate)
         for offset in range(1, SHARDS):
             triple_copies.append(
                 extra(
@@ -1416,36 +1421,101 @@
     return lows, outs[5][: vectors.shape[0]], outs[6], outs[7]
 
 
-def update_kernel(position, norms, gradient, state, master, wide, new_state, new_master):
-    grad = gradient[...].astype(jnp.float32)
-    moment = 0.5 * state[0] + 0.5 * grad
-    root = jnp.sqrt(0.5 * state[1] * state[1] + 0.5 * grad * grad)
-    wide[...] = grad
-    new_state[0] = moment
-    new_state[1] = root
-    ratio = norms[position : position + 1, 0:1] / (
-        norms[8 + position : 9 + position, 0:1] + 1e-06
-    )
-    new_master[...] = master[...] - (step_rate * ratio) * (moment / (root + 1e-06))
-
-
-def update_weight(position, norms, gradient, state, master):
-    rows, columns = master.shape
-    block = 256 if columns <= BLOCK else 64
-    plain = pl.BlockSpec((block, columns), lambda i: (i, 0))
-    paired = pl.BlockSpec((2, block, columns), lambda i: (0, i, 0))
-    return pl.pallas_call(
-        functools.partial(update_kernel, position),
-        grid=(rows // block,),
-        out_shape=[
-            jax.ShapeDtypeStruct(master.shape, jnp.float32),
-            jax.ShapeDtypeStruct(state.shape, jnp.float32),
-            jax.ShapeDtypeStruct(master.shape, jnp.float32),
+def update_kernel(blocks, norms, *refs):
+    gradients, states, masters = refs[0:5], refs[5:10], refs[10:15]
+    wides, new_states, new_masters = refs[15:20], refs[20:25], refs[25:30]
+    low_in, state_in, master_in, wide_out, state_out, master_out, in_sems, out_sems = refs[30:]
+    slots, height = low_in.shape[0], low_in.shape[1]
+
+    def copies(at, arriving):
+        index, row, column = blocks[at]
+        slot = at % slots
+        where = (pl.ds(row, height), pl.ds(column, BLOCK))
+        outside = (gradients, states, masters) if arriving else (wides, new_states, new_masters)
+        inside = (low_in, state_in, master_in) if arriving else (wide_out, state_out, master_out)
+        sems = in_sems if arriving else out_sems
+        result = []
+        for number in range(3):
+            far = outside[number][index].at[((slice(None),) if number == 1 else ()) + where]
+            near = inside[number].at[slot]
+            ends = (far, near) if arriving else (near, far)
+            result.append(pltpu.make_async_copy(*ends, sems.at[slot, number]))
+        return result
+
+    def start(at, arriving):
+        for copy in copies(at, arriving):
+            copy.start()
+
+    def wait(at, arriving):
+        for copy in copies(at, arriving):
+            copy.wait()
+
+    total = len(blocks)
+    ahead = slots - 1
+    for at in range(min(ahead, total)):
+        start(at, True)
+    for at in range(total):
+        index = blocks[at][0]
+        slot = at % slots
+        if at + ahead < total:
+            start(at + ahead, True)
+        wait(at, True)
+        if at >= slots:
+            wait(at - slots, False)
+        ratio = step_rate * (
+            norms[index : index + 1, 0:1] / (norms[8 + index : 9 + index, 0:1] + 1e-06)
+        )
+
+        @pl.loop(0, height // UNIT)
+        def _(step):
+            rows = pl.ds(pl.multiple_of(step * UNIT, UNIT), UNIT)
+            grad = low_in[slot, rows, :].astype(jnp.float32)
+            second = state_in[slot, 1, rows, :]
+            moment = 0.5 * state_in[slot, 0, rows, :] + 0.5 * grad
+            root = jnp.sqrt(0.5 * second * second + 0.5 * grad * grad)
+            wide_out[slot, rows, :] = grad
+            state_out[slot, 0, rows, :] = moment
+            state_out[slot, 1, rows, :] = root
+            master_out[slot, rows, :] = master_in[slot, rows, :] - ratio * (
+                moment / (root + 1e-06)
+            )
+
+        start(at, False)
+    for at in range(max(0, total - slots), total):
+        wait(at, False)
+
+
+def update_weights(norms, gradients, states, masters):
+    height, slots = UPDATE_ROWS, UPDATE_SLOTS
+    blocks = [
+        (index, row, column)
+        for index, master in enumerate(masters)
+        for row in range(0, master.shape[0], height)
+        for column in range(0, master.shape[1], BLOCK)
+    ]
+    square = (slots, height, BLOCK)
+    pair = (slots, 2, height, BLOCK)
+    outs = pl.pallas_call(
+        functools.partial(update_kernel, blocks),
+        out_shape=[jax.ShapeDtypeStruct(m.shape, jnp.float32) for m in masters]
+        + [jax.ShapeDtypeStruct(state.shape, jnp.float32) for state in states]
+        + [jax.ShapeDtypeStruct(m.shape, jnp.float32) for m in masters],
+        in_specs=[pl.BlockSpec(memory_space=pltpu.VMEM)] + [ANY] * 15,
+        out_specs=[ANY] * 15,
+        scratch_shapes=[
+            pltpu.VMEM(square, LOW),
+            pltpu.VMEM(pair, jnp.float32),
+            pltpu.VMEM(square, jnp.float32),
+            pltpu.VMEM(square, jnp.float32),
+            pltpu.VMEM(pair, jnp.float32),
+            pltpu.VMEM(square, jnp.float32),
+            pltpu.SemaphoreType.DMA((slots, 3)),
+            pltpu.SemaphoreType.DMA((slots, 3)),
         ],
-        in_specs=[pl.BlockSpec((16, 128), lambda i: (0, 0)), plain, paired, plain],
-        out_specs=[plain, paired, plain],
-        name="update_weight",
-    )(norms, gradient, state, master)
+        compiler_params=pltpu.CompilerParams(vmem_limit_bytes=48 * 2**20),
+        name="update_weights",
+    )(norms, *gradients, *states, *masters)
+    return outs[:5], outs[5:10], outs[10:]
 
 
 def fits(masters):
@@ -1660,21 +1730,18 @@
     lows, vector_total, norms, grad_joined = backward_pass(
         incoming, joined, table, kept, weights, masters, states, vectors, moments_vectors, portion
     )
-    steps = [
-        update_weight(position, norms, lows[position], states[position], masters[position])
-        for position in range(5)
-    ]
+    wides, new_states, new_masters = update_weights(norms, lows, states, masters)
     vector_state, direction = moment_step(vector_total, moments_vectors)
     ratio = norms[5, 0] / (norms[13, 0] + 1e-06)
     return (
         block_out[None, :portion],
         grad_joined[None, :portion, :model_width],
         grad_joined[None, :portion, model_width:],
-        *(step[0] for step in steps),
+        *wides,
         vector_total,
-        *(step[1] for step in steps),
+        *new_states,
         vector_state,
-        *(step[2] for step in steps),
+        *new_masters,
         vectors - step_rate * ratio * direction,
         jnp.stack([norms[:6, 0], norms[8:14, 0]]),
     )

time: 414 us -> 405 us (0.978)
  Pallas kernels: 399 us -> 388 us
    pallas_call x5 -> x1, Pallas kernels: 45.8 us -> 35.2 us  [update_weights(): pl.pallas_call(functools.partial(update_kernel, blocks), out_shape=[jax.S...]
where the time goes in v7:
time: 405 us; the launch traced here: 402 us
  Pallas kernels  388 us (96%)
  local copies, waits for them, and re-layouts  8.31 us (2%)
    pallas_call x1, Pallas kernels, backward_pass(): pl.pallas_call(functools.partial(backward_kernel, chunks, portion), out_s...  206 us
    pallas_call x1, Pallas kernels, forward_pass(): pl.pallas_call(functools.partial(forward_kernel, chunks, portion), out_sh...  147 us
    pallas_call x1, Pallas kernels, update_weights(): pl.pallas_call(functools.partial(update_kernel, blocks), out_shape=[jax.S...  35.2 us

profile of v7, /device:TPU:0, one launch (start us, length us, event | category | flops | bytes accessed | tf_op | source)
XLA Modules:
  0.0 401.8 jit_solution(13645454875769187923)
XLA Ops:
  0.7 0.0 copy-start.7
  0.7 1.9 pad.19.refs_0_
  2.6 2.3 fusion.2.refs_0_.refs_11_
  4.9 0.0 copy-done.7
  4.9 0.6 pad.18.refs_1_.refs_27_
  5.5 0.0 copy-start.8
  5.6 146.8 %forward_pass.1 = (bf16[4,2,2,2,2,2,16,1024]{7,6,5,4,3,2,1,0:T(8,128)(2,1)}, bf16[4,1,2,2,2,2,16,3072]{7,6,5,4,3,2,1,0:T(8,128)(2,1)}, bf16[4,1,2,2,2,2,16,1024]...) custom-call(bf16[288,2048]{1,0:T(8,128)(2,1)} %fusion.2.refs_0_.refs, ...), custom_call_target="tpu_custom_call" | custom-call | tf_op jit(solution)/shard_map/forward_pass/pallas_call | solution.py:610
  152.3 0.0 copy-done.8
  152.3 0.6 pad.20.refs_28_
  153.0 0.0 copy-start.5
  153.0 205.6 %backward_pass.1 = (bf16[2,2,2,2,2,16,1024]{6,5,4,3,2,1,0:T(8,128)(2,1)}, bf16[1,2,2,2,2,16,3072]{6,5,4,3,2,1,0:T(8,128)(2,1)}, bf16[1,2,2,2,2,16,1024]{6,5,4,3,...) custom-call(bf16[288,1024]{1,0:T(8,128)(2,1)} %pad.19.refs_0_, ...), custom_call_target="tpu_custom_call" | custom-call | tf_op jit(solution)/shard_map/backward_pass/pallas_call | solution.py:1355
  358.6 0.0 copy-start
  358.6 0.0 copy-start.1
  358.6 0.0 copy-start.3
  358.6 0.0 copy-start.4
  358.7 0.0 copy-done.5
  358.7 2.6 slice_bitcast_fusion
  361.3 0.0 copy-done
  361.3 0.0 copy-done.1
  361.3 0.0 copy-done.3
  361.3 0.0 copy-done.4
  361.3 0.0 copy-start.2
  361.3 1.2 copy-done.2
  362.5 0.0 copy-start.9
  362.5 35.2 %update_weights.1 = (f32[512,1024]{1,0:T(8,128)}, f32[256,3072]{1,0:T(8,128)}, f32[256,1024]{1,0:T(8,128)}, f32[256,4096]{1,0:T(8,128)}, f32[1024,1024]{1,0:T(8,...) custom-call(f32[16,128]{1,0:T(8,128)S(1)} %copy-done.4, ...), custom_call_target="tpu_custom_call" | custom-call | tf_op jit(solution)/shard_map/update_weights/pallas_call | solution.py:1498
  397.7 0.5 fusion.8
  399.6 0.0 copy-done.9
  399.6 0.6 multiply_subtract_fusion
  400.2 0.6 copy.44
  400.9 0.1 slice_reduce_fusion.1
  401.0 0.6 pad_maximum_fusion.1
  401.6 0.0 copy-done.6
  (4 shorter events, 0.0 us)
Async XLA Ops:
  0.7 4.3 %copy-start.7 = (f32[11,256]{1,0:T(8,128)S(1)}, f32[11,256]{1,0:T(8,128)}, u32[]{:S(2)}) copy-start(f32[11,256]{1,0:T(8,128)} %param.23) | copy-start | bytes 33796
  5.5 146.8 %copy-start.8 = (f32[2,11,256]{2,0,1:T(2,128)S(1)}, f32[2,11,256]{2,0,1:T(2,128)}, u32[]{:S(2)}) copy-start(f32[2,11,256]{2,0,1:T(2,128)} %param.29) | copy-start | bytes 67588
  153.0 205.7 %copy-start.5 = (bf16[288,1024]{1,0:T(8,128)(2,1)S(1)}, bf16[288,1024]{1,0:T(8,128)(2,1)}, u32[]{:S(2)}) copy-start(bf16[288,1024]{1,0:T(8,128)(2,1)} %get-tuple-element.61) | copy-start | bytes 1769476
  358.6 2.7 copy-start
  358.6 2.7 copy-start.1
  358.6 2.6 copy-start.3
  358.6 2.6 copy-start.4
  361.3 1.2 copy-start.2
  362.5 37.0 %copy-start.9 = (f32[16,256]{1,0:T(8,128)S(1)}, f32[16,256]{1,0:T(8,128)}, u32[]{:S(2)}) copy-start(f32[16,256]{1,0:T(8,128)} %get-tuple-element.89) | copy-start | bytes 49156
  400.2 1.4 copy-start.6

commit v8 on v7

--- a/solution.py
+++ b/solution.py
@@ -200,7 +200,7 @@
 
 
 def forward_kernel(chunks, portion, *refs):
-    joined, vectors = refs[0:2]
+    rows_in, vectors = refs[0:2]
     masters = refs[2:7]
     keeps = refs[7:12]
     (
@@ -229,6 +229,8 @@
         recv_sems,
         more_send,
         more_recv,
+        joined,
+        joined_sem,
     ) = refs[28:]
     place = Place()
     s, k, x, y = place.shard, place.core, place.x, place.y
@@ -385,7 +387,7 @@
         copy.start()
         kept.append(copy)
 
-    plan = Plan(latency=1.5, rate=45e3, pace=0.8)
+    plan = Plan(latency=2.0, rate=45e3, pace=0.8)
     done = [0] * total
     unit = UNIT * BLOCK * 2 / plan.rate
 
@@ -421,6 +423,10 @@
 
     load(0).start()
     load(1).start()
+    joined_copy = pltpu.make_async_copy(
+        rows_in.at[:, pl.ds(0, joined.shape[1])], joined, joined_sem.at[0]
+    )
+    joined_copy.start()
     table_own[...] = vectors[...].astype(LOW)
     table_all[0] = vectors[...].astype(LOW)
     greet(place)
@@ -439,6 +445,7 @@
     for offset in range(SHARDS):
         column = pl.multiple_of(place.source(offset) * own, own)
         table[:, pl.ds(column, own)] = table_all[offset].astype(jnp.float32)
+    joined_copy.wait()
     until(last[0])
 
     @pl.loop(0, width // 256)
@@ -596,7 +603,7 @@
     chunks = chunk_list(shapes)
     total = len(chunks)
     rows = joined.shape[0]
-    width = joined.shape[1] // 2
+    width = joined.shape[1] // 3
     own = width // SHARDS
     hidden = shapes[3][1]
     everyone = SHARDS * rows
@@ -623,7 +630,7 @@
             jax.ShapeDtypeStruct((rows, width), LOW),
             jax.ShapeDtypeStruct((16, width), jnp.float32),
         ],
-        in_specs=[inner] * 2 + [ANY] * 5,
+        in_specs=[ANY, inner] + [ANY] * 5,
         out_specs=[ANY] * 5 + [inner] * 11,
         scratch_shapes=[pltpu.VMEM(fold, LOW) for fold in folds]
         + [
@@ -638,6 +645,8 @@
             pltpu.SemaphoreType.DMA((total * SLOTS,)),
             pltpu.SemaphoreType.DMA((3 + 6 * (own // 128),)),
             pltpu.SemaphoreType.DMA((3 + 6 * (own // 128),)),
+            pltpu.VMEM((rows, 2 * width), LOW),
+            pltpu.SemaphoreType.DMA((1,)),
         ],
         compiler_params=pltpu.CompilerParams(
             collective_id=1, has_side_effects=True, vmem_limit_bytes=60 * 2**20
@@ -683,7 +692,7 @@
 
 def backward_kernel(chunks, portion, *refs):
     (
-        cotangent,
+        rows_in,
         vectors,
         log_total,
         activated,
@@ -732,6 +741,8 @@
         first_in,
         entering,
         joined,
+        cotangent,
+        cotangent_sem,
         load_sems,
         ring_sems,
         state_sems,
@@ -750,7 +761,9 @@
 
     inside = (second_in, slope, middle, mixed, heads, first_in, entering, joined)
     loads = [
-        pltpu.make_async_copy(source, target, load_sems.at[position])
+        pltpu.make_async_copy(
+            source.at[:, pl.ds(0, target.shape[1])], target, load_sems.at[position]
+        )
         for position, (source, target) in enumerate(zip(outside, inside))
     ]
     names = ["second_in", "slope", "middle", "mixed", "heads", "first_in", "entering", "joined"]
@@ -1064,11 +1077,16 @@
             copy.wait_recv()
 
     prime(4)
+    cotangent_copy = pltpu.make_async_copy(
+        rows_in.at[:, pl.ds(2 * width, width)], cotangent, cotangent_sem.at[0]
+    )
+    cotangent_copy.start()
     for copy in loads:
         copy.start()
     squares[...] = jnp.zeros_like(squares)
     table_own[...] = jnp.zeros_like(table_own)
     greet(place)
+    cotangent_copy.wait()
     allow(4)
 
     def put_row(row, value):
@@ -1360,7 +1378,10 @@
             jax.ShapeDtypeStruct((16, 128), jnp.float32),
             jax.ShapeDtypeStruct((rows, 2 * width), LOW),
         ],
-        in_specs=[inner] * 4 + [ANY] * 23 + [inner] * 2,
+        in_specs=[ANY]
+        + [inner] * 3
+        + [ANY] * 23
+        + [inner] * 2,
         out_specs=[ANY] * 5 + [inner] * 3,
         scratch_shapes=[
             pltpu.VMEM((8, 2, 2, 2, 2) + piece, LOW),
@@ -1391,7 +1412,10 @@
             pltpu.VMEM((everyone, 3 * own), LOW),
             pltpu.VMEM((SHARDS, rows, 3 * own), LOW),
             pltpu.VMEM((rows, width), LOW),
-            *[pltpu.VMEM(array.shape, array.dtype) for array in loaded],
+            *[pltpu.VMEM(array.shape, array.dtype) for array in loaded[:7]],
+            pltpu.VMEM((rows, 2 * width), LOW),
+            pltpu.VMEM((rows, width), LOW),
+            pltpu.SemaphoreType.DMA((1,)),
             pltpu.SemaphoreType.DMA((8,)),
             pltpu.SemaphoreType.DMA((8,)),
             pltpu.SemaphoreType.DMA((2, 2)),
@@ -1722,13 +1746,12 @@
             hidden_in, skip_path, cotangent, *masters, vectors, *states, moments_vectors
         )
     more = -portion % 32
-    joined = jnp.concatenate([hidden_in[0], skip_path[0]], 1)
+    joined = jnp.concatenate([hidden_in[0], skip_path[0], cotangent[0]], 1)
     joined = jnp.pad(joined, ((0, more), (0, 0)))
-    incoming = jnp.pad(cotangent[0], ((0, more), (0, 0)))
     weights, kept = forward_pass(joined, vectors, masters, portion)
     block_out, table = kept[9], kept[10]
     lows, vector_total, norms, grad_joined = backward_pass(
-        incoming, joined, table, kept, weights, masters, states, vectors, moments_vectors, portion
+        joined, joined, table, kept, weights, masters, states, vectors, moments_vectors, portion
     )
     wides, new_states, new_masters = update_weights(norms, lows, states, masters)
     vector_state, direction = moment_step(vector_total, moments_vectors)

time: 405 us -> 402 us (level)
  no operation moved by 1% of the time
where the time goes in v8:
time: 402 us; the launch traced here: 398 us
  Pallas kernels  386 us (96%)
  local copies, waits for them, and re-layouts  6.39 us (2%)
    pallas_call x1, Pallas kernels, backward_pass(): pl.pallas_call(functools.partial(backward_kernel, chunks, portion), out_s...  206 us
    pallas_call x1, Pallas kernels, forward_pass(): pl.pallas_call(functools.partial(forward_kernel, chunks, portion), out_sh...  145 us
    pallas_call x1, Pallas kernels, update_weights(): pl.pallas_call(functools.partial(update_kernel, blocks), out_shape=[jax.S...  35.2 us

profile of v8, /device:TPU:0, one launch (start us, length us, event | category | flops | bytes accessed | tf_op | source)
XLA Modules:
  0.0 398.4 jit_solution(16757999080550535758)
XLA Ops:
  0.7 0.0 copy-start.7
  0.7 2.8 fusion.4.refs_0_.refs_11_
  3.4 0.0 copy-done.7
  3.4 0.6 pad.14.refs_1_.refs_27_
  4.1 0.0 copy-start.8
  4.1 145.0 %forward_pass.1 = (bf16[4,2,2,2,2,2,16,1024]{7,6,5,4,3,2,1,0:T(8,128)(2,1)}, bf16[4,1,2,2,2,2,16,3072]{7,6,5,4,3,2,1,0:T(8,128)(2,1)}, bf16[4,1,2,2,2,2,16,1024]...) custom-call(bf16[288,3072]{1,0:T(8,128)(2,1)} %fusion.4.refs_0_.refs, ...), custom_call_target="tpu_custom_call" | custom-call | tf_op jit(solution)/shard_map/forward_pass/pallas_call | solution.py:617
  149.1 0.0 copy-done.8
  149.1 0.6 pad.15.refs_28_
  149.7 0.0 copy-start.5
  149.7 205.6 %backward_pass.1 = (bf16[2,2,2,2,2,16,1024]{6,5,4,3,2,1,0:T(8,128)(2,1)}, bf16[1,2,2,2,2,16,3072]{6,5,4,3,2,1,0:T(8,128)(2,1)}, bf16[1,2,2,2,2,16,1024]{6,5,4,3,...) custom-call(bf16[288,3072]{1,0:T(8,128)(2,1)} %fusion.4.refs_0_.refs, ...), custom_call_target="tpu_custom_call" | custom-call | tf_op jit(solution)/shard_map/backward_pass/pallas_call | solution.py:1373
  355.3 0.0 copy-start
  355.3 0.0 copy-start.1
  355.3 0.0 copy-start.3
  355.3 0.0 copy-start.4
  355.3 0.0 copy-done.5
  355.3 2.6 slice_bitcast_fusion
  358.0 0.0 copy-done
  358.0 0.0 copy-done.1
  358.0 0.0 copy-done.3
  358.0 0.0 copy-done.4
  358.0 0.0 copy-start.2
  358.0 1.2 copy-done.2
  359.2 0.0 copy-start.9
  359.2 35.2 %update_weights.1 = (f32[512,1024]{1,0:T(8,128)}, f32[256,3072]{1,0:T(8,128)}, f32[256,1024]{1,0:T(8,128)}, f32[256,4096]{1,0:T(8,128)}, f32[1024,1024]{1,0:T(8,...) custom-call(f32[16,128]{1,0:T(8,128)S(1)} %copy-done.4, ...), custom_call_target="tpu_custom_call" | custom-call | tf_op jit(solution)/shard_map/update_weights/pallas_call | solution.py:1522
  394.4 0.5 fusion.10
  396.2 0.0 copy-done.9
  396.2 0.6 multiply_subtract_fusion
  396.9 0.0 copy-start.6
  396.9 0.6 copy.44
  397.5 0.1 slice_reduce_fusion.1
  397.7 0.6 pad_maximum_fusion.1
  398.3 0.0 copy-done.6
  (3 shorter events, 0.0 us)
Async XLA Ops:
  0.7 2.8 copy-start.7
  4.1 145.0 %copy-start.8 = (f32[2,11,256]{2,0,1:T(2,128)S(1)}, f32[2,11,256]{2,0,1:T(2,128)}, u32[]{:S(2)}) copy-start(f32[2,11,256]{2,0,1:T(2,128)} %param.29) | copy-start | bytes 67588
  149.7 205.6 %copy-start.5 = (bf16[288,1024]{1,0:T(8,128)(2,1)S(1)}, bf16[288,1024]{1,0:T(8,128)(2,1)}, u32[]{:S(2)}) copy-start(bf16[288,1024]{1,0:T(8,128)(2,1)} %get-tuple-element.61) | copy-start | bytes 1769476
  355.3 2.7 copy-start
  355.3 2.7 copy-start.1
  355.3 2.6 copy-start.3
  355.3 2.6 copy-start.4
  358.0 1.2 copy-start.2
  359.2 37.0 %copy-start.9 = (f32[16,256]{1,0:T(8,128)S(1)}, f32[16,256]{1,0:T(8,128)}, u32[]{:S(2)}) copy-start(f32[16,256]{1,0:T(8,128)} %get-tuple-element.89) | copy-start | bytes 49156
  396.9 1.4 copy-start.6
